TPU v7x, 32 devices: a whole 2x2x4 slice. The times are simulated.
32 devices in a mesh: row: 4 (over x, core), col: 8 (over z, y).
Axes of the slice: x: 2, y: 2, z: 4, core: 2. Of those that a mesh axis runs over, the one named last changes fastest.
Arguments:
- inputs: bfloat16 [256, 8192], P('col', 'row'), may hold values from -1.5 to 1.5
- grad_out: bfloat16 [256, 8192], P('col', 'row'), may hold values from -3 to 3
- gate: bfloat16 [256, 30720], P('row', 'col'), may hold values from -6 to 6
- up: bfloat16 [256, 30720], P('row', 'col'), may hold values from -6 to 6
- gate_weight: bfloat16 [8192, 30720], P('row', 'col'), may hold values from -0.0625 to 0.0625
- up_weight: bfloat16 [8192, 30720], P('row', 'col'), may hold values from -0.0625 to 0.0625
- down_weight: bfloat16 [30720, 8192], P('col', 'row'), may hold values from -0.03125 to 0.03125
Outputs:
- grad_inputs: bfloat16 [256, 8192], P('col', 'row')
- grad_gate_weight: bfloat16 [8192, 30720], P('row', 'col')
- grad_up_weight: bfloat16 [8192, 30720], P('row', 'col')
- grad_down_weight: bfloat16 [30720, 8192], P('col', 'row')
All inputs are finite; a program needn't handle non-finite values.
Results may differ from a plain program's by a relative error of at most 0.022.
Values may be sent and summed in bfloat16 or wider, within the bound.
No kernel may reach another device: no remote copies, remote signals or barrier semaphores. Data moves between devices by JAX's collectives and lax.ppermute only.
A program may use at most 192 MiB of HBM per device.

v0:
```python
import jax
import jax.numpy as jnp
from jax import lax
from jax.sharding import PartitionSpec as P


def swiglu_backward(grad_hidden, gate_part, up_part):
    gate_vals = gate_part.astype(jnp.float32)
    up_vals = up_part.astype(jnp.float32)
    sigmoid_gate = jax.nn.sigmoid(gate_vals)
    activated = gate_vals * sigmoid_gate
    grad_gate = (
        grad_hidden * up_vals * sigmoid_gate * (1.0 + gate_vals * (1.0 - sigmoid_gate))
    ).astype(jnp.bfloat16)
    grad_up = (grad_hidden * activated).astype(jnp.bfloat16)
    hidden = (activated * up_vals).astype(jnp.bfloat16)
    return (grad_gate, grad_up, hidden)


def local(inputs, grad_out, gate, up, gate_weight, up_weight, down_weight):
    out_all = lax.all_gather(grad_out, "col", axis=0, tiled=True)
    contract_last = (((1,), (1,)), ((), ()))
    contract_first = (((0,), (0,)), ((), ()))
    grad_hidden = lax.psum_scatter(
        lax.dot_general(
            out_all, down_weight, contract_last, preferred_element_type=jnp.float32
        ).astype(jnp.bfloat16),
        "row",
        scatter_dimension=0,
        tiled=True,
    ).astype(jnp.float32)
    grad_gate_own, grad_up_own, hidden_own = swiglu_backward(grad_hidden, gate, up)
    grad_gate_all, grad_up_all, hidden_all = (
        lax.all_gather(grad_gate_own, "row", axis=0, tiled=True),
        lax.all_gather(grad_up_own, "row", axis=0, tiled=True),
        lax.all_gather(hidden_own, "row", axis=0, tiled=True),
    )
    gate_rows = grad_gate_all
    up_rows = grad_up_all
    total = lax.dot_general(
        gate_rows, gate_weight, contract_last, preferred_element_type=jnp.float32
    )
    grad_inputs = lax.psum_scatter(
        total
        + lax.dot_general(up_rows, up_weight, contract_last, preferred_element_type=jnp.float32),
        "col",
        scatter_dimension=0,
        tiled=True,
    ).astype(jnp.bfloat16)
    grad_down = lax.dot_general(
        hidden_all, out_all, contract_first, preferred_element_type=jnp.float32
    )
    shard_rows = lax.all_gather(inputs, "col", axis=0, tiled=True)
    gate_rows = grad_gate_all
    up_rows = grad_up_all
    gate_total = lax.dot_general(
        shard_rows, gate_rows, contract_first, preferred_element_type=jnp.float32
    )
    up_total = lax.dot_general(
        shard_rows, up_rows, contract_first, preferred_element_type=jnp.float32
    )
    return (
        grad_inputs,
        gate_total.astype(jnp.bfloat16),
        up_total.astype(jnp.bfloat16),
        grad_down.astype(jnp.bfloat16),
    )


def solution(mesh):
    return jax.shard_map(
        local,
        mesh=mesh,
        in_specs=(
            P("col", "row"),
            P("col", "row"),
            P("row", "col"),
            P("row", "col"),
            P("row", "col"),
            P("row", "col"),
            P("col", "row"),
        ),
        out_specs=(P("col", "row"), P("row", "col"), P("row", "col"), P("col", "row")),
        check_vma=False,
    )
```

profile of v0, /device:TPU:0, one launch (start us, length us, event | category | flops | bytes accessed | tf_op | source)
XLA Modules:
  0.0 287.2 jit_solution(6254856339674520264)
XLA Ops:
  7.2 0.7 all-gather.6.cloned.1.call-update
  7.9 0.0 reduce-scatter.3.cloned.1.call-start
  7.9 45.1 %all-gather.6.cloned.1.call-done = bf16[256,2048]{1,0:T(8,128)(2,1)} async-done(((bf16[32,2048]{1,0:T(8,128)(2,1)}), bf16[256,2048]{1,0:T(8,128)(2,1)}) %all-gather.6.cloned.1.call-update) | async-done | bytes 1048592 | tf_op jit(solution)/shard_map/all_gather | solution.py:21
  53.0 11.3 %convolution_convert_fusion.1 = bf16[256,3840]{1,0:T(8,128)(2,1)} fusion(bf16[256,2048]{1,0:T(8,128)(2,1)} %all-gather.6.cloned.1.call-done, bf16[3840,2048]{1,0:T(8,128)(2,1)} %param.13), kind=kOutput, calls=%fused_computation.3 | convolution fusion | flops 4027514880 | bytes 18743296 | tf_op jit(solution)/shard_map/dot_general | solution.py:25
  64.4 0.0 all-gather.8.cloned.1.call-start
  64.4 29.5 %reduce-scatter.3.cloned.1.call-done = bf16[64,3840]{1,0:T(8,128)(2,1)} async-done(((bf16[256,3840]{1,0:T(8,128)(2,1)}), bf16[64,3840]{1,0:T(8,128)(2,1)}) %reduce-scatter.3.cloned.1.call-update) | async-done | bytes 491536 | tf_op jit(solution)/shard_map/reduce_scatter | solution.py:24
  93.9 2.6 fusion.4
  96.6 0.0 all-gather.10.cloned.1.call-start
  96.6 0.5 all-gather.10.cloned.1.call-update
  97.2 0.5 all-gather.12.cloned.1.call-update
  97.8 0.5 all-gather.14.cloned.1.call-update
  98.3 0.2 reduce-scatter.5.cloned.1.call-start
  98.5 20.0 %all-gather.8.cloned.1.call-done = bf16[256,3840]{1,0:T(8,128)(2,1)} async-done(((bf16[64,3840]{1,0:T(8,128)(2,1)}), bf16[256,3840]{1,0:T(8,128)(2,1)}) %all-gather.8.cloned.1.call-update) | async-done | bytes 1966096 | tf_op jit(solution)/shard_map/all_gather | solution.py:34
  118.6 8.3 %fusion.9 = f32[256,2048]{1,0:T(8,128)S(1)} fusion(bf16[256,3840]{1,0:T(8,128)(2,1)} %all-gather.8.cloned.1.call-done, bf16[2048,3840]{1,0:T(8,128)(2,1)} %param.11), kind=kOutput, calls=%fused_computation.20 | convolution fusion | flops 4026531840 | bytes 19791872 | tf_op jit(solution)/shard_map/dot_general | solution.py:40
  126.8 15.7 %all-gather.10.cloned.1.call-done = bf16[256,3840]{1,0:T(8,128)(2,1)} async-done(((bf16[64,3840]{1,0:T(8,128)(2,1)}), bf16[256,3840]{1,0:T(8,128)(2,1)}) %all-gather.10.cloned.1.call-update) | async-done | bytes 1966096 | tf_op jit(solution)/shard_map/all_gather | solution.py:35
  142.5 11.6 %convolution_add_fusion = f32[256,2048]{1,0:T(8,128)} fusion(f32[256,2048]{1,0:T(8,128)S(1)} %fusion.9, bf16[256,3840]{1,0:T(8,128)(2,1)} %all-gather.10.cloned.1.call-done, bf16[2048,3840]{1,0:T(8,128)(2,1)} %param.12), kind=kOutput, calls=%fused_computation.4 | convolution fusion | flops 4027056128 | bytes 21889024 | tf_op jit(solution)/shard_map/dot_general | solution.py:45
  154.2 30.7 %all-gather.12.cloned.1.call-done = bf16[256,2048]{1,0:T(8,128)(2,1)} async-done(((bf16[32,2048]{1,0:T(8,128)(2,1)}), bf16[256,2048]{1,0:T(8,128)(2,1)}) %all-gather.12.cloned.1.call-update) | async-done | bytes 1048592 | tf_op jit(solution)/shard_map/all_gather | solution.py:53
  184.9 9.3 %convert_bitcast_fusion.1 = bf16[2048,3840]{0,1:T(8,128)(2,1)} fusion(bf16[256,3840]{1,0:T(8,128)(2,1)S(1)} %copy-done.1, bf16[256,2048]{1,0:T(8,128)(2,1)} %all-gather.12.cloned.1.call-done), kind=kOutput, calls=%fused_computation.1 | convolution fusion | flops 4034396160 | bytes 18743296 | tf_op jit(solution)/shard_map/dot_general | solution.py:56
  194.2 20.8 %copy.11 = bf16[2048,3840]{1,0:T(8,128)(2,1)} copy(bf16[2048,3840]{0,1:T(8,128)(2,1)} %convert_bitcast_fusion.1) | data formatting | bytes 31457280
  214.9 8.1 %convert_bitcast_fusion = bf16[2048,3840]{0,1:T(8,128)(2,1)} fusion(bf16[256,3840]{1,0:T(8,128)(2,1)S(1)} %copy-done.2, bf16[256,2048]{1,0:T(8,128)(2,1)S(1)} %copy-done), kind=kOutput, calls=%fused_computation | convolution fusion | flops 4034396160 | bytes 18743296 | tf_op jit(solution)/shard_map/dot_general | solution.py:59
  223.0 20.8 %copy.12 = bf16[2048,3840]{1,0:T(8,128)(2,1)} copy(bf16[2048,3840]{0,1:T(8,128)(2,1)} %convert_bitcast_fusion) | data formatting | bytes 31457280
  243.8 9.6 %convolution_convert_fusion = bf16[3840,2048]{1,0:T(8,128)(2,1)} fusion(bf16[256,3840]{1,0:T(8,128)(2,1)} %all-gather.14.cloned.1.call-done, bf16[256,2048]{1,0:T(8,128)(2,1)S(1)} %copy-done.3), kind=kOutput, calls=%fused_computation.2 | convolution fusion | flops 4034396160 | bytes 18743296 | tf_op jit(solution)/shard_map/dot_general | solution.py:50
  253.4 25.4 %reduce-scatter.5.cloned.1.call-done = f32[32,2048]{1,0:T(8,128)} async-done(((f32[256,2048]{1,0:T(8,128)}), f32[32,2048]{1,0:T(8,128)}) %reduce-scatter.5.cloned.1.call-update) | async-done | bytes 262160 | tf_op jit(solution)/shard_map/reduce_scatter | solution.py:43
  278.8 1.6 convert_element_type.45
  (19 shorter events, 0.2 us)
Async XLA Ops:
  7.2 45.8 %all-gather.6.cloned.1.call-start = ((), (), s32[]{:S(2)}) async-start(), calls=%async_computation.2 | async-start | bytes 1179648 | tf_op jit(solution)/shard_map/all_gather | solution.py:21
  7.9 86.0 %reduce-scatter.3.cloned.1.call-start = ((), (), s32[]{:S(2)}) async-start(), calls=%async_computation.3 | async-start | bytes 2457600 | tf_op jit(solution)/shard_map/reduce_scatter | solution.py:24
  64.4 29.5 %copy-start.4 = (bf16[64,3840]{1,0:T(8,128)(2,1)S(1)}, bf16[64,3840]{1,0:T(8,128)(2,1)}, u32[]{:S(2)}) copy-start(bf16[64,3840]{1,0:T(8,128)(2,1)} %param.10) | copy-start | bytes 1474564
  64.4 29.5 %copy-start.5 = (bf16[64,3840]{1,0:T(8,128)(2,1)S(1)}, bf16[64,3840]{1,0:T(8,128)(2,1)}, u32[]{:S(2)}) copy-start(bf16[64,3840]{1,0:T(8,128)(2,1)} %param.9) | copy-start | bytes 1474564
  64.4 54.2 %all-gather.8.cloned.1.call-start = ((), (), s32[]{:S(2)}) async-start(), calls=%async_computation.4 | async-start | bytes 2457600 | tf_op jit(solution)/shard_map/all_gather | solution.py:34
  96.6 46.0 %all-gather.10.cloned.1.call-start = ((), (), s32[]{:S(2)}) async-start(), calls=%async_computation.5 | async-start | bytes 2457600 | tf_op jit(solution)/shard_map/all_gather | solution.py:35
  97.1 87.8 %all-gather.12.cloned.1.call-start = ((), (), s32[]{:S(2)}) async-start(), calls=%async_computation.7 | async-start | bytes 1179648 | tf_op jit(solution)/shard_map/all_gather | solution.py:53
  97.7 146.1 %all-gather.14.cloned.1.call-start = ((), (), s32[]{:S(2)}) async-start(), calls=%async_computation.8 | async-start | bytes 2457600 | tf_op jit(solution)/shard_map/all_gather | solution.py:36
  98.3 180.5 %reduce-scatter.5.cloned.1.call-start = ((), (), s32[]{:S(2)}) async-start(), calls=%async_computation.6 | async-start | bytes 2359296 | tf_op jit(solution)/shard_map/reduce_scatter | solution.py:43
  154.2 30.7 %copy-start.1 = (bf16[256,3840]{1,0:T(8,128)(2,1)S(1)}, bf16[256,3840]{1,0:T(8,128)(2,1)}, u32[]{:S(2)}) copy-start(bf16[256,3840]{1,0:T(8,128)(2,1)} %all-gather.8.cloned.1.call-done) | copy-start | bytes 5898244
  194.2 20.8 %copy-start = (bf16[256,2048]{1,0:T(8,128)(2,1)S(1)}, bf16[256,2048]{1,0:T(8,128)(2,1)}, u32[]{:S(2)}) copy-start(bf16[256,2048]{1,0:T(8,128)(2,1)} %all-gather.12.cloned.1.call-done) | copy-start | bytes 3145732
  194.2 20.8 %copy-start.2 = (bf16[256,3840]{1,0:T(8,128)(2,1)S(1)}, bf16[256,3840]{1,0:T(8,128)(2,1)}, u32[]{:S(2)}) copy-start(bf16[256,3840]{1,0:T(8,128)(2,1)} %all-gather.10.cloned.1.call-done) | copy-start | bytes 5898244
  223.0 20.8 %copy-start.3 = (bf16[256,2048]{1,0:T(8,128)(2,1)S(1)}, bf16[256,2048]{1,0:T(8,128)(2,1)}, u32[]{:S(2)}) copy-start(bf16[256,2048]{1,0:T(8,128)(2,1)} %all-gather.6.cloned.1.call-done) | copy-start | bytes 3145732
Sparse Core Ops, SparseCore 0:
  10.1 42.8 all-gather.5
  64.5 29.3 reduce-scatter.2
  96.7 21.8 all-gather.7
  120.6 21.8 all-gather.9
  144.7 40.1 all-gather.11
  186.4 20.5 all-gather.13
  211.0 67.7 reduce-scatter.4
where the time goes:
time: 288 us; the launch traced here: 287 us
  waiting for transfers between devices  169 us (59%)
  matrix products  58.2 us (20%)
  local copies, waits for them, and re-layouts  41.5 us (14%)
  between operations  14.1 us (5%)
  other arithmetic  4.24 us (1%)
    all_gather x1, waiting for transfers between devices, local(): out_all = lax.all_gather(grad_out, 'col', axis=0, tiled=True)  45.1 us
    unnamed x14, local copies, waits for them, and re-layouts  41.5 us
    all_gather x1, waiting for transfers between devices, local(): shard_rows = lax.all_gather(inputs, 'col', axis=0, tiled=True)  30.7 us
    reduce_scatter x1, waiting for transfers between devices, local(): lax.psum_scatter(lax.dot_general(out_all, down_weight, contract_last, pre...  29.5 us
    reduce_scatter x1, waiting for transfers between devices, local(): lax.psum_scatter(total + lax.dot_general(up_rows, up_weight, contract_las...  25.4 us
    all_gather x1, waiting for transfers between devices, local(): lax.all_gather(grad_gate_own, 'row', axis=0, tiled=True)  20 us
    all_gather x1, waiting for transfers between devices, local(): lax.all_gather(grad_up_own, 'row', axis=0, tiled=True)  15.7 us
    dot_general x1, matrix products, local(): lax.dot_general(up_rows, up_weight, contract_last, preferred_element_type...  11.6 us
  transfers between devices with their start and end apart: 7, of which 6 were waited for; matrix products, arithmetic and copies ran while one was open for 31% of the time, Pallas kernels for 0%

commit v1 on v0

v1 whole, which is shorter than its diff:
```python
import functools

import jax
import jax.numpy as jnp
from jax import lax
from jax.experimental import pallas as pl
from jax.experimental.pallas import tpu as pltpu
from jax.sharding import PartitionSpec as P

F32 = jnp.float32
BF16 = jnp.bfloat16
CORES = 2
VMEM = 40 * 2**20
NT = (((1,), (1,)), ((), ()))
TN = (((0,), (0,)), ((), ()))


def divisor(size, target, step=128):
    best = size
    for cand in range(step, target + 1, step):
        if size % cand == 0:
            best = cand
    return best


def params(semantics=("arbitrary",)):
    return pltpu.CompilerParams(dimension_semantics=semantics, vmem_limit_bytes=VMEM)


def cost(flops, nbytes):
    return pl.CostEstimate(flops=int(flops), bytes_accessed=int(nbytes), transcendentals=0)


def assemble(blocks, offsets):
    rows, width = blocks[0].shape
    count = len(blocks)

    def kernel(offs, *refs):
        out = refs[count]
        for i in range(count):
            out[pl.ds(pl.multiple_of(offs[i], rows), rows), :] = refs[i][...]

    full = pl.BlockSpec(memory_space=pltpu.VMEM)
    return pl.pallas_call(
        kernel,
        out_shape=jax.ShapeDtypeStruct((rows * count, width), BF16),
        in_specs=[pl.BlockSpec(memory_space=pltpu.SMEM)] + [full] * count,
        out_specs=full,
        compiler_params=pltpu.CompilerParams(vmem_limit_bytes=VMEM),
        cost_estimate=cost(0, 4 * rows * count * width),
        name="assemble",
    )(offsets, *blocks)


def partial_hidden(out_all, down, chunk, chunks):
    tokens, width = out_all.shape
    units = down.shape[0] // chunks
    half = tokens // CORES
    block = divisor(units, 640)
    steps = units // block

    def kernel(a, w, keep, send):
        part = lax.dot_general(a[...], w[...], NT, preferred_element_type=F32).astype(BF16)
        keep[...] = part[:half]
        send[...] = part[half:]

    shape = jax.ShapeDtypeStruct((half, units), BF16)
    return pl.pallas_call(
        kernel,
        grid=(steps,),
        out_shape=(shape, shape),
        in_specs=[
            pl.BlockSpec((tokens, width), lambda i: (0, 0)),
            pl.BlockSpec((block, width), lambda i: (chunk * steps + i, 0)),
        ],
        out_specs=[pl.BlockSpec((half, block), lambda i: (0, i))] * 2,
        compiler_params=params(),
        cost_estimate=cost(2 * tokens * units * width, 2 * units * width + 4 * tokens * units),
        name="partial_hidden",
    )(out_all, down)


def activations(gates, ups):
    count = len(gates)
    rows, width = gates[0].shape
    block = divisor(width, 768)

    def kernel(*refs):
        out = refs[2 * count]
        for i in range(count):
            gate = refs[i][...].astype(F32)
            up = refs[count + i][...].astype(F32)
            out[i * rows : (i + 1) * rows, :] = (gate * jax.nn.sigmoid(gate) * up).astype(BF16)

    return pl.pallas_call(
        kernel,
        grid=(width // block,),
        out_shape=jax.ShapeDtypeStruct((rows * count, width), BF16),
        in_specs=[pl.BlockSpec((rows, block), lambda i: (0, i))] * (2 * count),
        out_specs=pl.BlockSpec((rows * count, block), lambda i: (0, i)),
        compiler_params=params(),
        cost_estimate=cost(10 * rows * count * width, 6 * rows * count * width),
        name="activations",
    )(*gates, *ups)


def hidden_grads(sums, gates, ups, chunk):
    count = len(gates)
    rows = gates[0].shape[0]
    units = sums[0].shape[1]
    block = divisor(units, 640)
    steps = units // block

    def kernel(*refs):
        out = refs[3 * count]
        for i in range(count):
            grad = 0.0
            for o in range(count):
                j = (i - o) % count
                grad = grad + refs[o][j * rows : (j + 1) * rows, :].astype(F32)
            gate = refs[count + i][...].astype(F32)
            up = refs[2 * count + i][...].astype(F32)
            sig = jax.nn.sigmoid(gate)
            at = slice(i * rows, (i + 1) * rows)
            out[0, at, :] = (grad * up * sig * (1.0 + gate * (1.0 - sig))).astype(BF16)
            out[1, at, :] = (grad * gate * sig).astype(BF16)

    return pl.pallas_call(
        kernel,
        grid=(steps,),
        out_shape=jax.ShapeDtypeStruct((2, rows * count, units), BF16),
        in_specs=[pl.BlockSpec((rows * count, block), lambda i: (0, i))] * count
        + [pl.BlockSpec((rows, block), lambda i: (0, chunk * steps + i))] * (2 * count),
        out_specs=pl.BlockSpec((2, rows * count, block), lambda i: (0, 0, i)),
        compiler_params=params(),
        cost_estimate=cost(20 * rows * count * units, 12 * rows * count * units),
        name="hidden_grads",
    )(*sums, *gates, *ups)


def down_grad(mine, other, out_all):
    half, units = mine.shape
    tokens, width = out_all.shape
    block = divisor(units, 384)

    def kernel(a, b, g, out):
        hidden = jnp.concatenate([a[...], b[...]], axis=0)
        out[...] = lax.dot_general(hidden, g[...], TN, preferred_element_type=F32).astype(BF16)

    return pl.pallas_call(
        kernel,
        grid=(units // block,),
        out_shape=jax.ShapeDtypeStruct((units, width), BF16),
        in_specs=[pl.BlockSpec((half, block), lambda i: (0, i))] * 2
        + [pl.BlockSpec((tokens, width), lambda i: (0, 0))],
        out_specs=pl.BlockSpec((block, width), lambda i: (i, 0)),
        compiler_params=params(),
        cost_estimate=cost(2 * tokens * units * width, 2 * units * width),
        name="down_grad",
    )(mine, other, out_all)


def input_grads(mine, other, gate_weight, up_weight, before, offsets, chunk, rows):
    _, half, units = mine.shape
    tokens = 2 * half
    width = gate_weight.shape[0]
    block = divisor(width, 512)
    last = offsets is not None
    count = tokens // rows
    operands, specs = [], []
    if last:
        operands.append(offsets)
        specs.append(pl.BlockSpec(memory_space=pltpu.SMEM))
    operands += [mine, other, gate_weight, up_weight]
    specs += [pl.BlockSpec((2, half, units), lambda i: (0, 0, 0))] * 2
    specs += [pl.BlockSpec((block, units), lambda i: (i, chunk))] * 2
    if before is not None:
        operands.append(before)
        specs.append(pl.BlockSpec((tokens, block), lambda i: (0, i)))

    def kernel(*refs):
        refs = list(refs)
        offs = refs.pop(0) if last else None
        a, b, gw, uw = refs[:4]
        refs = refs[4:]
        total = refs.pop(0)[...] if before is not None else 0.0
        for i, w in enumerate((gw, uw)):
            grads = jnp.concatenate([a[i], b[i]], axis=0)
            total = total + lax.dot_general(grads, w[...], NT, preferred_element_type=F32)
        if not last:
            refs[0][...] = total
            return
        scratch = refs[count]
        scratch[...] = total
        for m in range(count):
            refs[m][...] = scratch[pl.ds(pl.multiple_of(offs[m], rows), rows), :].astype(BF16)

    if last:
        out_shape = [jax.ShapeDtypeStruct((rows, width), BF16)] * count
        out_specs = [pl.BlockSpec((rows, block), lambda i: (0, i))] * count
        scratch = [pltpu.VMEM((tokens, block), F32)]
    else:
        out_shape = jax.ShapeDtypeStruct((tokens, width), F32)
        out_specs = pl.BlockSpec((tokens, block), lambda i: (0, i))
        scratch = []
    return pl.pallas_call(
        kernel,
        grid=(width // block,),
        out_shape=out_shape,
        in_specs=specs,
        out_specs=out_specs,
        scratch_shapes=scratch,
        compiler_params=params(),
        cost_estimate=cost(4 * tokens * units * width, 4 * units * width),
        name="input_grads",
    )(*operands)


def weight_grads(mine, other, in_all, before, chunk, chunks):
    _, half, units = mine.shape
    tokens, width = in_all.shape
    block = divisor(width, 512)

    def kernel(*refs):
        a, b, x = refs[:3]
        for i, out in enumerate(refs[-2:]):
            grads = jnp.concatenate([a[i], b[i]], axis=0)
            out[...] = lax.dot_general(x[...], grads, TN, preferred_element_type=F32).astype(BF16)

    specs = [pl.BlockSpec((2, half, units), lambda i: (0, 0, 0))] * 2
    specs += [pl.BlockSpec((tokens, block), lambda i: (0, i))]
    operands = [mine, other, in_all]
    aliases = {}
    if before is not None:
        operands += list(before)
        specs += [pl.BlockSpec(memory_space=pl.ANY)] * 2
        aliases = {3: 0, 4: 1}
    shape = jax.ShapeDtypeStruct((width, units * chunks), BF16)
    return pl.pallas_call(
        kernel,
        grid=(width // block,),
        out_shape=(shape, shape),
        in_specs=specs,
        out_specs=[pl.BlockSpec((block, units), lambda i: (i, chunk))] * 2,
        input_output_aliases=aliases,
        compiler_params=params(),
        cost_estimate=cost(4 * tokens * units * width, 4 * units * width),
        name="weight_grads",
    )(*operands)


def after(value, *others):
    return lax.optimization_barrier((value, *others))[0]


def local(nr, nc, inputs, grad_out, gate, up, gate_weight, up_weight, down_weight):
    nx = nr // CORES
    row, col = lax.axis_index("row"), lax.axis_index("col")
    x, core = row // CORES, row % CORES
    own_tokens = gate.shape[0]
    col_tokens = grad_out.shape[0]
    units = down_weight.shape[0]
    chunks = 3 if units % 384 == 0 else 1
    direct = nc == 8 and nr * own_tokens == nc * col_tokens and own_tokens % col_tokens == 0

    def swap_core(value):
        return lax.ppermute(value, "row", [(r, r ^ 1) for r in range(nr)])

    def from_x(value, offset):
        return lax.ppermute(value, "row", [((r + offset * CORES) % nr, r) for r in range(nr)])

    def swap_col(value, mask):
        return lax.ppermute(value, "col", [(c, c ^ mask) for c in range(nc)])

    def place(block):
        block_x, block_core = block // CORES, block % CORES
        return ((block_core ^ core) * nx + (block_x - x + nx) % nx) * own_tokens

    if direct:
        rows = col_tokens
        per = own_tokens // col_tokens
        places = [
            place((col ^ m) // per) + ((col ^ m) % per) * col_tokens for m in range(nc)
        ]
    else:
        rows = own_tokens
        places = [place(r) for r in range(nr)]
    offsets = jnp.stack(places).astype(jnp.int32)

    def gather(value):
        if not direct:
            whole = lax.all_gather(value, "col", axis=0, tiled=True)
            return [whole[r * rows : (r + 1) * rows] for r in range(nr)]
        got = {0: value}
        for m in (1, 2, 4, 6):
            got[m] = swap_col(value, m)
        for m in (2, 4, 6):
            got[m + 1] = swap_col(got[m], 1)
        return [got[m] for m in range(nc)]

    def scatter(blocks):
        if not direct:
            return lax.psum_scatter(
                jnp.concatenate(blocks, axis=0), "col", scatter_dimension=0, tiled=True
            )
        summed = {}
        for m in (6, 4, 2, 0):
            other = swap_col(blocks[m + 1], 1)
            summed[m] = blocks[m].astype(F32) + other.astype(F32)
        total = summed[0]
        for m in (6, 4, 2):
            total = total + swap_col(summed[m].astype(BF16), m).astype(F32)
        return total.astype(BF16)

    gates = [gate] + [from_x(gate, o) for o in range(1, nx)]
    ups = [up] + [from_x(up, o) for o in range(1, nx)]

    out_blocks = gather(grad_out)
    out_all = assemble(out_blocks, offsets)

    sums = []
    for c in range(chunks):
        keep, send = partial_hidden(out_all, down_weight, c, chunks)
        total = (keep.astype(F32) + swap_core(send).astype(F32)).astype(BF16)
        sums.append([total] + [from_x(total, o) for o in range(1, nx)])

    in_all = assemble(gather(after(inputs, out_all)), offsets)

    hidden = activations(gates, ups)
    grad_down = down_grad(hidden, swap_core(hidden), out_all)

    total, weights = None, None
    for c in range(chunks):
        mine = hidden_grads(sums[c], gates, ups, c)
        other = swap_core(mine)
        last = c == chunks - 1
        total = input_grads(
            mine, other, gate_weight, up_weight, total, offsets if last else None, c, rows
        )
        weights = weight_grads(mine, other, in_all, weights, c, chunks)
    grad_inputs = scatter(total)
    return grad_inputs, weights[0], weights[1], grad_down


def solution(mesh):
    return jax.shard_map(
        functools.partial(local, mesh.shape["row"], mesh.shape["col"]),
        mesh=mesh,
        in_specs=(
            P("col", "row"),
            P("col", "row"),
            P("row", "col"),
            P("row", "col"),
            P("row", "col"),
            P("row", "col"),
            P("col", "row"),
        ),
        out_specs=(P("col", "row"), P("row", "col"), P("row", "col"), P("col", "row")),
        check_vma=False,
    )
```

time: 288 us -> 135 us (0.47)
  waiting for transfers between devices: 169 us -> 35.9 us
  Pallas kernels: 0 us -> 59.5 us
  matrix products: 58.2 us -> 0 us
  local copies, waits for them, and re-layouts: 41.5 us -> 1.01 us
  starting transfers between devices: 0.45 us -> 35.9 us
  between operations: 14.1 us -> 0.91 us
  other arithmetic: 4.24 us -> 1.12 us
    all_gather x5 -> x0, waiting for transfers between devices: 111 us -> none  [the longest x1 45.1 us: local(): out_all = lax.all_gather(grad_out, 'col', axis=0, tiled=True)]
    pallas_call x0 -> x16, Pallas kernels: none -> 59.5 us  [the longest x3 19.4 us: input_grads(): pl.pallas_call(kernel, grid=(width // block,), out_shape=out_shape, in_sp...]
    dot_general x6 -> x0, matrix products: 58.2 us -> none  [the longest x1 11.6 us: local(): lax.dot_general(up_rows, up_weight, contract_last, preferred_element_type...]
    reduce_scatter x2 -> x0, waiting for transfers between devices: 54.8 us -> none  [the longest x1 29.5 us: local(): lax.psum_scatter(lax.dot_general(out_all, down_weight, contract_last, pre...]
    unnamed x14 -> x8, local copies, waits for them, and re-layouts: 41.5 us -> 0.92 us
    ppermute x0 -> x33, starting transfers between devices: none -> 35.9 us  [the longest x21 29.3 us: swap_col(): return lax.ppermute(value, 'col', [(c, c ^ mask) for c in range(nc)])]
    ppermute x0 -> x33, waiting for transfers between devices: none -> 35.9 us  [the longest x21 20.8 us: swap_col(): return lax.ppermute(value, 'col', [(c, c ^ mask) for c in range(nc)])]
    convert_element_type x2 -> x7, other arithmetic: 4.24 us -> 1.12 us  [the longest x1 0.74 us: scatter(): return total.astype(BF16)]
  transfers between devices with their start and end apart: 7 -> 33, of which waited for: 6 -> 11; matrix products, arithmetic and copies ran while one was open for 31% -> 0% of each run, Pallas kernels for 0% -> 39%
where the time goes in v1:
time: 135 us; the launch traced here: 134 us
  Pallas kernels  59.5 us (44%)
  starting transfers between devices  35.9 us (27%)
  waiting for transfers between devices  35.9 us (27%)
    ppermute x21, starting transfers between devices, swap_col(): return lax.ppermute(value, 'col', [(c, c ^ mask) for c in range(nc)])  29.3 us
    ppermute x21, waiting for transfers between devices, swap_col(): return lax.ppermute(value, 'col', [(c, c ^ mask) for c in range(nc)])  20.8 us
    pallas_call x3, Pallas kernels, input_grads(): pl.pallas_call(kernel, grid=(width // block,), out_shape=out_shape, in_sp...  19.4 us
    pallas_call x3, Pallas kernels, weight_grads(): pl.pallas_call(kernel, grid=(width // block,), out_shape=(shape, shape),...  15.3 us
    ppermute x5, waiting for transfers between devices, from_x(): lax.ppermute(value, 'row', [((r + offset * CORES) % nr, r) for r in range...  13.9 us
    pallas_call x3, Pallas kernels, partial_hidden(): pl.pallas_call(kernel, grid=(steps,), out_shape=(shape, shape), in_specs=...  11.5 us
    pallas_call x1, Pallas kernels, down_grad(): pl.pallas_call(kernel, grid=(units // block,), out_shape=jax.ShapeDtypeSt...  9.48 us
    ppermute x5, starting transfers between devices, from_x(): lax.ppermute(value, 'row', [((r + offset * CORES) % nr, r) for r in range...  5.54 us
  transfers between devices with their start and end apart: 33, of which 11 were waited for; matrix products, arithmetic and copies ran while one was open for 0% of the time, Pallas kernels for 39%

profile of v1, /device:TPU:0, one launch (start us, length us, event | category | flops | bytes accessed | tf_op | source)
XLA Modules:
  0.0 134.3 jit_solution(14521353193066030606)
XLA Ops:
  0.6 3.1 %collective-permute-start.1 = (bf16[32,2048]{1,0:T(8,128)(2,1)}, bf16[32,2048]{1,0:T(8,128)(2,1)S(1)}, u32[]{:S(2)}, u32[]{:S(2)}) collective-permute-start(bf16[32,2048]{1,0:T(8,128)(2,1)} %refs_0_.2), channel_id=1, source_target_pairs={{0,2},{1,3},{2,0},{3,1},{4,6},{5,7},{6,4},{7,5},{8,10},{9,11},{10,... | collective-permute-start | bytes 393224 | tf_op jit(solution)/shard_map/ppermute | solution.py:273
  3.7 2.6 %collective-permute-start.3 = (bf16[32,2048]{1,0:T(8,128)(2,1)}, bf16[32,2048]{1,0:T(8,128)(2,1)S(1)}, u32[]{:S(2)}, u32[]{:S(2)}) collective-permute-start(bf16[32,2048]{1,0:T(8,128)(2,1)} %refs_0_.2), channel_id=1, source_target_pairs={{0,4},{1,5},{2,6},{3,7},{4,0},{5,1},{6,2},{7,3},{8,12},{9,13},{10,... | collective-permute-start | bytes 393224 | tf_op jit(solution)/shard_map/ppermute | solution.py:273
  6.3 1.7 %collective-permute-start = (bf16[32,2048]{1,0:T(8,128)(2,1)}, bf16[32,2048]{1,0:T(8,128)(2,1)S(1)}, u32[]{:S(2)}, u32[]{:S(2)}) collective-permute-start(bf16[32,2048]{1,0:T(8,128)(2,1)} %refs_0_.2), channel_id=1, source_target_pairs={{0,1},{1,0},{2,3},{3,2},{4,5},{5,4},{6,7},{7,6},{8,9},{9,8},{10,11... | collective-permute-start | bytes 393224 | tf_op jit(solution)/shard_map/ppermute | solution.py:273
  9.0 1.7 %collective-permute-start.2 = (bf16[32,2048]{1,0:T(8,128)(2,1)S(1)}, bf16[32,2048]{1,0:T(8,128)(2,1)S(1)}, u32[]{:S(2)}, u32[]{:S(2)}) collective-permute-start(bf16[32,2048]{1,0:T(8,128)(2,1)S(1)} %collective-permute-done.1.refs_2_), channel_id=1, source_target_pairs={{0,1},{1,0},{2,3},{3,2},{4,5},{5,4},{6,7},{7,6},{8,9},{9,8},{10,11... | collective-permute-start | bytes 393224 | tf_op jit(solution)/shard_map/ppermute | solution.py:273
  10.7 6.2 %collective-permute-done.3.refs_4_ = bf16[32,2048]{1,0:T(8,128)(2,1)S(1)} collective-permute-done((bf16[32,2048]{1,0:T(8,128)(2,1)}, bf16[32,2048]{1,0:T(8,128)(2,1)S(1)}, u32[]{:S(2)}, u32[]{:S(2)}) %collective-permute-start.3) | collective-permute-done | bytes 131104 | tf_op jit(solution)/shard_map/ppermute | solution.py:273
  21.8 1.5 %collective-permute-done.6.refs_7_ = bf16[32,2048]{1,0:T(8,128)(2,1)S(1)} collective-permute-done((bf16[32,2048]{1,0:T(8,128)(2,1)S(1)}, bf16[32,2048]{1,0:T(8,128)(2,1)S(1)}, u32[]{:S(2)}, u32[]{:S(2)}) %collective-permute-start.6) | collective-permute-done | bytes 131104 | tf_op jit(solution)/shard_map/ppermute | solution.py:273
  24.9 3.8 %partial_hidden.4 = (bf16[128,1280]{1,0:T(8,128)(2,1)S(1)}, bf16[128,1280]{1,0:T(8,128)(2,1)S(1)}) custom-call(bf16[256,2048]{1,0:T(8,128)(2,1)S(1)} %assemble.2.a.g, bf16[3840,2048]{1,0:T(8,128)(2,1)} %w.5), custom_call_target="tpu_custom_call" | custom-call | flops 1342177280 | bytes 6553600 | tf_op jit(solution)/shard_map/partial_hidden/pallas_call | solution.py:68
  31.1 3.8 %partial_hidden.3 = (bf16[128,1280]{1,0:T(8,128)(2,1)S(1)}, bf16[128,1280]{1,0:T(8,128)(2,1)S(1)}) custom-call(bf16[256,2048]{1,0:T(8,128)(2,1)S(1)} %assemble.2.a.g, bf16[3840,2048]{1,0:T(8,128)(2,1)} %w.5), custom_call_target="tpu_custom_call" | custom-call | flops 1342177280 | bytes 6553600 | tf_op jit(solution)/shard_map/partial_hidden/pallas_call | solution.py:68
  35.0 3.8 %partial_hidden.5 = (bf16[128,1280]{1,0:T(8,128)(2,1)S(1)}, bf16[128,1280]{1,0:T(8,128)(2,1)S(1)}) custom-call(bf16[256,2048]{1,0:T(8,128)(2,1)S(1)} %assemble.2.a.g, bf16[3840,2048]{1,0:T(8,128)(2,1)} %w.5), custom_call_target="tpu_custom_call" | custom-call | flops 1342177280 | bytes 6553600 | tf_op jit(solution)/shard_map/partial_hidden/pallas_call | solution.py:68
  38.8 2.1 %collective-permute-start.28 = (bf16[32,2048]{1,0:T(8,128)(2,1)S(1)}, bf16[32,2048]{1,0:T(8,128)(2,1)S(1)}, u32[]{:S(2)}, u32[]{:S(2)}) collective-permute-start(bf16[32,2048]{1,0:T(8,128)(2,1)S(1)} %copy-done.3), channel_id=1, source_target_pairs={{0,4},{1,5},{2,6},{3,7},{4,0},{5,1},{6,2},{7,3},{8,12},{9,13},{10,... | collective-permute-start | bytes 393224 | tf_op jit(solution)/shard_map/ppermute | solution.py:273
  44.0 1.6 %collective-permute-start.30 = (bf16[32,2048]{1,0:T(8,128)(2,1)S(1)}, bf16[32,2048]{1,0:T(8,128)(2,1)S(1)}, u32[]{:S(2)}, u32[]{:S(2)}) collective-permute-start(bf16[32,2048]{1,0:T(8,128)(2,1)S(1)} %copy-done.3), channel_id=1, source_target_pairs={{0,6},{1,7},{2,4},{3,5},{4,2},{5,3},{6,0},{7,1},{8,14},{9,15},{10,... | collective-permute-start | bytes 393224 | tf_op jit(solution)/shard_map/ppermute | solution.py:273
  49.4 13.9 %collective-permute-done.16.refs_1_ = bf16[128,1280]{1,0:T(8,128)(2,1)S(1)} collective-permute-done((bf16[128,1280]{1,0:T(8,128)(2,1)S(1)}, bf16[128,1280]{1,0:T(8,128)(2,1)S(1)}, u32[]{:S(2)}, u32[]{:S(2)}) %collective-permute-start.16) | collective-permute-done | bytes 327712 | tf_op jit(solution)/shard_map/ppermute | solution.py:270
  65.2 3.1 %collective-permute-done.27.refs_3_ = bf16[32,2048]{1,0:T(8,128)(2,1)S(1)} collective-permute-done((bf16[32,2048]{1,0:T(8,128)(2,1)S(1)}, bf16[32,2048]{1,0:T(8,128)(2,1)S(1)}, u32[]{:S(2)}, u32[]{:S(2)}) %collective-permute-start.27) | collective-permute-done | bytes 131104 | tf_op jit(solution)/shard_map/ppermute | solution.py:273
  70.9 2.3 %collective-permute-done.29.refs_5_ = bf16[32,2048]{1,0:T(8,128)(2,1)S(1)} collective-permute-done((bf16[32,2048]{1,0:T(8,128)(2,1)S(1)}, bf16[32,2048]{1,0:T(8,128)(2,1)S(1)}, u32[]{:S(2)}, u32[]{:S(2)}) %collective-permute-start.29) | collective-permute-done | bytes 131104 | tf_op jit(solution)/shard_map/ppermute | solution.py:273
  76.1 9.5 %down_grad.1 = bf16[3840,2048]{1,0:T(8,128)(2,1)} custom-call(bf16[128,3840]{1,0:T(8,128)(2,1)S(1)} %activations.1.a, bf16[128,3840]{1,0:T(8,128)(2,1)S(1)} %collective-permute-done.32.b, bf16[256,2048]{1,0:T(8,128)(2,1)S(1)} %assemble.2.a.g), custom_call_target="tpu_custom_call" | custom-call | flops 4026531840 | bytes 15728640 | tf_op jit(solution)/shard_map/down_grad/pallas_call | solution.py:150
  85.6 6.4 %input_grads.3.refs_4_ = f32[256,2048]{1,0:T(8,128)S(1)} custom-call(bf16[2,128,1280]{2,1,0:T(8,128)(2,1)S(1)} %hidden_grads.5.refs_0_, bf16[2,128,1280]{2,1,0:T(8,128)(2,1)S(1)} %collective-permute-done.17.refs_1_, bf16[2048,3840]{1,0:T(8,128)(2,1)} %refs_3_.5, bf16[2048,3840]{1,0:T(8,128)(2,1)} %refs_4_.7), custom_call_target="tpu_custom_call" | custom-call | flops 2684354560 | bytes 10485760 | tf_op jit(solution)/shard_map/input_grads/pallas_call | solution.py:206
  92.0 6.4 %input_grads.4.refs_5_ = f32[256,2048]{1,0:T(8,128)S(1)} custom-call(bf16[2,128,1280]{2,1,0:T(8,128)(2,1)S(1)} %hidden_grads.4.refs_0_, bf16[2,128,1280]{2,1,0:T(8,128)(2,1)S(1)} %collective-permute-done.14.refs_1_, bf16[2048,3840]{1,0:T(8,128)(2,1)} %refs_3_.5, bf16[2048,3840]{1,0:T(8,128)(2,1)} %refs_4_.7, f32[256,2048]{1,0:T(8,128)S(1)} %input_grads.3.refs_4_), custom_call_target="tpu_custom_call" | custom-call | flops 2684354560 | bytes 10485760 | tf_op jit(solution)/shard_map/input_grads/pallas_call | solution.py:206
  98.4 6.6 %input_grads.5 = (bf16[32,2048]{1,0:T(8,128)(2,1)S(1)}, bf16[32,2048]{1,0:T(8,128)(2,1)S(1)}, bf16[32,2048]{1,0:T(8,128)(2,1)S(1)}, bf16[32,2048]{1,0:T(8,128)(2...) custom-call(s32[8]{0:T(128)S(1)} %stack.35.offs.refs_0_, ...), custom_call_target="tpu_custom_call" | custom-call | flops 2684354560 | bytes 10485760 | tf_op jit(solution)/shard_map/input_grads/pallas_call | solution.py:206
  109.1 5.1 %weight_grads.3 = (bf16[2048,3840]{1,0:T(8,128)(2,1)}, bf16[2048,3840]{1,0:T(8,128)(2,1)}) custom-call(bf16[2,128,1280]{2,1,0:T(8,128)(2,1)S(1)} %hidden_grads.5.refs_0_, bf16[2,128,1280]{2,1,0:T(8,128)(2,1)S(1)} %collective-permute-done.17.refs_1_, bf16[256,2048]{1,0:T(8,128)(2,1)S(1)} %assemble.3.refs_2_), custom_call_target="tpu_custom_call" | custom-call | flops 2684354560 | bytes 10485760 | tf_op jit(solution)/shard_map/weight_grads/pallas_call | solution.py:239
  114.2 5.1 %weight_grads.4 = (bf16[2048,3840]{1,0:T(8,128)(2,1)}, bf16[2048,3840]{1,0:T(8,128)(2,1)}) custom-call(bf16[2,128,1280]{2,1,0:T(8,128)(2,1)S(1)} %hidden_grads.4.refs_0_, bf16[2,128,1280]{2,1,0:T(8,128)(2,1)S(1)} %collective-permute-done.14.refs_1_, bf16[256,2048]{1,0:T(8,128)(2,1)S(1)} %assemble.3.refs_2_, ...), custom_call_target="tpu_custom_call", output_to_operand_aliasing={{0}: (3, {}), {1}: (4, {})} | custom-call | flops 2684354560 | bytes 10485760 | tf_op jit(solution)/shard_map/weight_grads/pallas_call | solution.py:239
  119.3 2.2 %collective-permute-start.24 = (bf16[32,2048]{1,0:T(8,128)(2,1)S(1)}, bf16[32,2048]{1,0:T(8,128)(2,1)S(1)}, u32[]{:S(2)}, u32[]{:S(2)}) collective-permute-start(bf16[32,2048]{1,0:T(8,128)(2,1)S(1)} %add_convert_fusion.4), channel_id=1, source_target_pairs={{0,2},{1,3},{2,0},{3,1},{4,6},{5,7},{6,4},{7,5},{8,10},{9,11},{10,... | collective-permute-start | bytes 393224 | tf_op jit(solution)/shard_map/ppermute | solution.py:273
  122.7 1.5 %collective-permute-start.20 = (bf16[32,2048]{1,0:T(8,128)(2,1)S(1)}, bf16[32,2048]{1,0:T(8,128)(2,1)S(1)}, u32[]{:S(2)}, u32[]{:S(2)}) collective-permute-start(bf16[32,2048]{1,0:T(8,128)(2,1)S(1)} %add_convert_fusion.6), channel_id=1, source_target_pairs={{0,6},{1,7},{2,4},{3,5},{4,2},{5,3},{6,0},{7,1},{8,14},{9,15},{10,... | collective-permute-start | bytes 393224 | tf_op jit(solution)/shard_map/ppermute | solution.py:273
  124.2 5.1 %weight_grads.5 = (bf16[2048,3840]{1,0:T(8,128)(2,1)}, bf16[2048,3840]{1,0:T(8,128)(2,1)}) custom-call(bf16[2,128,1280]{2,1,0:T(8,128)(2,1)S(1)} %hidden_grads.3.refs_1_.refs_0_, bf16[2,128,1280]{2,1,0:T(8,128)(2,1)S(1)} %collective-permute-done.11.refs_2_.refs_1_, ...), custom_call_target="tpu_custom_call", output_to_operand_aliasing={{0}: (3, {}), {1}: (4, {})} | custom-call | flops 2684354560 | bytes 10485760 | tf_op jit(solution)/shard_map/weight_grads/pallas_call | solution.py:239
  129.3 4.3 %collective-permute-done.22 = bf16[32,2048]{1,0:T(8,128)(2,1)S(1)} collective-permute-done((bf16[32,2048]{1,0:T(8,128)(2,1)S(1)}, bf16[32,2048]{1,0:T(8,128)(2,1)S(1)}, u32[]{:S(2)}, u32[]{:S(2)}) %collective-permute-start.22) | collective-permute-done | bytes 131104 | tf_op jit(solution)/shard_map/ppermute | solution.py:273
  (74 shorter events, 29.9 us)
Async XLA Ops:
  3.7 13.2 %collective-permute-start.3 = (bf16[32,2048]{1,0:T(8,128)(2,1)}, bf16[32,2048]{1,0:T(8,128)(2,1)S(1)}, u32[]{:S(2)}, u32[]{:S(2)}) collective-permute-start(bf16[32,2048]{1,0:T(8,128)(2,1)} %refs_0_.2), channel_id=1, source_target_pairs={{0,4},{1,5},{2,6},{3,7},{4,0},{5,1},{6,2},{7,3},{8,12},{9,13},{10,... | collective-permute-start | bytes 393224 | tf_op jit(solution)/shard_map/ppermute | solution.py:273
  6.3 12.1 %collective-permute-start.5 = (bf16[32,2048]{1,0:T(8,128)(2,1)}, bf16[32,2048]{1,0:T(8,128)(2,1)S(1)}, u32[]{:S(2)}, u32[]{:S(2)}) collective-permute-start(bf16[32,2048]{1,0:T(8,128)(2,1)} %refs_0_.2), channel_id=1, source_target_pairs={{0,6},{1,7},{2,4},{3,5},{4,2},{5,3},{6,0},{7,1},{8,14},{9,15},{10,... | collective-permute-start | bytes 393224 | tf_op jit(solution)/shard_map/ppermute | solution.py:273
  6.3 14.1 %collective-permute-start = (bf16[32,2048]{1,0:T(8,128)(2,1)}, bf16[32,2048]{1,0:T(8,128)(2,1)S(1)}, u32[]{:S(2)}, u32[]{:S(2)}) collective-permute-start(bf16[32,2048]{1,0:T(8,128)(2,1)} %refs_0_.2), channel_id=1, source_target_pairs={{0,1},{1,0},{2,3},{3,2},{4,5},{5,4},{6,7},{7,6},{8,9},{9,8},{10,11... | collective-permute-start | bytes 393224 | tf_op jit(solution)/shard_map/ppermute | solution.py:273
  9.0 12.0 %collective-permute-start.2 = (bf16[32,2048]{1,0:T(8,128)(2,1)S(1)}, bf16[32,2048]{1,0:T(8,128)(2,1)S(1)}, u32[]{:S(2)}, u32[]{:S(2)}) collective-permute-start(bf16[32,2048]{1,0:T(8,128)(2,1)S(1)} %collective-permute-done.1.refs_2_), channel_id=1, source_target_pairs={{0,1},{1,0},{2,3},{3,2},{4,5},{5,4},{6,7},{7,6},{8,9},{9,8},{10,11... | collective-permute-start | bytes 393224 | tf_op jit(solution)/shard_map/ppermute | solution.py:273
  18.9 19.9 %collective-permute-start.9 = (bf16[64,3840]{1,0:T(8,128)(2,1)}, bf16[64,3840]{1,0:T(8,128)(2,1)S(1)}, u32[]{:S(2)}, u32[]{:S(2)}) collective-permute-start(bf16[64,3840]{1,0:T(8,128)(2,1)} %refs_0_.4), channel_id=1, source_target_pairs={{16,0},{24,8},{0,16},{8,24},{17,1},{25,9},{1,17},{9,25},{18,2},{26... | collective-permute-start | bytes 1474568 | tf_op jit(solution)/shard_map/ppermute | solution.py:270
  20.4 20.5 %collective-permute-start.10 = (bf16[64,3840]{1,0:T(8,128)(2,1)}, bf16[64,3840]{1,0:T(8,128)(2,1)S(1)}, u32[]{:S(2)}, u32[]{:S(2)}) collective-permute-start(bf16[64,3840]{1,0:T(8,128)(2,1)} %refs_2_.11), channel_id=1, source_target_pairs={{16,0},{24,8},{0,16},{8,24},{17,1},{25,9},{1,17},{9,25},{18,2},{26... | collective-permute-start | bytes 1474568 | tf_op jit(solution)/shard_map/ppermute | solution.py:270
  28.8 13.0 %collective-permute-start.12 = (bf16[128,1280]{1,0:T(8,128)(2,1)S(1)}, bf16[128,1280]{1,0:T(8,128)(2,1)S(1)}, u32[]{:S(2)}, u32[]{:S(2)}) collective-permute-start(bf16[128,1280]{1,0:T(8,128)(2,1)S(1)} %get-tuple-element.28), channel_id=1, source_target_pairs={{0,8},{8,0},{16,24},{24,16},{1,9},{9,1},{17,25},{25,17},{2,10},{10... | collective-permute-start | bytes 983048 | tf_op jit(solution)/shard_map/ppermute | solution.py:267
  28.9 15.2 %collective-permute-start.25 = (bf16[32,2048]{1,0:T(8,128)(2,1)S(1)}, bf16[32,2048]{1,0:T(8,128)(2,1)S(1)}, u32[]{:S(2)}, u32[]{:S(2)}) collective-permute-start(bf16[32,2048]{1,0:T(8,128)(2,1)S(1)} %copy-done.3), channel_id=1, source_target_pairs={{0,1},{1,0},{2,3},{3,2},{4,5},{5,4},{6,7},{7,6},{8,9},{9,8},{10,11... | collective-permute-start | bytes 393224 | tf_op jit(solution)/shard_map/ppermute | solution.py:273
  30.3 15.3 %collective-permute-start.26 = (bf16[32,2048]{1,0:T(8,128)(2,1)S(1)}, bf16[32,2048]{1,0:T(8,128)(2,1)S(1)}, u32[]{:S(2)}, u32[]{:S(2)}) collective-permute-start(bf16[32,2048]{1,0:T(8,128)(2,1)S(1)} %copy-done.3), channel_id=1, source_target_pairs={{0,2},{1,3},{2,0},{3,1},{4,6},{5,7},{6,4},{7,5},{8,10},{9,11},{10,... | collective-permute-start | bytes 393224 | tf_op jit(solution)/shard_map/ppermute | solution.py:273
  43.5 32.5 %collective-permute-start.32 = (bf16[128,3840]{1,0:T(8,128)(2,1)S(1)}, bf16[128,3840]{1,0:T(8,128)(2,1)S(1)}, u32[]{:S(2)}, u32[]{:S(2)}) collective-permute-start(bf16[128,3840]{1,0:T(8,128)(2,1)S(1)} %activations.1.a), channel_id=1, source_target_pairs={{0,8},{8,0},{16,24},{24,16},{1,9},{9,1},{17,25},{25,17},{2,10},{10... | collective-permute-start | bytes 2949128 | tf_op jit(solution)/shard_map/ppermute | solution.py:267
  44.0 21.0 %collective-permute-start.30 = (bf16[32,2048]{1,0:T(8,128)(2,1)S(1)}, bf16[32,2048]{1,0:T(8,128)(2,1)S(1)}, u32[]{:S(2)}, u32[]{:S(2)}) collective-permute-start(bf16[32,2048]{1,0:T(8,128)(2,1)S(1)} %copy-done.3), channel_id=1, source_target_pairs={{0,6},{1,7},{2,4},{3,5},{4,2},{5,3},{6,0},{7,1},{8,14},{9,15},{10,... | collective-permute-start | bytes 393224 | tf_op jit(solution)/shard_map/ppermute | solution.py:273
  45.6 24.1 %collective-permute-start.13 = (bf16[128,1280]{1,0:T(8,128)(2,1)S(1)}, bf16[128,1280]{1,0:T(8,128)(2,1)S(1)}, u32[]{:S(2)}, u32[]{:S(2)}) collective-permute-start(bf16[128,1280]{1,0:T(8,128)(2,1)S(1)} %add_convert_fusion.1.refs_0_), channel_id=1, source_target_pairs={{16,0},{24,8},{0,16},{8,24},{17,1},{25,9},{1,17},{9,25},{18,2},{26... | collective-permute-start | bytes 983048 | tf_op jit(solution)/shard_map/ppermute | solution.py:270
  47.1 16.1 %collective-permute-start.16 = (bf16[128,1280]{1,0:T(8,128)(2,1)S(1)}, bf16[128,1280]{1,0:T(8,128)(2,1)S(1)}, u32[]{:S(2)}, u32[]{:S(2)}) collective-permute-start(bf16[128,1280]{1,0:T(8,128)(2,1)S(1)} %add_convert_fusion.refs_0_), channel_id=1, source_target_pairs={{16,0},{24,8},{0,16},{8,24},{17,1},{25,9},{1,17},{9,25},{18,2},{26... | collective-permute-start | bytes 983048 | tf_op jit(solution)/shard_map/ppermute | solution.py:270
  47.9 27.5 %collective-permute-start.8 = (bf16[128,1280]{1,0:T(8,128)(2,1)S(1)}, bf16[128,1280]{1,0:T(8,128)(2,1)S(1)}, u32[]{:S(2)}, u32[]{:S(2)}) collective-permute-start(bf16[128,1280]{1,0:T(8,128)(2,1)S(1)} %add_convert_fusion.2.refs_0_), channel_id=1, source_target_pairs={{16,0},{24,8},{0,16},{8,24},{17,1},{25,9},{1,17},{9,25},{18,2},{26... | collective-permute-start | bytes 983048 | tf_op jit(solution)/shard_map/ppermute | solution.py:270
  65.1 20.5 %collective-permute-start.17 = (bf16[2,128,1280]{2,1,0:T(8,128)(2,1)S(1)}, bf16[2,128,1280]{2,1,0:T(8,128)(2,1)S(1)}, u32[]{:S(2)}, u32[]{:S(2)}) collective-permute-start(bf16[2,128,1280]{2,1,0:T(8,128)(2,1)S(1)} %hidden_grads.5.refs_0_), channel_id=1, source_target_pairs={{0,8},{8,0},{16,24},{24,16},{1,9},{9,1},{17,25},{25,17},{2,10},{10... | collective-permute-start | bytes 1966088 | tf_op jit(solution)/shard_map/ppermute | solution.py:267
  73.2 18.7 %collective-permute-start.14 = (bf16[2,128,1280]{2,1,0:T(8,128)(2,1)S(1)}, bf16[2,128,1280]{2,1,0:T(8,128)(2,1)S(1)}, u32[]{:S(2)}, u32[]{:S(2)}) collective-permute-start(bf16[2,128,1280]{2,1,0:T(8,128)(2,1)S(1)} %hidden_grads.4.refs_0_), channel_id=1, source_target_pairs={{0,8},{8,0},{16,24},{24,16},{1,9},{9,1},{17,25},{25,17},{2,10},{10... | collective-permute-start | bytes 1966088 | tf_op jit(solution)/shard_map/ppermute | solution.py:267
  76.0 22.4 %collective-permute-start.11 = (bf16[2,128,1280]{2,1,0:T(8,128)(2,1)S(1)}, bf16[2,128,1280]{2,1,0:T(8,128)(2,1)S(1)}, u32[]{:S(2)}, u32[]{:S(2)}) collective-permute-start(bf16[2,128,1280]{2,1,0:T(8,128)(2,1)S(1)} %hidden_grads.3.refs_1_.refs_0_), channel_id=1, source_target_pairs={{0,8},{8,0},{16,24},{24,16},{1,9},{9,1},{17,25},{25,17},{2,10},{10... | collective-permute-start | bytes 1966088 | tf_op jit(solution)/shard_map/ppermute | solution.py:267
  105.0 14.3 %collective-permute-start.23 = (bf16[32,2048]{1,0:T(8,128)(2,1)S(1)}, bf16[32,2048]{1,0:T(8,128)(2,1)S(1)}, u32[]{:S(2)}, u32[]{:S(2)}) collective-permute-start(bf16[32,2048]{1,0:T(8,128)(2,1)S(1)} %get-tuple-element.38), channel_id=1, source_target_pairs={{0,1},{1,0},{2,3},{3,2},{4,5},{5,4},{6,7},{7,6},{8,9},{9,8},{10,11... | collective-permute-start | bytes 393224 | tf_op jit(solution)/shard_map/ppermute | solution.py:273
  106.5 15.1 %collective-permute-start.21 = (bf16[32,2048]{1,0:T(8,128)(2,1)S(1)}, bf16[32,2048]{1,0:T(8,128)(2,1)S(1)}, u32[]{:S(2)}, u32[]{:S(2)}) collective-permute-start(bf16[32,2048]{1,0:T(8,128)(2,1)S(1)} %get-tuple-element.36), channel_id=1, source_target_pairs={{0,1},{1,0},{2,3},{3,2},{4,5},{5,4},{6,7},{7,6},{8,9},{9,8},{10,11... | collective-permute-start | bytes 393224 | tf_op jit(solution)/shard_map/ppermute | solution.py:273
  107.1 15.5 %collective-permute-start.19 = (bf16[32,2048]{1,0:T(8,128)(2,1)S(1)}, bf16[32,2048]{1,0:T(8,128)(2,1)S(1)}, u32[]{:S(2)}, u32[]{:S(2)}) collective-permute-start(bf16[32,2048]{1,0:T(8,128)(2,1)S(1)} %get-tuple-element.34), channel_id=1, source_target_pairs={{0,1},{1,0},{2,3},{3,2},{4,5},{5,4},{6,7},{7,6},{8,9},{9,8},{10,11... | collective-permute-start | bytes 393224 | tf_op jit(solution)/shard_map/ppermute | solution.py:273
  108.5 20.8 %collective-permute-start.18 = (bf16[32,2048]{1,0:T(8,128)(2,1)S(1)}, bf16[32,2048]{1,0:T(8,128)(2,1)S(1)}, u32[]{:S(2)}, u32[]{:S(2)}) collective-permute-start(bf16[32,2048]{1,0:T(8,128)(2,1)S(1)} %get-tuple-element.32), channel_id=1, source_target_pairs={{0,1},{1,0},{2,3},{3,2},{4,5},{5,4},{6,7},{7,6},{8,9},{9,8},{10,11... | collective-permute-start | bytes 393224 | tf_op jit(solution)/shard_map/ppermute | solution.py:273
  119.3 9.9 %collective-permute-start.24 = (bf16[32,2048]{1,0:T(8,128)(2,1)S(1)}, bf16[32,2048]{1,0:T(8,128)(2,1)S(1)}, u32[]{:S(2)}, u32[]{:S(2)}) collective-permute-start(bf16[32,2048]{1,0:T(8,128)(2,1)S(1)} %add_convert_fusion.4), channel_id=1, source_target_pairs={{0,2},{1,3},{2,0},{3,1},{4,6},{5,7},{6,4},{7,5},{8,10},{9,11},{10,... | collective-permute-start | bytes 393224 | tf_op jit(solution)/shard_map/ppermute | solution.py:273
  121.6 11.9 %collective-permute-start.22 = (bf16[32,2048]{1,0:T(8,128)(2,1)S(1)}, bf16[32,2048]{1,0:T(8,128)(2,1)S(1)}, u32[]{:S(2)}, u32[]{:S(2)}) collective-permute-start(bf16[32,2048]{1,0:T(8,128)(2,1)S(1)} %add_convert_fusion.5), channel_id=1, source_target_pairs={{0,4},{1,5},{2,6},{3,7},{4,0},{5,1},{6,2},{7,3},{8,12},{9,13},{10,... | collective-permute-start | bytes 393224 | tf_op jit(solution)/shard_map/ppermute | solution.py:273
  122.7 10.9 %collective-permute-start.20 = (bf16[32,2048]{1,0:T(8,128)(2,1)S(1)}, bf16[32,2048]{1,0:T(8,128)(2,1)S(1)}, u32[]{:S(2)}, u32[]{:S(2)}) collective-permute-start(bf16[32,2048]{1,0:T(8,128)(2,1)S(1)} %add_convert_fusion.6), channel_id=1, source_target_pairs={{0,6},{1,7},{2,4},{3,5},{4,2},{5,3},{6,0},{7,1},{8,14},{9,15},{10,... | collective-permute-start | bytes 393224 | tf_op jit(solution)/shard_map/ppermute | solution.py:273
  (13 other events, 103.7 us)

commit v2 on v0

v2 whole, which is shorter than its diff:
```python
import functools
import math

import jax
import jax.numpy as jnp
from jax import lax
from jax.experimental import pallas as pl
from jax.experimental.pallas import tpu as pltpu
from jax.sharding import PartitionSpec as P

F32 = jnp.float32
BF16 = jnp.bfloat16
CORES = 2
VMEM = 10 * 2**20
ANYWHERE = pl.BlockSpec(memory_space=pl.ANY)
REMAIN = pl.BlockSpec(memory_space=pltpu.HBM)
RESIDENT = pl.BlockSpec(memory_space=pltpu.VMEM)
SCALARS = pl.BlockSpec(memory_space=pltpu.SMEM)
WHOLE = pl.BlockSpec(memory_space=pltpu.VMEM)
NT = (((1,), (1,)), ((), ()))
TN = (((0,), (0,)), ((), ()))


def divisor(size, target, step=128):
    best = size
    for cand in range(step, target + 1, step):
        if size % cand == 0:
            best = cand
    return best


def call(kernel, operands, in_specs, out_shape, out_specs, deps=(), scratch=(), aliases=None, **kwargs):
    given = len(operands)
    total = given + len(deps)
    kept = {id(REMAIN): pltpu.HBM, id(RESIDENT): pltpu.VMEM}
    operands = [
        pltpu.with_memory_space_constraint(operand, kept[id(spec)]) if id(spec) in kept else operand
        for operand, spec in zip(operands, in_specs)
    ]

    held = sum(math.prod(s.shape) * s.dtype.itemsize for s in scratch if s.memory_space is pltpu.VMEM)

    def body(*refs):
        kernel(*refs[:given], *refs[total:])

    return pl.pallas_call(
        body,
        out_shape=out_shape,
        in_specs=list(in_specs) + [ANYWHERE] * len(deps),
        out_specs=out_specs,
        scratch_shapes=list(scratch),
        input_output_aliases=aliases or {},
        compiler_params=pltpu.CompilerParams(vmem_limit_bytes=VMEM + held),
        **kwargs,
    )(*operands, *deps)


def lay(blocks, offs, out, rows, first=0):
    i = first
    for block in blocks:
        for lo in range(0, block.shape[0], rows):
            out[pl.ds(pl.multiple_of(offs[i], rows), rows), :] = block[lo : lo + rows, :]
            i += 1


def assemble(blocks, offsets, deps=()):
    count, width = len(blocks), blocks[0].shape[1]
    tokens = sum(block.shape[0] for block in blocks)
    rows = tokens // offsets.shape[0]

    def kernel(offs, *refs):
        lay(refs[:count], offs, refs[count], rows)

    return call(
        kernel,
        [offsets, *blocks],
        [SCALARS] + [WHOLE] * count,
        jax.ShapeDtypeStruct((tokens, width), BF16),
        WHOLE,
        deps,
        name="assemble",
    )


def copies_of(weight, lo, units, piece, ready, sems):
    copies = []
    for i in range(units // piece):
        at = pl.ds(i * piece, piece)
        copies.append(
            pltpu.make_async_copy(weight.at[pl.ds(lo + i * piece, piece)], ready.at[at], sems.at[i])
        )
        copies[-1].start()
    return copies


def dots_of(a, copies, piece, ready, keep, send):
    half = keep.shape[0]
    for i, copy in enumerate(copies):
        copy.wait()
        at = slice(i * piece, (i + 1) * piece)
        part = lax.dot_general(a[...], ready[at, :], NT, preferred_element_type=F32).astype(BF16)
        keep[:, at] = part[:half]
        send[:, at] = part[half:]


def first_partial(blocks, offsets, down, span, deps=()):
    count, width = len(blocks), blocks[0].shape[1]
    tokens = sum(block.shape[0] for block in blocks)
    run = tokens // offsets.shape[0]
    lo, units = span
    piece = divisor(units, 640)
    pieces = units // piece

    def kernel(offs, *refs):
        own, others, weight = refs[0], refs[1:count], refs[count]
        keep, send, a, ready, sems = refs[count + 1 :]
        moves = []
        if count > 1:
            at = pl.ds(pl.multiple_of(offs[0], run), run)
            moves.append(pltpu.make_async_copy(own, a.at[at], sems.at[pieces]))
            moves[0].start()
        copies = copies_of(weight, lo, units, piece, ready, sems)
        lay(others if count > 1 else [own], offs, a, run, 1 if count > 1 else 0)
        for move in moves:
            move.wait()
        dots_of(a, copies, piece, ready, keep, send)

    part = jax.ShapeDtypeStruct((tokens // CORES, units), BF16)
    return call(
        kernel,
        [offsets, *blocks, down],
        [SCALARS, REMAIN if count > 1 else WHOLE] + [WHOLE] * (count - 1) + [REMAIN],
        (part, part, jax.ShapeDtypeStruct((tokens, width), BF16)),
        [WHOLE] * 3,
        deps,
        scratch=[pltpu.VMEM((units, width), BF16), pltpu.SemaphoreType.DMA((pieces + 1,))],
        name="first_partial",
    )


def activations(gates, ups, deps=()):
    count = len(gates)
    rows, width = gates[0].shape

    def kernel(*refs):
        out = refs[2 * count]
        for i in range(count):
            gate = refs[i][...].astype(F32)
            up = refs[count + i][...].astype(F32)
            out[i * rows : (i + 1) * rows, :] = (gate * jax.nn.sigmoid(gate) * up).astype(BF16)

    return call(
        kernel,
        [*gates, *ups],
        [WHOLE] * (2 * count),
        jax.ShapeDtypeStruct((rows * count, width), BF16),
        WHOLE,
        deps,
        name="activations",
    )


def hidden_grads(sums, gates, ups, span, passed=(), deps=()):
    count = len(gates)
    rows = gates[0].shape[0]
    lo, units = span
    cols = slice(lo, lo + units)

    def kernel(*refs):
        out = refs[3 * count + len(passed)]
        for i in range(count):
            grad = 0.0
            for o in range(count):
                j = (i - o) % count
                grad = grad + refs[o][j * rows : (j + 1) * rows, :].astype(F32)
            gate = refs[count + i][:, cols].astype(F32)
            up = refs[2 * count + i][:, cols].astype(F32)
            sig = jax.nn.sigmoid(gate)
            at = slice(i * rows, (i + 1) * rows)
            out[0, at, :] = (grad * up * sig * (1.0 + gate * (1.0 - sig))).astype(BF16)
            out[1, at, :] = (grad * gate * sig).astype(BF16)

    shapes = [jax.ShapeDtypeStruct((2, rows * count, units), BF16)]
    shapes += [jax.ShapeDtypeStruct(p.shape, p.dtype) for p in passed]
    return call(
        kernel,
        [*sums, *gates, *ups, *passed],
        [WHOLE] * (3 * count) + [ANYWHERE] * len(passed),
        shapes,
        [WHOLE] + [ANYWHERE] * len(passed),
        deps,
        aliases={3 * count + i: 1 + i for i in range(len(passed))},
        name="hidden_grads",
    )


def both(mine, other, *at):
    return jnp.concatenate([mine[at], other[at]], axis=0)


def down_grad(hidden, hidden_other, out_all, down=None, span=(0, 0), deps=()):
    half, units = hidden.shape
    tokens, width = out_all.shape
    piece = divisor(units, 256)
    count = units // piece
    slots = min(8, count)
    lo, taken = span
    operands, specs = [hidden, hidden_other, out_all], [WHOLE] * 3
    shapes = [jax.ShapeDtypeStruct((units, width), BF16), jax.ShapeDtypeStruct((8, 128), F32)]
    scratch = [pltpu.VMEM((slots, piece, width), BF16), pltpu.SemaphoreType.DMA((slots,))]
    if taken:
        operands.append(down)
        specs.append(REMAIN)
        shapes += [jax.ShapeDtypeStruct((half, taken), BF16)] * 2
        run = divisor(taken, 640)
        scratch += [pltpu.VMEM((taken, width), BF16), pltpu.SemaphoreType.DMA((taken // run,))]

    def kernel(*refs):
        a, b, g = refs[:3]
        given = len(operands)
        out, token = refs[given : given + 2]
        ready, sems = refs[given + len(shapes) : given + len(shapes) + 2]
        token[...] = jnp.zeros(token.shape, F32)
        if taken:
            copies = copies_of(refs[3], lo, taken, run, refs[-2], refs[-1])
        stores = []
        for i in range(count):
            at, slot = slice(i * piece, (i + 1) * piece), i % slots
            if i >= slots:
                stores[i - slots].wait()
            ready[slot] = lax.dot_general(
                both(a, b, slice(None), at), g[...], TN, preferred_element_type=F32
            ).astype(BF16)
            store = pltpu.make_async_copy(ready.at[slot], out.at[at], sems.at[slot])
            store.start()
            stores.append(store)
        if taken:
            dots_of(g, copies, run, refs[-2], refs[given + 2], refs[given + 3])
        for store in stores[count - slots :]:
            store.wait()

    return call(
        kernel,
        operands,
        specs,
        shapes,
        [REMAIN] + [WHOLE] * (len(shapes) - 1),
        deps,
        scratch=scratch,
        name="down_grad",
    )


def input_grads(mine, other, gate_weight, up_weight, before, offsets, span, rows, groups, deps=()):
    _, half, units = mine.shape
    tokens = 2 * half
    width = gate_weight.shape[0]
    piece = divisor(width, 512)
    pieces = width // piece
    slots = min(4, pieces)
    cols = slice(span[0], span[0] + units)
    operands = [offsets, mine, other, gate_weight, up_weight] + ([] if before is None else [before])
    specs = [SCALARS, WHOLE, WHOLE, REMAIN, REMAIN] + ([] if before is None else [WHOLE])
    if groups is None:
        shapes = [jax.ShapeDtypeStruct((tokens, width), F32)]
    else:
        shapes = [jax.ShapeDtypeStruct((rows * len(group), width), BF16) for group in groups]

    def kernel(*refs):
        offs, a, b, gw, uw = refs[:5]
        outs = refs[len(operands) : len(operands) + len(shapes)]
        sums, ready, sems = refs[-3:]
        copies = []
        for j in range(pieces):
            at = slice(j * piece, (j + 1) * piece)
            for i, w in enumerate((gw, uw)):
                copies.append(
                    pltpu.make_async_copy(
                        w.at[at, cols], ready.at[i, j % slots], sems.at[i, j % slots]
                    )
                )
        for copy in copies[: 2 * slots]:
            copy.start()
        for j in range(pieces):
            at = slice(j * piece, (j + 1) * piece)
            total = 0.0 if before is None else refs[5][:, at]
            for i in range(2):
                copies[2 * j + i].wait()
            for i in range(2):
                total = total + lax.dot_general(
                    both(a, b, i), ready[i, j % slots], NT, preferred_element_type=F32
                )
            sums[:, at] = total
            for copy in copies[2 * (j + slots) : 2 * (j + slots + 1)]:
                copy.start()
        if groups is None:
            outs[0][...] = sums[...]
        for out, group in zip(outs, groups or ()):
            for i, m in enumerate(group):
                at = pl.ds(pl.multiple_of(offs[m], rows), rows)
                out[i * rows : (i + 1) * rows, :] = sums[at, :].astype(BF16)

    return call(
        kernel,
        operands,
        specs,
        shapes,
        [WHOLE] * len(shapes),
        deps,
        scratch=[
            pltpu.VMEM((tokens, width), F32),
            pltpu.VMEM((2, slots, piece, units), BF16),
            pltpu.SemaphoreType.DMA((2, slots)),
        ],
        name="input_grads",
    )


def fold(own, other, deps=()):
    rows, width = own.shape[0] // 2, own.shape[1]

    def kernel(a, b, *outs):
        for i, out in enumerate(outs[:2]):
            at = slice(i * rows, (i + 1) * rows)
            total = a[at, :].astype(F32) + b[at, :].astype(F32)
            out[...] = total.astype(BF16)
        outs[2][...] = total

    shape = (rows, width)
    return call(
        kernel,
        [own, other],
        [WHOLE] * 2,
        (
            jax.ShapeDtypeStruct(shape, BF16),
            jax.ShapeDtypeStruct(shape, BF16),
            jax.ShapeDtypeStruct(shape, F32),
        ),
        [WHOLE] * 3,
        deps,
        name="fold",
    )


def weight_grads(mine, other, in_all, before, start, span, whole, deps=()):
    skip, units = span[0] - start, span[1]
    tokens, width = in_all.shape
    piece = divisor(width, 256)
    count = width // piece
    slots = min(8, count)
    cols = slice(span[0], span[0] + units)

    def kernel(*refs):
        a, b, x = refs[:3]
        outs, token, ready, sems = refs[-5:-3], refs[-3], refs[-2], refs[-1]
        token[...] = jnp.zeros(token.shape, F32)
        taken = slice(skip, skip + units)
        copies = []
        for j in range(count):
            at, slot = slice(j * piece, (j + 1) * piece), j % slots
            for i in range(2):
                if j >= slots:
                    copies[2 * (j - slots) + i].wait()
                ready[i, slot] = lax.dot_general(
                    x[:, at], both(a, b, i, slice(None), taken), TN, preferred_element_type=F32
                ).astype(BF16)
                copy = pltpu.make_async_copy(
                    ready.at[i, slot], outs[i].at[at, cols], sems.at[i, slot]
                )
                copy.start()
                copies.append(copy)
        for copy in copies[2 * (count - slots) :]:
            copy.wait()

    shape = jax.ShapeDtypeStruct((width, whole), BF16)
    return call(
        kernel,
        [mine, other, in_all, *(before or ())],
        [WHOLE] * 3 + [REMAIN] * (2 if before else 0),
        (shape, shape, jax.ShapeDtypeStruct((8, 128), F32)),
        [REMAIN, REMAIN, WHOLE],
        deps,
        scratch=[
            pltpu.VMEM((2, slots, piece, units), BF16),
            pltpu.SemaphoreType.DMA((2, slots)),
        ],
        aliases={3: 0, 4: 1} if before else None,
        name="weight_grads",
    )


def local(nr, nc, inputs, grad_out, gate, up, gate_weight, up_weight, down_weight):
    nx = nr // CORES
    row, col = lax.axis_index("row"), lax.axis_index("col")
    x, core = row // CORES, row % CORES
    own_tokens = gate.shape[0]
    col_tokens = grad_out.shape[0]
    units = down_weight.shape[0]
    first = units // 3 * 2 if units % 384 == 0 else units
    spans = [(0, first)] + ([(first, units - first)] if first < units else [])
    direct = nc == 8 and nr * own_tokens == nc * col_tokens and own_tokens % col_tokens == 0

    def swap_core(value):
        return lax.ppermute(value, "row", [(r, r ^ 1) for r in range(nr)])

    def from_x(value, offset):
        return lax.ppermute(value, "row", [((r + offset * CORES) % nr, r) for r in range(nr)])

    def swap_col(value, mask):
        return lax.ppermute(value, "col", [(c, c ^ mask) for c in range(nc)])

    def place(block):
        block_x, block_core = block // CORES, block % CORES
        return ((block_core ^ core) * nx + (block_x - x + nx) % nx) * own_tokens

    in_order = jnp.stack([place(r) for r in range(nr)]).astype(jnp.int32)
    if direct:
        rows, per = col_tokens, own_tokens // col_tokens
        places = [place((col ^ m) // per) + ((col ^ m) % per) * rows for m in range(nc)]
        offsets = jnp.stack(places).astype(jnp.int32)
    else:
        rows, offsets = own_tokens, in_order

    def gather(value):
        if not direct:
            return [lax.all_gather(value, "col", axis=0, tiled=True)]
        got = {0: value}
        got[1] = swap_col(value, 1)
        got[4] = swap_col(value, 4)
        got[2] = swap_col(value, 2)
        got[3] = swap_col(got[1], 2)
        got[6] = swap_col(got[4], 2)
        got[5] = swap_col(got[4], 1)
        got[7] = swap_col(got[6], 1)
        return [got[m] for m in range(nc)]

    gates = [gate] + [from_x(gate, o) for o in range(1, nx)]
    ups = [up] + [from_x(up, o) for o in range(1, nx)]

    def exchanged(keep, send):
        total = (keep.astype(F32) + swap_core(send).astype(F32)).astype(BF16)
        return [total] + [from_x(total, o) for o in range(1, nx)]

    out_blocks = gather(grad_out)
    hidden = activations(gates, ups, deps=out_blocks[-2:-1])
    keep, send, out_all = first_partial(
        out_blocks, offsets, down_weight, spans[0], deps=[hidden]
    )
    hidden_other = swap_core(hidden)
    sums = [exchanged(keep, send)]
    if direct:
        own = jnp.concatenate([inputs, swap_col(inputs, 1)], axis=0)
        in_blocks = [own, swap_col(own, 2), swap_col(own, 4)]
    else:
        own = sums[0][0]
        in_blocks = [lax.all_gather(inputs, "col", axis=0, tiled=True)]
    span = spans[1] if len(spans) > 1 else (0, 0)
    grad_down, token, *parts = down_grad(
        hidden, hidden_other, out_all, down_weight, span, deps=[sums[0][0], own]
    )

    mine, *parts = hidden_grads(sums[0], gates, ups, spans[0], parts, [token, *in_blocks])
    grads = [(mine, swap_core(mine))]
    groups = [(7, 5), (3, 1), (6, 4), (2, 0)] if direct else [range(nr)]
    if direct:
        in_blocks.append(swap_col(in_blocks[2], 2))
    total = None
    if len(spans) > 1:
        sums.append(exchanged(*parts))
        (total,) = input_grads(
            *grads[0], gate_weight, up_weight, None, offsets, spans[0], rows, None, sums[1][:1]
        )
        (mine,) = hidden_grads(sums[1], gates, ups, spans[1], deps=[total, *in_blocks])
        grads.append((mine, swap_core(mine)))
    blocks = input_grads(
        *grads[-1], gate_weight, up_weight, total, offsets, spans[-1], rows, groups
    )
    in_all = assemble(in_blocks, offsets if direct else in_order, deps=blocks[:1])

    def weight_part(before, i, span, deps):
        *weights, token = weight_grads(
            *grads[i], in_all, before, spans[i][0], span, units, deps
        )
        return weights, token

    cut = divisor(first, first // 2)
    weights, token = weight_part(None, 0, (0, cut), [])
    if direct:
        far, near = swap_col(blocks[0], 1), swap_col(blocks[1], 1)
        sent6, sent4, _ = fold(blocks[2], far, deps=[token])
        part6, part4 = swap_col(sent6, 6), swap_col(sent4, 4)
        ready = sent4
    else:
        ready = blocks[0]
    if cut < first:
        weights, token = weight_part(weights, 0, (cut, first - cut), [ready])
    if direct:
        sent2, _, result = fold(blocks[3], near, deps=[token, part6])
        part2 = swap_col(sent2, 2)
        ready = sent2
    if len(spans) > 1:
        weights, token = weight_part(weights, 1, spans[1], [ready])
    if direct:
        for part in (part6, part4, part2):
            result = result + part.astype(F32)
        grad_inputs = result.astype(BF16)
    else:
        grad_inputs = lax.psum_scatter(blocks[0], "col", scatter_dimension=0, tiled=True)
    return grad_inputs, *weights, grad_down


def solution(mesh):
    return jax.shard_map(
        functools.partial(local, mesh.shape["row"], mesh.shape["col"]),
        mesh=mesh,
        in_specs=(
            P("col", "row"),
            P("col", "row"),
            P("row", "col"),
            P("row", "col"),
            P("row", "col"),
            P("row", "col"),
            P("col", "row"),
        ),
        out_specs=(P("col", "row"), P("row", "col"), P("row", "col"), P("col", "row")),
        check_vma=False,
    )
```

time: 288 us -> 111 us (0.39)
  waiting for transfers between devices: 169 us -> 21.4 us
  matrix products: 58.2 us -> 0 us
  Pallas kernels: 0 us -> 50.3 us
  local copies, waits for them, and re-layouts: 41.5 us -> 2.18 us
  starting transfers between devices: 0.45 us -> 35.2 us
  between operations: 14.1 us -> 0.87 us
  other arithmetic: 4.24 us -> 0.95 us
    all_gather x5 -> x0, waiting for transfers between devices: 111 us -> none  [the longest x1 45.1 us: local(): out_all = lax.all_gather(grad_out, 'col', axis=0, tiled=True)]
    dot_general x6 -> x0, matrix products: 58.2 us -> none  [the longest x1 11.6 us: local(): lax.dot_general(up_rows, up_weight, contract_last, preferred_element_type...]
    reduce_scatter x2 -> x0, waiting for transfers between devices: 54.8 us -> none  [the longest x1 29.5 us: local(): lax.psum_scatter(lax.dot_general(out_all, down_weight, contract_last, pre...]
    pallas_call x0 -> x13, Pallas kernels: none -> 50.3 us  [call(): pl.pallas_call(body, out_shape=out_shape, in_specs=list(in_specs) + [ANYW...]
    unnamed x14 -> x11, local copies, waits for them, and re-layouts: 41.5 us -> 2.09 us
    ppermute x0 -> x25, starting transfers between devices: none -> 35.2 us  [the longest x16 27.8 us: swap_col(): return lax.ppermute(value, 'col', [(c, c ^ mask) for c in range(nc)])]
    ppermute x0 -> x25, waiting for transfers between devices: none -> 21.4 us  [the longest x16 12.1 us: swap_col(): return lax.ppermute(value, 'col', [(c, c ^ mask) for c in range(nc)])]
    convert_element_type x2 -> x3, other arithmetic: 4.24 us -> 0.95 us  [the longest x1 0.73 us: local(): grad_inputs = result.astype(BF16)]
  transfers between devices with their start and end apart: 7 -> 25, of which waited for: 6 -> 11; matrix products, arithmetic and copies ran while one was open for 31% -> 0% of each run, Pallas kernels for 0% -> 32%
where the time goes in v2:
time: 111 us
  Pallas kernels  50.3 us (45%)
  starting transfers between devices  35.2 us (32%)
  waiting for transfers between devices  21.4 us (19%)
  local copies, waits for them, and re-layouts  2.18 us (2%)
    pallas_call x13, Pallas kernels, call(): pl.pallas_call(body, out_shape=out_shape, in_specs=list(in_specs) + [ANYW...  50.3 us
    ppermute x16, starting transfers between devices, swap_col(): return lax.ppermute(value, 'col', [(c, c ^ mask) for c in range(nc)])  27.8 us
    ppermute x16, waiting for transfers between devices, swap_col(): return lax.ppermute(value, 'col', [(c, c ^ mask) for c in range(nc)])  12.1 us
    ppermute x4, starting transfers between devices, from_x(): lax.ppermute(value, 'row', [((r + offset * CORES) % nr, r) for r in range...  6.49 us
    ppermute x5, waiting for transfers between devices, swap_core(): return lax.ppermute(value, 'row', [(r, r ^ 1) for r in range(nr)])  5.17 us
    ppermute x4, waiting for transfers between devices, from_x(): lax.ppermute(value, 'row', [((r + offset * CORES) % nr, r) for r in range...  4.07 us
  transfers between devices with their start and end apart: 25, of which 11 were waited for; matrix products, arithmetic and copies ran while one was open for 0% of the time, Pallas kernels for 32%

profile of v2, /device:TPU:0, one launch (start us, length us, event | category | flops | bytes accessed | tf_op | source)
XLA Modules:
  0.0 110.8 jit_solution(10051781652863156800)
XLA Ops:
  0.6 3.0 %collective-permute-start.7 = (bf16[64,3840]{1,0:T(8,128)(2,1)}, bf16[64,3840]{1,0:T(8,128)(2,1)S(1)}, u32[]{:S(2)}, u32[]{:S(2)}) collective-permute-start(bf16[64,3840]{1,0:T(8,128)(2,1)} %refs_2_.5), channel_id=1, source_target_pairs={{16,0},{24,8},{0,16},{8,24},{17,1},{25,9},{1,17},{9,25},{18,2},{26... | collective-permute-start | bytes 1474568 | tf_op jit(solution)/shard_map/ppermute | solution.py:407
  3.7 3.0 %collective-permute-start.3 = (bf16[32,2048]{1,0:T(8,128)(2,1)}, bf16[32,2048]{1,0:T(8,128)(2,1)S(1)}, u32[]{:S(2)}, u32[]{:S(2)}) collective-permute-start(bf16[32,2048]{1,0:T(8,128)(2,1)} %refs_1_.1), channel_id=1, source_target_pairs={{0,4},{1,5},{2,6},{3,7},{4,0},{5,1},{6,2},{7,3},{8,12},{9,13},{10,... | collective-permute-start | bytes 393224 | tf_op jit(solution)/shard_map/ppermute | solution.py:410
  8.3 4.4 %collective-permute-done.3.refs_5_ = bf16[32,2048]{1,0:T(8,128)(2,1)S(1)} collective-permute-done((bf16[32,2048]{1,0:T(8,128)(2,1)}, bf16[32,2048]{1,0:T(8,128)(2,1)S(1)}, u32[]{:S(2)}, u32[]{:S(2)}) %collective-permute-start.3) | collective-permute-done | bytes 131104 | tf_op jit(solution)/shard_map/ppermute | solution.py:410
  16.3 2.4 %collective-permute-done.5.refs_4_.refs_7_ = bf16[32,2048]{1,0:T(8,128)(2,1)S(1)} collective-permute-done((bf16[32,2048]{1,0:T(8,128)(2,1)S(1)}, bf16[32,2048]{1,0:T(8,128)(2,1)S(1)}, u32[]{:S(2)}, u32[]{:S(2)}) %collective-permute-start.5) | collective-permute-done | bytes 131104 | tf_op jit(solution)/shard_map/ppermute | solution.py:410
  21.5 4.1 %collective-permute-done.8.refs_3_.refs_5_ = bf16[64,3840]{1,0:T(8,128)(2,1)S(1)} collective-permute-done((bf16[64,3840]{1,0:T(8,128)(2,1)}, bf16[64,3840]{1,0:T(8,128)(2,1)S(1)}, u32[]{:S(2)}, u32[]{:S(2)}) %collective-permute-start.8) | collective-permute-done | bytes 491552 | tf_op jit(solution)/shard_map/ppermute | solution.py:407
  28.2 7.5 %first_partial.1 = (bf16[128,2560]{1,0:T(8,128)(2,1)S(1)}, bf16[128,2560]{1,0:T(8,128)(2,1)S(1)}, bf16[256,2048]{1,0:T(8,128)(2,1)S(1)}) custom-call(s32[8]{0:T(128)S(1)} %stack.35.refs_0_, bf16[32,2048]{1,0:T(8,128)(2,1)} %refs_1_.1, bf16[32,2048]{1,0:T(8,128)(2,1)S(1)} %collective-permute-done.refs_2_, ...), custom_call_target="tpu_custom_call" | custom-call | tf_op jit(solution)/shard_map/first_partial/pallas_call | solution.py:46
  35.8 1.8 %collective-permute-start.12 = (bf16[32,2048]{1,0:T(8,128)(2,1)S(1)}, bf16[32,2048]{1,0:T(8,128)(2,1)S(1)}, u32[]{:S(2)}, u32[]{:S(2)}) collective-permute-start(bf16[32,2048]{1,0:T(8,128)(2,1)S(1)} %copy-done.4), channel_id=1, source_target_pairs={{0,1},{1,0},{2,3},{3,2},{4,5},{5,4},{6,7},{7,6},{8,9},{9,8},{10,11... | collective-permute-start | bytes 393224 | tf_op jit(solution)/shard_map/ppermute | solution.py:410
  38.0 1.8 %collective-permute-start.10 = (bf16[128,2560]{1,0:T(8,128)(2,1)S(1)}, bf16[128,2560]{1,0:T(8,128)(2,1)S(1)}, u32[]{:S(2)}, u32[]{:S(2)}) collective-permute-start(bf16[128,2560]{1,0:T(8,128)(2,1)S(1)} %add_convert_fusion.refs_4_.refs_0_), channel_id=1, source_target_pairs={{16,0},{24,8},{0,16},{8,24},{17,1},{25,9},{1,17},{9,25},{18,2},{26... | collective-permute-start | bytes 1966088 | tf_op jit(solution)/shard_map/ppermute | solution.py:407
  39.8 1.9 %collective-permute-done.12 = bf16[32,2048]{1,0:T(8,128)(2,1)S(1)} collective-permute-done((bf16[32,2048]{1,0:T(8,128)(2,1)S(1)}, bf16[32,2048]{1,0:T(8,128)(2,1)S(1)}, u32[]{:S(2)}, u32[]{:S(2)}) %collective-permute-start.12) | collective-permute-done | bytes 131104 | tf_op jit(solution)/shard_map/ppermute | solution.py:410
  41.7 2.9 %collective-permute-start.14 = (bf16[64,2048]{1,0:T(8,128)(2,1)S(1)}, bf16[64,2048]{1,0:T(8,128)(2,1)S(1)}, u32[]{:S(2)}, u32[]{:S(2)}) collective-permute-start(bf16[64,2048]{1,0:T(8,128)(2,1)S(1)} %constant_dynamic-update-slice_fusion.refs_5_.refs_9_.refs_7_.refs_1_), channel_id=1, source_target_pairs={{0,4},{1,5},{2,6},{3,7},{4,0},{5,1},{6,2},{7,3},{8,12},{9,13},{10,... | collective-permute-start | bytes 786440 | tf_op jit(solution)/shard_map/ppermute | solution.py:410
  44.6 1.6 %collective-permute-start.13 = (bf16[64,2048]{1,0:T(8,128)(2,1)S(1)}, bf16[64,2048]{1,0:T(8,128)(2,1)S(1)}, u32[]{:S(2)}, u32[]{:S(2)}) collective-permute-start(bf16[64,2048]{1,0:T(8,128)(2,1)S(1)} %constant_dynamic-update-slice_fusion.refs_5_.refs_9_.refs_7_.refs_1_), channel_id=1, source_target_pairs={{0,2},{1,3},{2,0},{3,1},{4,6},{5,7},{6,4},{7,5},{8,10},{9,11},{10,... | collective-permute-start | bytes 786440 | tf_op jit(solution)/shard_map/ppermute | solution.py:410
  46.2 9.4 %down_grad.1 = (bf16[3840,2048]{1,0:T(8,128)(2,1)}, f32[8,128]{1,0:T(8,128)S(1)}, bf16[128,1280]{1,0:T(8,128)(2,1)S(1)}, bf16[128,1280]{1,0:T(8,128)(2,1)S(1)}) custom-call(bf16[128,3840]{1,0:T(8,128)(2,1)S(1)} %activations.1.refs_10_.refs_0_, bf16[128,3840]{1,0:T(8,128)(2,1)S(1)} %collective-permute-done.11.refs_1_, ...), custom_call_target="tpu_custom_call" | custom-call | tf_op jit(solution)/shard_map/down_grad/pallas_call | solution.py:46
  58.2 3.0 %collective-permute-done.15 = bf16[128,1280]{1,0:T(8,128)(2,1)S(1)} collective-permute-done((bf16[128,1280]{1,0:T(8,128)(2,1)S(1)}, bf16[128,1280]{1,0:T(8,128)(2,1)S(1)}, u32[]{:S(2)}, u32[]{:S(2)}) %collective-permute-start.15) | collective-permute-done | bytes 327712 | tf_op jit(solution)/shard_map/ppermute | solution.py:404
  61.2 1.6 %collective-permute-start.16 = (bf16[128,1280]{1,0:T(8,128)(2,1)S(1)}, bf16[128,1280]{1,0:T(8,128)(2,1)S(1)}, u32[]{:S(2)}, u32[]{:S(2)}) collective-permute-start(bf16[128,1280]{1,0:T(8,128)(2,1)S(1)} %add_convert_fusion.1.refs_5_.refs_0_), channel_id=1, source_target_pairs={{16,0},{24,8},{0,16},{8,24},{17,1},{25,9},{1,17},{9,25},{18,2},{26... | collective-permute-start | bytes 983048 | tf_op jit(solution)/shard_map/ppermute | solution.py:407
  64.3 9.5 %input_grads.2.refs_6_.refs_5_ = f32[256,2048]{1,0:T(8,128)S(1)} custom-call(s32[8]{0:T(128)S(1)} %stack.35.refs_0_, bf16[2,128,2560]{2,1,0:T(8,128)(2,1)S(1)} %get-tuple-element.38.refs_1_.refs_0_, bf16[2,128,2560]{2,1,0:T(8,128)(2,1)S(1)} %collective-permute-done.17.refs_2_.refs_1_, bf16[2048,3840]{1,0:T(8,128)(2,1)} %refs_3_.5, ...), custom_call_target="tpu_custom_call" | custom-call | tf_op jit(solution)/shard_map/input_grads/pallas_call | solution.py:46
  74.2 2.1 %collective-permute-done.19.refs_2_.refs_1_ = bf16[2,128,1280]{2,1,0:T(8,128)(2,1)S(1)} collective-permute-done((bf16[2,128,1280]{2,1,0:T(8,128)(2,1)S(1)}, bf16[2,128,1280]{2,1,0:T(8,128)(2,1)S(1)}, u32[]{:S(2)}, u32[]{:S(2)}) %collective-permute-start.19) | collective-permute-done | bytes 655392 | tf_op jit(solution)/shard_map/ppermute | solution.py:404
  76.3 6.0 %input_grads.3 = (bf16[64,2048]{1,0:T(8,128)(2,1)S(1)}, bf16[64,2048]{1,0:T(8,128)(2,1)S(1)}, bf16[64,2048]{1,0:T(8,128)(2,1)S(1)}, bf16[64,2048]{1,0:T(8,128)(2,1)S(1)}) custom-call(s32[8]{0:T(128)S(1)} %stack.35.refs_0_, bf16[2,128,1280]{2,1,0:T(8,128)(2,1)S(1)} %hidden_grads.3.refs_1_.refs_0_, ...), custom_call_target="tpu_custom_call" | custom-call | tf_op jit(solution)/shard_map/input_grads/pallas_call | solution.py:46
  82.3 1.6 %collective-permute-start.21 = (bf16[64,2048]{1,0:T(8,128)(2,1)S(1)}, bf16[64,2048]{1,0:T(8,128)(2,1)S(1)}, u32[]{:S(2)}, u32[]{:S(2)}) collective-permute-start(bf16[64,2048]{1,0:T(8,128)(2,1)S(1)} %get-tuple-element.41.refs_5_), channel_id=1, source_target_pairs={{0,1},{1,0},{2,3},{3,2},{4,5},{5,4},{6,7},{7,6},{8,9},{9,8},{10,11... | collective-permute-start | bytes 786440 | tf_op jit(solution)/shard_map/ppermute | solution.py:410
  85.1 4.5 %weight_grads.3 = (bf16[2048,3840]{1,0:T(8,128)(2,1)}, bf16[2048,3840]{1,0:T(8,128)(2,1)}, f32[8,128]{1,0:T(8,128)S(1)}) custom-call(bf16[2,128,2560]{2,1,0:T(8,128)(2,1)S(1)} %get-tuple-element.38.refs_1_.refs_0_, bf16[2,128,2560]{2,1,0:T(8,128)(2,1)S(1)} %collective-permute-done.17.refs_2_.refs_1_, bf16[256,2048]{1,0:T(8,128)(2,1)S(1)} %assemble.1.refs_2_), custom_call_target="tpu_custom_call" | custom-call | tf_op jit(solution)/shard_map/weight_grads/pallas_call | solution.py:46
  89.5 2.0 %collective-permute-done.21.refs_1_ = bf16[64,2048]{1,0:T(8,128)(2,1)S(1)} collective-permute-done((bf16[64,2048]{1,0:T(8,128)(2,1)S(1)}, bf16[64,2048]{1,0:T(8,128)(2,1)S(1)}, u32[]{:S(2)}, u32[]{:S(2)}) %collective-permute-start.21) | collective-permute-done | bytes 262176 | tf_op jit(solution)/shard_map/ppermute | solution.py:410
  92.3 1.8 %collective-permute-start.22 = (bf16[32,2048]{1,0:T(8,128)(2,1)S(1)}, bf16[32,2048]{1,0:T(8,128)(2,1)S(1)}, u32[]{:S(2)}, u32[]{:S(2)}) collective-permute-start(bf16[32,2048]{1,0:T(8,128)(2,1)S(1)} %get-tuple-element.48), channel_id=1, source_target_pairs={{0,6},{1,7},{2,4},{3,5},{4,2},{5,3},{6,0},{7,1},{8,14},{9,15},{10,... | collective-permute-start | bytes 393224 | tf_op jit(solution)/shard_map/ppermute | solution.py:410
  94.6 4.6 %weight_grads.4 = (bf16[2048,3840]{1,0:T(8,128)(2,1)}, bf16[2048,3840]{1,0:T(8,128)(2,1)}, f32[8,128]{1,0:T(8,128)S(1)}) custom-call(bf16[2,128,2560]{2,1,0:T(8,128)(2,1)S(1)} %get-tuple-element.38.refs_1_.refs_0_, bf16[2,128,2560]{2,1,0:T(8,128)(2,1)S(1)} %collective-permute-done.17.refs_2_.refs_1_, ...), custom_call_target="tpu_custom_call", output_to_operand_aliasing={{0}: (3, {}), {1}: (4, {})} | custom-call | tf_op jit(solution)/shard_map/weight_grads/pallas_call | solution.py:46
  100.2 4.8 %collective-permute-start.24 = (bf16[32,2048]{1,0:T(8,128)(2,1)S(1)}, bf16[32,2048]{1,0:T(8,128)(2,1)S(1)}, u32[]{:S(2)}, u32[]{:S(2)}) collective-permute-start(bf16[32,2048]{1,0:T(8,128)(2,1)S(1)} %get-tuple-element.50.refs_5_), channel_id=1, source_target_pairs={{0,2},{1,3},{2,0},{3,1},{4,6},{5,7},{6,4},{7,5},{8,10},{9,11},{10,... | collective-permute-start | bytes 393224 | tf_op jit(solution)/shard_map/ppermute | solution.py:410
  105.0 5.0 %weight_grads.5 = (bf16[2048,3840]{1,0:T(8,128)(2,1)}, bf16[2048,3840]{1,0:T(8,128)(2,1)}, f32[8,128]{1,0:T(8,128)}) custom-call(bf16[2,128,1280]{2,1,0:T(8,128)(2,1)S(1)} %hidden_grads.3.refs_1_.refs_0_, bf16[2,128,1280]{2,1,0:T(8,128)(2,1)S(1)} %collective-permute-done.19.refs_2_.refs_1_, ...), custom_call_target="tpu_custom_call", output_to_operand_aliasing={{0}: (3, {}), {1}: (4, {})} | custom-call | tf_op jit(solution)/shard_map/weight_grads/pallas_call | solution.py:46
  (55 shorter events, 19.6 us)
Async XLA Ops:
  0.6 19.3 %collective-permute-start.7 = (bf16[64,3840]{1,0:T(8,128)(2,1)}, bf16[64,3840]{1,0:T(8,128)(2,1)S(1)}, u32[]{:S(2)}, u32[]{:S(2)}) collective-permute-start(bf16[64,3840]{1,0:T(8,128)(2,1)} %refs_2_.5), channel_id=1, source_target_pairs={{16,0},{24,8},{0,16},{8,24},{17,1},{25,9},{1,17},{9,25},{18,2},{26... | collective-permute-start | bytes 1474568 | tf_op jit(solution)/shard_map/ppermute | solution.py:407
  3.6 22.0 %collective-permute-start.8 = (bf16[64,3840]{1,0:T(8,128)(2,1)}, bf16[64,3840]{1,0:T(8,128)(2,1)S(1)}, u32[]{:S(2)}, u32[]{:S(2)}) collective-permute-start(bf16[64,3840]{1,0:T(8,128)(2,1)} %refs_4_.6), channel_id=1, source_target_pairs={{16,0},{24,8},{0,16},{8,24},{17,1},{25,9},{1,17},{9,25},{18,2},{26... | collective-permute-start | bytes 1474568 | tf_op jit(solution)/shard_map/ppermute | solution.py:407
  3.7 9.0 %collective-permute-start.3 = (bf16[32,2048]{1,0:T(8,128)(2,1)}, bf16[32,2048]{1,0:T(8,128)(2,1)S(1)}, u32[]{:S(2)}, u32[]{:S(2)}) collective-permute-start(bf16[32,2048]{1,0:T(8,128)(2,1)} %refs_1_.1), channel_id=1, source_target_pairs={{0,4},{1,5},{2,6},{3,7},{4,0},{5,1},{6,2},{7,3},{8,12},{9,13},{10,... | collective-permute-start | bytes 393224 | tf_op jit(solution)/shard_map/ppermute | solution.py:410
  6.8 8.0 %collective-permute-start = (bf16[32,2048]{1,0:T(8,128)(2,1)}, bf16[32,2048]{1,0:T(8,128)(2,1)S(1)}, u32[]{:S(2)}, u32[]{:S(2)}) collective-permute-start(bf16[32,2048]{1,0:T(8,128)(2,1)} %refs_1_.1), channel_id=1, source_target_pairs={{0,1},{1,0},{2,3},{3,2},{4,5},{5,4},{6,7},{7,6},{8,9},{9,8},{10,11... | collective-permute-start | bytes 393224 | tf_op jit(solution)/shard_map/ppermute | solution.py:410
  12.7 6.0 %collective-permute-start.5 = (bf16[32,2048]{1,0:T(8,128)(2,1)S(1)}, bf16[32,2048]{1,0:T(8,128)(2,1)S(1)}, u32[]{:S(2)}, u32[]{:S(2)}) collective-permute-start(bf16[32,2048]{1,0:T(8,128)(2,1)S(1)} %collective-permute-done.3.refs_5_), channel_id=1, source_target_pairs={{0,2},{1,3},{2,0},{3,1},{4,6},{5,7},{6,4},{7,5},{8,10},{9,11},{10,... | collective-permute-start | bytes 393224 | tf_op jit(solution)/shard_map/ppermute | solution.py:410
  13.6 14.6 %collective-permute-start.1 = (bf16[32,2048]{1,0:T(8,128)(2,1)}, bf16[32,2048]{1,0:T(8,128)(2,1)S(1)}, u32[]{:S(2)}, u32[]{:S(2)}) collective-permute-start(bf16[32,2048]{1,0:T(8,128)(2,1)} %refs_1_.1), channel_id=1, source_target_pairs={{0,2},{1,3},{2,0},{3,1},{4,6},{5,7},{6,4},{7,5},{8,10},{9,11},{10,... | collective-permute-start | bytes 393224 | tf_op jit(solution)/shard_map/ppermute | solution.py:410
  14.8 13.4 %collective-permute-start.4 = (bf16[32,2048]{1,0:T(8,128)(2,1)S(1)}, bf16[32,2048]{1,0:T(8,128)(2,1)S(1)}, u32[]{:S(2)}, u32[]{:S(2)}) collective-permute-start(bf16[32,2048]{1,0:T(8,128)(2,1)S(1)} %collective-permute-done.3.refs_5_), channel_id=1, source_target_pairs={{0,1},{1,0},{2,3},{3,2},{4,5},{5,4},{6,7},{7,6},{8,9},{9,8},{10,11... | collective-permute-start | bytes 393224 | tf_op jit(solution)/shard_map/ppermute | solution.py:410
  18.8 9.4 %collective-permute-start.2 = (bf16[32,2048]{1,0:T(8,128)(2,1)S(1)}, bf16[32,2048]{1,0:T(8,128)(2,1)S(1)}, u32[]{:S(2)}, u32[]{:S(2)}) collective-permute-start(bf16[32,2048]{1,0:T(8,128)(2,1)S(1)} %collective-permute-done.refs_2_), channel_id=1, source_target_pairs={{0,2},{1,3},{2,0},{3,1},{4,6},{5,7},{6,4},{7,5},{8,10},{9,11},{10,... | collective-permute-start | bytes 393224 | tf_op jit(solution)/shard_map/ppermute | solution.py:410
  19.9 8.2 %collective-permute-start.6 = (bf16[32,2048]{1,0:T(8,128)(2,1)S(1)}, bf16[32,2048]{1,0:T(8,128)(2,1)S(1)}, u32[]{:S(2)}, u32[]{:S(2)}) collective-permute-start(bf16[32,2048]{1,0:T(8,128)(2,1)S(1)} %collective-permute-done.5.refs_4_.refs_7_), channel_id=1, source_target_pairs={{0,1},{1,0},{2,3},{3,2},{4,5},{5,4},{6,7},{7,6},{8,9},{9,8},{10,11... | collective-permute-start | bytes 393224 | tf_op jit(solution)/shard_map/ppermute | solution.py:410
  35.8 5.9 %collective-permute-start.12 = (bf16[32,2048]{1,0:T(8,128)(2,1)S(1)}, bf16[32,2048]{1,0:T(8,128)(2,1)S(1)}, u32[]{:S(2)}, u32[]{:S(2)}) collective-permute-start(bf16[32,2048]{1,0:T(8,128)(2,1)S(1)} %copy-done.4), channel_id=1, source_target_pairs={{0,1},{1,0},{2,3},{3,2},{4,5},{5,4},{6,7},{7,6},{8,9},{9,8},{10,11... | collective-permute-start | bytes 393224 | tf_op jit(solution)/shard_map/ppermute | solution.py:410
  37.6 8.6 %collective-permute-start.11 = (bf16[128,3840]{1,0:T(8,128)(2,1)S(1)}, bf16[128,3840]{1,0:T(8,128)(2,1)S(1)}, u32[]{:S(2)}, u32[]{:S(2)}) collective-permute-start(bf16[128,3840]{1,0:T(8,128)(2,1)S(1)} %activations.1.refs_10_.refs_0_), channel_id=1, source_target_pairs={{0,8},{8,0},{16,24},{24,16},{1,9},{9,1},{17,25},{25,17},{2,10},{10... | collective-permute-start | bytes 2949128 | tf_op jit(solution)/shard_map/ppermute | solution.py:404
  38.0 18.6 %collective-permute-start.10 = (bf16[128,2560]{1,0:T(8,128)(2,1)S(1)}, bf16[128,2560]{1,0:T(8,128)(2,1)S(1)}, u32[]{:S(2)}, u32[]{:S(2)}) collective-permute-start(bf16[128,2560]{1,0:T(8,128)(2,1)S(1)} %add_convert_fusion.refs_4_.refs_0_), channel_id=1, source_target_pairs={{16,0},{24,8},{0,16},{8,24},{17,1},{25,9},{1,17},{9,25},{18,2},{26... | collective-permute-start | bytes 1966088 | tf_op jit(solution)/shard_map/ppermute | solution.py:407
  41.7 14.7 %collective-permute-start.14 = (bf16[64,2048]{1,0:T(8,128)(2,1)S(1)}, bf16[64,2048]{1,0:T(8,128)(2,1)S(1)}, u32[]{:S(2)}, u32[]{:S(2)}) collective-permute-start(bf16[64,2048]{1,0:T(8,128)(2,1)S(1)} %constant_dynamic-update-slice_fusion.refs_5_.refs_9_.refs_7_.refs_1_), channel_id=1, source_target_pairs={{0,4},{1,5},{2,6},{3,7},{4,0},{5,1},{6,2},{7,3},{8,12},{9,13},{10,... | collective-permute-start | bytes 786440 | tf_op jit(solution)/shard_map/ppermute | solution.py:410
  44.6 12.0 %collective-permute-start.13 = (bf16[64,2048]{1,0:T(8,128)(2,1)S(1)}, bf16[64,2048]{1,0:T(8,128)(2,1)S(1)}, u32[]{:S(2)}, u32[]{:S(2)}) collective-permute-start(bf16[64,2048]{1,0:T(8,128)(2,1)S(1)} %constant_dynamic-update-slice_fusion.refs_5_.refs_9_.refs_7_.refs_1_), channel_id=1, source_target_pairs={{0,2},{1,3},{2,0},{3,1},{4,6},{5,7},{6,4},{7,5},{8,10},{9,11},{10,... | collective-permute-start | bytes 786440 | tf_op jit(solution)/shard_map/ppermute | solution.py:410
  57.6 6.7 %collective-permute-start.17 = (bf16[2,128,2560]{2,1,0:T(8,128)(2,1)S(1)}, bf16[2,128,2560]{2,1,0:T(8,128)(2,1)S(1)}, u32[]{:S(2)}, u32[]{:S(2)}) collective-permute-start(bf16[2,128,2560]{2,1,0:T(8,128)(2,1)S(1)} %get-tuple-element.38.refs_1_.refs_0_), channel_id=1, source_target_pairs={{0,8},{8,0},{16,24},{24,16},{1,9},{9,1},{17,25},{25,17},{2,10},{10... | collective-permute-start | bytes 3932168 | tf_op jit(solution)/shard_map/ppermute | solution.py:404
  57.7 3.5 %collective-permute-start.15 = (bf16[128,1280]{1,0:T(8,128)(2,1)S(1)}, bf16[128,1280]{1,0:T(8,128)(2,1)S(1)}, u32[]{:S(2)}, u32[]{:S(2)}) collective-permute-start(bf16[128,1280]{1,0:T(8,128)(2,1)S(1)} %get-tuple-element.37), channel_id=1, source_target_pairs={{0,8},{8,0},{16,24},{24,16},{1,9},{9,1},{17,25},{25,17},{2,10},{10... | collective-permute-start | bytes 983048 | tf_op jit(solution)/shard_map/ppermute | solution.py:404
  61.2 12.5 %collective-permute-start.16 = (bf16[128,1280]{1,0:T(8,128)(2,1)S(1)}, bf16[128,1280]{1,0:T(8,128)(2,1)S(1)}, u32[]{:S(2)}, u32[]{:S(2)}) collective-permute-start(bf16[128,1280]{1,0:T(8,128)(2,1)S(1)} %add_convert_fusion.1.refs_5_.refs_0_), channel_id=1, source_target_pairs={{16,0},{24,8},{0,16},{8,24},{17,1},{25,9},{1,17},{9,25},{18,2},{26... | collective-permute-start | bytes 983048 | tf_op jit(solution)/shard_map/ppermute | solution.py:407
  62.8 10.9 %collective-permute-start.18 = (bf16[64,2048]{1,0:T(8,128)(2,1)S(1)}, bf16[64,2048]{1,0:T(8,128)(2,1)S(1)}, u32[]{:S(2)}, u32[]{:S(2)}) collective-permute-start(bf16[64,2048]{1,0:T(8,128)(2,1)S(1)} %collective-permute-done.14.refs_11_.refs_9_.refs_3_), channel_id=1, source_target_pairs={{0,2},{1,3},{2,0},{3,1},{4,6},{5,7},{6,4},{7,5},{8,10},{9,11},{10,... | collective-permute-start | bytes 786440 | tf_op jit(solution)/shard_map/ppermute | solution.py:410
  74.2 2.2 %collective-permute-start.19 = (bf16[2,128,1280]{2,1,0:T(8,128)(2,1)S(1)}, bf16[2,128,1280]{2,1,0:T(8,128)(2,1)S(1)}, u32[]{:S(2)}, u32[]{:S(2)}) collective-permute-start(bf16[2,128,1280]{2,1,0:T(8,128)(2,1)S(1)} %hidden_grads.3.refs_1_.refs_0_), channel_id=1, source_target_pairs={{0,8},{8,0},{16,24},{24,16},{1,9},{9,1},{17,25},{25,17},{2,10},{10... | collective-permute-start | bytes 1966088 | tf_op jit(solution)/shard_map/ppermute | solution.py:404
  82.3 9.2 %collective-permute-start.21 = (bf16[64,2048]{1,0:T(8,128)(2,1)S(1)}, bf16[64,2048]{1,0:T(8,128)(2,1)S(1)}, u32[]{:S(2)}, u32[]{:S(2)}) collective-permute-start(bf16[64,2048]{1,0:T(8,128)(2,1)S(1)} %get-tuple-element.41.refs_5_), channel_id=1, source_target_pairs={{0,1},{1,0},{2,3},{3,2},{4,5},{5,4},{6,7},{7,6},{8,9},{9,8},{10,11... | collective-permute-start | bytes 786440 | tf_op jit(solution)/shard_map/ppermute | solution.py:410
  83.9 15.3 %collective-permute-start.20 = (bf16[64,2048]{1,0:T(8,128)(2,1)S(1)}, bf16[64,2048]{1,0:T(8,128)(2,1)S(1)}, u32[]{:S(2)}, u32[]{:S(2)}) collective-permute-start(bf16[64,2048]{1,0:T(8,128)(2,1)S(1)} %get-tuple-element.40), channel_id=1, source_target_pairs={{0,1},{1,0},{2,3},{3,2},{4,5},{5,4},{6,7},{7,6},{8,9},{9,8},{10,11... | collective-permute-start | bytes 786440 | tf_op jit(solution)/shard_map/ppermute | solution.py:410
  92.3 7.2 %collective-permute-start.22 = (bf16[32,2048]{1,0:T(8,128)(2,1)S(1)}, bf16[32,2048]{1,0:T(8,128)(2,1)S(1)}, u32[]{:S(2)}, u32[]{:S(2)}) collective-permute-start(bf16[32,2048]{1,0:T(8,128)(2,1)S(1)} %get-tuple-element.48), channel_id=1, source_target_pairs={{0,6},{1,7},{2,4},{3,5},{4,2},{5,3},{6,0},{7,1},{8,14},{9,15},{10,... | collective-permute-start | bytes 393224 | tf_op jit(solution)/shard_map/ppermute | solution.py:410
  94.1 16.0 %collective-permute-start.23 = (bf16[32,2048]{1,0:T(8,128)(2,1)S(1)}, bf16[32,2048]{1,0:T(8,128)(2,1)S(1)}, u32[]{:S(2)}, u32[]{:S(2)}) collective-permute-start(bf16[32,2048]{1,0:T(8,128)(2,1)S(1)} %get-tuple-element.46.refs_5_), channel_id=1, source_target_pairs={{0,4},{1,5},{2,6},{3,7},{4,0},{5,1},{6,2},{7,3},{8,12},{9,13},{10,... | collective-permute-start | bytes 393224 | tf_op jit(solution)/shard_map/ppermute | solution.py:410
  100.2 9.9 %collective-permute-start.24 = (bf16[32,2048]{1,0:T(8,128)(2,1)S(1)}, bf16[32,2048]{1,0:T(8,128)(2,1)S(1)}, u32[]{:S(2)}, u32[]{:S(2)}) collective-permute-start(bf16[32,2048]{1,0:T(8,128)(2,1)S(1)} %get-tuple-element.50.refs_5_), channel_id=1, source_target_pairs={{0,2},{1,3},{2,0},{3,1},{4,6},{5,7},{6,4},{7,5},{8,10},{9,11},{10,... | collective-permute-start | bytes 393224 | tf_op jit(solution)/shard_map/ppermute | solution.py:410
  (6 other events, 96.5 us)

commit v3 on v2

--- a/solution.py
+++ b/solution.py
@@ -82,58 +82,85 @@
     )
 
 
-def copies_of(weight, lo, units, piece, ready, sems):
-    copies = []
-    for i in range(units // piece):
-        at = pl.ds(i * piece, piece)
-        copies.append(
-            pltpu.make_async_copy(weight.at[pl.ds(lo + i * piece, piece)], ready.at[at], sems.at[i])
-        )
-        copies[-1].start()
-    return copies
-
-
-def dots_of(a, copies, piece, ready, keep, send):
+def fetch(weight, span, others, deps=()):
+    lo, units = span
+    arrays = [weight, *others]
+    shapes = [(units, weight.shape[1]), *(o.shape for o in others)]
+
+    def kernel(*refs):
+        given, outs, sems = refs[: len(arrays)], refs[len(arrays) : -1], refs[-1]
+        copies = []
+        for i, (source, out) in enumerate(zip(given, outs)):
+            if i == 0:
+                source = source.at[pl.ds(lo, units)]
+            copies.append(pltpu.make_async_copy(source, out, sems.at[i]))
+            copies[-1].start()
+        for copy in copies:
+            copy.wait()
+
+    return call(
+        kernel,
+        arrays,
+        [REMAIN] * len(arrays),
+        [pltpu.VMEM(shape, BF16) for shape in shapes],
+        [WHOLE] * len(arrays),
+        deps,
+        scratch=[pltpu.SemaphoreType.DMA((len(arrays),))],
+        name="fetch",
+    )
+
+
+def run_copy(weight, lo, i, piece, ready, sems):
+    at = pl.ds(pl.multiple_of(i * piece, piece), piece)
+    return pltpu.make_async_copy(
+        weight.at[pl.ds(pl.multiple_of(lo + i * piece, piece), piece)], ready.at[at], sems.at[i]
+    )
+
+
+def start_copies(weight, lo, count, piece, ready, sems):
+    for i in range(count):
+        run_copy(weight, lo, i, piece, ready, sems).start()
+
+
+def dots_of(a, weight, lo, count, piece, ready, sems, keep, send):
     half = keep.shape[0]
-    for i, copy in enumerate(copies):
-        copy.wait()
-        at = slice(i * piece, (i + 1) * piece)
+
+    def step(i, carry):
+        run_copy(weight, lo, i, piece, ready, sems).wait()
+        at = pl.ds(pl.multiple_of(i * piece, piece), piece)
         part = lax.dot_general(a[...], ready[at, :], NT, preferred_element_type=F32).astype(BF16)
         keep[:, at] = part[:half]
         send[:, at] = part[half:]
-
-
-def first_partial(blocks, offsets, down, span, deps=()):
+        return carry
+
+    lax.fori_loop(0, count, step, 0)
+
+
+def first_partial(blocks, offsets, rows, deps=()):
     count, width = len(blocks), blocks[0].shape[1]
     tokens = sum(block.shape[0] for block in blocks)
     run = tokens // offsets.shape[0]
-    lo, units = span
-    piece = divisor(units, 640)
-    pieces = units // piece
+    half, units = tokens // CORES, rows.shape[0]
+    piece = divisor(units, 640, 256)
 
     def kernel(offs, *refs):
-        own, others, weight = refs[0], refs[1:count], refs[count]
-        keep, send, a, ready, sems = refs[count + 1 :]
-        moves = []
-        if count > 1:
-            at = pl.ds(pl.multiple_of(offs[0], run), run)
-            moves.append(pltpu.make_async_copy(own, a.at[at], sems.at[pieces]))
-            moves[0].start()
-        copies = copies_of(weight, lo, units, piece, ready, sems)
-        lay(others if count > 1 else [own], offs, a, run, 1 if count > 1 else 0)
-        for move in moves:
-            move.wait()
-        dots_of(a, copies, piece, ready, keep, send)
-
-    part = jax.ShapeDtypeStruct((tokens // CORES, units), BF16)
-    return call(
-        kernel,
-        [offsets, *blocks, down],
-        [SCALARS, REMAIN if count > 1 else WHOLE] + [WHOLE] * (count - 1) + [REMAIN],
+        weight, keep, send, a = refs[count:]
+        lay(refs[:count], offs, a, run)
+        for lo in range(0, units, piece):
+            at = slice(lo, lo + piece)
+            part = lax.dot_general(a[...], weight[at, :], NT, preferred_element_type=F32)
+            part = part.astype(BF16)
+            keep[:, at] = part[:half]
+            send[:, at] = part[half:]
+
+    part = jax.ShapeDtypeStruct((half, units), BF16)
+    return call(
+        kernel,
+        [offsets, *blocks, rows],
+        [SCALARS] + [WHOLE] * count + [RESIDENT],
         (part, part, jax.ShapeDtypeStruct((tokens, width), BF16)),
         [WHOLE] * 3,
         deps,
-        scratch=[pltpu.VMEM((units, width), BF16), pltpu.SemaphoreType.DMA((pieces + 1,))],
         name="first_partial",
     )
 
@@ -201,9 +228,9 @@
 def down_grad(hidden, hidden_other, out_all, down=None, span=(0, 0), deps=()):
     half, units = hidden.shape
     tokens, width = out_all.shape
-    piece = divisor(units, 256)
+    piece = divisor(units, 640)
     count = units // piece
-    slots = min(8, count)
+    slots = min(3, count)
     lo, taken = span
     operands, specs = [hidden, hidden_other, out_all], [WHOLE] * 3
     shapes = [jax.ShapeDtypeStruct((units, width), BF16), jax.ShapeDtypeStruct((8, 128), F32)]
@@ -212,7 +239,7 @@
         operands.append(down)
         specs.append(REMAIN)
         shapes += [jax.ShapeDtypeStruct((half, taken), BF16)] * 2
-        run = divisor(taken, 640)
+        run = divisor(taken, 1280)
         scratch += [pltpu.VMEM((taken, width), BF16), pltpu.SemaphoreType.DMA((taken // run,))]
 
     def kernel(*refs):
@@ -222,22 +249,32 @@
         ready, sems = refs[given + len(shapes) : given + len(shapes) + 2]
         token[...] = jnp.zeros(token.shape, F32)
         if taken:
-            copies = copies_of(refs[3], lo, taken, run, refs[-2], refs[-1])
-        stores = []
-        for i in range(count):
-            at, slot = slice(i * piece, (i + 1) * piece), i % slots
-            if i >= slots:
-                stores[i - slots].wait()
-            ready[slot] = lax.dot_general(
+            start_copies(refs[3], lo, taken // run, run, refs[-2], refs[-1])
+
+        def store(i):
+            slot = lax.rem(i, slots)
+            at = pl.ds(pl.multiple_of(i * piece, piece), piece)
+            return pltpu.make_async_copy(ready.at[slot], out.at[at], sems.at[slot])
+
+        def step(i, carry):
+            @pl.when(i >= slots)
+            def _():
+                store(i - slots).wait()
+
+            at = pl.ds(pl.multiple_of(i * piece, piece), piece)
+            ready[lax.rem(i, slots)] = lax.dot_general(
                 both(a, b, slice(None), at), g[...], TN, preferred_element_type=F32
             ).astype(BF16)
-            store = pltpu.make_async_copy(ready.at[slot], out.at[at], sems.at[slot])
-            store.start()
-            stores.append(store)
+            store(i).start()
+            return carry
+
+        lax.fori_loop(0, count, step, 0)
         if taken:
-            dots_of(g, copies, run, refs[-2], refs[given + 2], refs[given + 3])
-        for store in stores[count - slots :]:
-            store.wait()
+            dots_of(
+                g, refs[3], lo, taken // run, run, refs[-2], refs[-1], refs[given + 2], refs[given + 3]
+            )
+        for i in range(count - slots, count):
+            store(i).wait()
 
     return call(
         kernel,
@@ -316,27 +353,31 @@
     )
 
 
-def fold(own, other, deps=()):
-    rows, width = own.shape[0] // 2, own.shape[1]
-
-    def kernel(a, b, *outs):
-        for i, out in enumerate(outs[:2]):
-            at = slice(i * rows, (i + 1) * rows)
-            total = a[at, :].astype(F32) + b[at, :].astype(F32)
-            out[...] = total.astype(BF16)
-        outs[2][...] = total
-
-    shape = (rows, width)
-    return call(
-        kernel,
-        [own, other],
-        [WHOLE] * 2,
-        (
-            jax.ShapeDtypeStruct(shape, BF16),
-            jax.ShapeDtypeStruct(shape, BF16),
-            jax.ShapeDtypeStruct(shape, F32),
-        ),
-        [WHOLE] * 3,
+def fold(terms, wide, deps=()):
+    arrays, refs_of = [], []
+    for term in terms:
+        refs_of.append([])
+        for array, row in term:
+            known = [i for i, a in enumerate(arrays) if a is array]
+            if not known:
+                arrays.append(array)
+            refs_of[-1].append((known[0] if known else len(arrays) - 1, row))
+    rows, width = min(a.shape[0] for a in arrays), arrays[0].shape[1]
+    kinds = [F32 if w else BF16 for w in wide]
+
+    def kernel(*refs):
+        for out, pairs in zip(refs[len(arrays) :], refs_of):
+            total = 0.0
+            for i, row in pairs:
+                total = total + refs[i][row * rows : (row + 1) * rows, :].astype(F32)
+            out[...] = total.astype(out.dtype)
+
+    return call(
+        kernel,
+        arrays,
+        [WHOLE] * len(arrays),
+        [jax.ShapeDtypeStruct((rows, width), kind) for kind in kinds],
+        [WHOLE] * len(terms),
         deps,
         name="fold",
     )
@@ -396,7 +437,7 @@
     own_tokens = gate.shape[0]
     col_tokens = grad_out.shape[0]
     units = down_weight.shape[0]
-    first = units // 3 * 2 if units % 384 == 0 else units
+    first = units // 5 * 3 if units % 640 == 0 else units
     spans = [(0, first)] + ([(first, units - first)] if first < units else [])
     direct = nc == 8 and nr * own_tokens == nc * col_tokens and own_tokens % col_tokens == 0
 
@@ -441,15 +482,23 @@
         total = (keep.astype(F32) + swap_core(send).astype(F32)).astype(BF16)
         return [total] + [from_x(total, o) for o in range(1, nx)]
 
-    out_blocks = gather(grad_out)
-    hidden = activations(gates, ups, deps=out_blocks[-2:-1])
+    blocks = gather(grad_out)
+    late = blocks[6:7]
+    if direct:
+        rows_here, blocks[0], gates[0], ups[0] = fetch(
+            down_weight, spans[0], [grad_out, gate, up], deps=late
+        )
+    else:
+        rows_here, gates[0], ups[0] = fetch(down_weight, spans[0], [gate, up])
+    beside = [swap_col(inputs, 1)] if direct else []
     keep, send, out_all = first_partial(
-        out_blocks, offsets, down_weight, spans[0], deps=[hidden]
-    )
+        blocks, offsets, rows_here, deps=[*gates[1:], *ups[1:], *beside]
+    )
+    hidden = activations(gates, ups, deps=[keep])
     hidden_other = swap_core(hidden)
     sums = [exchanged(keep, send)]
     if direct:
-        own = jnp.concatenate([inputs, swap_col(inputs, 1)], axis=0)
+        own = jnp.concatenate([inputs, *beside], axis=0)
         in_blocks = [own, swap_col(own, 2), swap_col(own, 4)]
     else:
         own = sums[0][0]
@@ -461,7 +510,7 @@
 
     mine, *parts = hidden_grads(sums[0], gates, ups, spans[0], parts, [token, *in_blocks])
     grads = [(mine, swap_core(mine))]
-    groups = [(7, 5), (3, 1), (6, 4), (2, 0)] if direct else [range(nr)]
+    groups = [(7, 5), (3,), (6, 4, 1), (2,), (0,)] if direct else [range(nr)]
     if direct:
         in_blocks.append(swap_col(in_blocks[2], 2))
     total = None
@@ -472,10 +521,10 @@
         )
         (mine,) = hidden_grads(sums[1], gates, ups, spans[1], deps=[total, *in_blocks])
         grads.append((mine, swap_core(mine)))
+    in_all = assemble(in_blocks, offsets if direct else in_order, deps=[mine])
     blocks = input_grads(
-        *grads[-1], gate_weight, up_weight, total, offsets, spans[-1], rows, groups
-    )
-    in_all = assemble(in_blocks, offsets if direct else in_order, deps=blocks[:1])
+        *grads[-1], gate_weight, up_weight, total, offsets, spans[-1], rows, groups, [in_all]
+    )
 
     def weight_part(before, i, span, deps):
         *weights, token = weight_grads(
@@ -485,23 +534,27 @@
 
     cut = divisor(first, first // 2)
     weights, token = weight_part(None, 0, (0, cut), [])
-    if direct:
-        far, near = swap_col(blocks[0], 1), swap_col(blocks[1], 1)
-        sent6, sent4, _ = fold(blocks[2], far, deps=[token])
-        part6, part4 = swap_col(sent6, 6), swap_col(sent4, 4)
-        ready = sent4
-    else:
-        ready = blocks[0]
+    ready = blocks[0]
+    if direct:
+        far, third, kept, second, result = blocks
+        far, third = swap_col(far, 1), swap_col(third, 2)
+        sent6, sum4, sent1 = fold(
+            [[(kept, 0), (far, 0)], [(kept, 1), (far, 1)], [(kept, 2), (third, 0)]],
+            [False, True, False],
+            deps=[token],
+        )
+        part6, part1 = swap_col(sent6, 2), swap_col(sent1, 1)
+        ready = sent1
     if cut < first:
         weights, token = weight_part(weights, 0, (cut, first - cut), [ready])
     if direct:
-        sent2, _, result = fold(blocks[3], near, deps=[token, part6])
-        part2 = swap_col(sent2, 2)
-        ready = sent2
+        (sent4,) = fold([[(sum4, 0), (part6, 0)]], [False], deps=[token, part1])
+        ready = sent4
     if len(spans) > 1:
         weights, token = weight_part(weights, 1, spans[1], [ready])
     if direct:
-        for part in (part6, part4, part2):
+        result = result.astype(F32) + part1.astype(F32)
+        for part in (swap_col(second, 2), swap_col(sent4, 4)):
             result = result + part.astype(F32)
         grad_inputs = result.astype(BF16)
     else:

time: 111 us -> 96.5 us (0.87)
  waiting for transfers between devices: 21.4 us -> 15.1 us
  Pallas kernels: 50.3 us -> 47 us
  starting transfers between devices: 35.2 us -> 32.4 us
  local copies, waits for them, and re-layouts: 2.18 us -> 0.11 us
    pallas_call x13 -> x14, Pallas kernels: 50.3 us -> 47 us  [call(): pl.pallas_call(body, out_shape=out_shape, in_specs=list(in_specs) + [ANYW...]
    ppermute x4, waiting for transfers between devices: 4.07 us -> 1.02 us  [from_x(): lax.ppermute(value, 'row', [((r + offset * CORES) % nr, r) for r in range...]
    ppermute x16 -> x17, starting transfers between devices: 27.8 us -> 25.7 us  [swap_col(): return lax.ppermute(value, 'col', [(c, c ^ mask) for c in range(nc)])]
    unnamed x11 -> x3, local copies, waits for them, and re-layouts: 2.09 us -> 0.01 us
    ppermute x16 -> x17, waiting for transfers between devices: 12.1 us -> 10.2 us  [swap_col(): return lax.ppermute(value, 'col', [(c, c ^ mask) for c in range(nc)])]
    ppermute x5, waiting for transfers between devices: 5.17 us -> 3.87 us  [swap_core(): return lax.ppermute(value, 'row', [(r, r ^ 1) for r in range(nr)])]
  transfers between devices with their start and end apart: 25 -> 26, of which waited for: 11 -> 10; matrix products, arithmetic and copies ran while one was open for 0% -> 0% of each run, Pallas kernels for 32% -> 37%
where the time goes in v3:
time: 96.5 us; the launch traced here: 96.4 us
  Pallas kernels  47 us (49%)
  starting transfers between devices  32.4 us (34%)
  waiting for transfers between devices  15.1 us (16%)
    pallas_call x14, Pallas kernels, call(): pl.pallas_call(body, out_shape=out_shape, in_specs=list(in_specs) + [ANYW...  47 us
    ppermute x17, starting transfers between devices, swap_col(): return lax.ppermute(value, 'col', [(c, c ^ mask) for c in range(nc)])  25.7 us
    ppermute x17, waiting for transfers between devices, swap_col(): return lax.ppermute(value, 'col', [(c, c ^ mask) for c in range(nc)])  10.2 us
    ppermute x4, starting transfers between devices, from_x(): lax.ppermute(value, 'row', [((r + offset * CORES) % nr, r) for r in range...  5.44 us
    ppermute x5, waiting for transfers between devices, swap_core(): return lax.ppermute(value, 'row', [(r, r ^ 1) for r in range(nr)])  3.87 us
  transfers between devices with their start and end apart: 26, of which 10 were waited for; matrix products, arithmetic and copies ran while one was open for 0% of the time, Pallas kernels for 37%

profile of v3, /device:TPU:0, one launch (start us, length us, event | category | flops | bytes accessed | tf_op | source)
XLA Modules:
  0.0 96.4 jit_solution(4524474336209074844)
XLA Ops:
  0.6 3.0 %collective-permute-start.7 = (bf16[64,3840]{1,0:T(8,128)(2,1)}, bf16[64,3840]{1,0:T(8,128)(2,1)S(1)}, u32[]{:S(2)}, u32[]{:S(2)}) collective-permute-start(bf16[64,3840]{1,0:T(8,128)(2,1)} %refs_2_.1), channel_id=1, source_target_pairs={{16,0},{24,8},{0,16},{8,24},{17,1},{25,9},{1,17},{9,25},{18,2},{26... | collective-permute-start | bytes 1474568 | tf_op jit(solution)/shard_map/ppermute | solution.py:448
  3.7 2.0 %collective-permute-start.9 = (bf16[32,2048]{1,0:T(8,128)(2,1)}, bf16[32,2048]{1,0:T(8,128)(2,1)S(1)}, u32[]{:S(2)}, u32[]{:S(2)}) collective-permute-start(bf16[32,2048]{1,0:T(8,128)(2,1)} %param.7), channel_id=1, source_target_pairs={{0,1},{1,0},{2,3},{3,2},{4,5},{5,4},{6,7},{7,6},{8,9},{9,8},{10,11... | collective-permute-start | bytes 393224 | tf_op jit(solution)/shard_map/ppermute | solution.py:451
  5.7 2.6 %collective-permute-start = (bf16[32,2048]{1,0:T(8,128)(2,1)}, bf16[32,2048]{1,0:T(8,128)(2,1)S(1)}, u32[]{:S(2)}, u32[]{:S(2)}) collective-permute-start(bf16[32,2048]{1,0:T(8,128)(2,1)} %refs_1_.1), channel_id=1, source_target_pairs={{0,4},{1,5},{2,6},{3,7},{4,0},{5,1},{6,2},{7,3},{8,12},{9,13},{10,... | collective-permute-start | bytes 393224 | tf_op jit(solution)/shard_map/ppermute | solution.py:451
  8.3 1.6 %collective-permute-start.3 = (bf16[32,2048]{1,0:T(8,128)(2,1)}, bf16[32,2048]{1,0:T(8,128)(2,1)S(1)}, u32[]{:S(2)}, u32[]{:S(2)}) collective-permute-start(bf16[32,2048]{1,0:T(8,128)(2,1)} %refs_1_.1), channel_id=1, source_target_pairs={{0,2},{1,3},{2,0},{3,1},{4,6},{5,7},{6,4},{7,5},{8,10},{9,11},{10,... | collective-permute-start | bytes 393224 | tf_op jit(solution)/shard_map/ppermute | solution.py:451
  10.9 3.2 %collective-permute-done.refs_5_ = bf16[32,2048]{1,0:T(8,128)(2,1)S(1)} collective-permute-done((bf16[32,2048]{1,0:T(8,128)(2,1)}, bf16[32,2048]{1,0:T(8,128)(2,1)S(1)}, u32[]{:S(2)}, u32[]{:S(2)}) %collective-permute-start) | collective-permute-done | bytes 131104 | tf_op jit(solution)/shard_map/ppermute | solution.py:451
  16.6 2.8 %collective-permute-done.1.refs_4_.refs_7_ = bf16[32,2048]{1,0:T(8,128)(2,1)S(1)} collective-permute-done((bf16[32,2048]{1,0:T(8,128)(2,1)S(1)}, bf16[32,2048]{1,0:T(8,128)(2,1)S(1)}, u32[]{:S(2)}, u32[]{:S(2)}) %collective-permute-start.1) | collective-permute-done | bytes 131104 | tf_op jit(solution)/shard_map/ppermute | solution.py:451
  19.4 1.5 %collective-permute-start.6 = (bf16[32,2048]{1,0:T(8,128)(2,1)S(1)}, bf16[32,2048]{1,0:T(8,128)(2,1)S(1)}, u32[]{:S(2)}, u32[]{:S(2)}) collective-permute-start(bf16[32,2048]{1,0:T(8,128)(2,1)S(1)} %collective-permute-done.1.refs_4_.refs_7_), channel_id=1, source_target_pairs={{0,1},{1,0},{2,3},{3,2},{4,5},{5,4},{6,7},{7,6},{8,9},{9,8},{10,11... | collective-permute-start | bytes 393224 | tf_op jit(solution)/shard_map/ppermute | solution.py:451
  21.0 4.0 %fetch.1 = (bf16[2304,2048]{1,0:T(8,128)(2,1)S(1)}, bf16[32,2048]{1,0:T(8,128)(2,1)S(1)}, bf16[64,3840]{1,0:T(8,128)(2,1)S(1)}, bf16[64,3840]{1,0:T(8,128)(2,1)S(1)}) custom-call(bf16[3840,2048]{1,0:T(8,128)(2,1)} %refs_3_.5, bf16[32,2048]{1,0:T(8,128)(2,1)} %refs_1_.1, bf16[64,3840]{1,0:T(8,128)(2,1)} %refs_2_.1, bf16[64,3840]{1,0:T(8,128)(2,1)} %refs_3_.4, ...), custom_call_target="tpu_custom_call" | custom-call | tf_op jit(solution)/shard_map/fetch/pallas_call | solution.py:46
  25.6 3.2 %first_partial.1 = (bf16[128,2304]{1,0:T(8,128)(2,1)S(1)}, bf16[128,2304]{1,0:T(8,128)(2,1)S(1)}, bf16[256,2048]{1,0:T(8,128)(2,1)S(1)}) custom-call(s32[8]{0:T(128)S(1)} %stack.35.refs_0_, bf16[32,2048]{1,0:T(8,128)(2,1)S(1)} %get-tuple-element.34.refs_1_, bf16[32,2048]{1,0:T(8,128)(2,1)S(1)} %collective-permute-done.2.refs_2_, ...), custom_call_target="tpu_custom_call" | custom-call | tf_op jit(solution)/shard_map/first_partial/pallas_call | solution.py:46
  31.0 1.8 %collective-permute-start.11 = (bf16[128,2304]{1,0:T(8,128)(2,1)S(1)}, bf16[128,2304]{1,0:T(8,128)(2,1)S(1)}, u32[]{:S(2)}, u32[]{:S(2)}) collective-permute-start(bf16[128,2304]{1,0:T(8,128)(2,1)S(1)} %add_convert_fusion.refs_4_.refs_0_), channel_id=1, source_target_pairs={{16,0},{24,8},{0,16},{8,24},{17,1},{25,9},{1,17},{9,25},{18,2},{26... | collective-permute-start | bytes 1769480 | tf_op jit(solution)/shard_map/ppermute | solution.py:448
  32.9 2.7 %collective-permute-start.14 = (bf16[64,2048]{1,0:T(8,128)(2,1)S(1)}, bf16[64,2048]{1,0:T(8,128)(2,1)S(1)}, u32[]{:S(2)}, u32[]{:S(2)}) collective-permute-start(bf16[64,2048]{1,0:T(8,128)(2,1)S(1)} %constant_dynamic-update-slice_fusion.refs_5_.refs_9_.refs_7_.refs_1_), channel_id=1, source_target_pairs={{0,4},{1,5},{2,6},{3,7},{4,0},{5,1},{6,2},{7,3},{8,12},{9,13},{10,... | collective-permute-start | bytes 786440 | tf_op jit(solution)/shard_map/ppermute | solution.py:451
  35.5 1.6 %collective-permute-start.13 = (bf16[64,2048]{1,0:T(8,128)(2,1)S(1)}, bf16[64,2048]{1,0:T(8,128)(2,1)S(1)}, u32[]{:S(2)}, u32[]{:S(2)}) collective-permute-start(bf16[64,2048]{1,0:T(8,128)(2,1)S(1)} %constant_dynamic-update-slice_fusion.refs_5_.refs_9_.refs_7_.refs_1_), channel_id=1, source_target_pairs={{0,2},{1,3},{2,0},{3,1},{4,6},{5,7},{6,4},{7,5},{8,10},{9,11},{10,... | collective-permute-start | bytes 786440 | tf_op jit(solution)/shard_map/ppermute | solution.py:451
  37.1 7.8 %down_grad.1 = (bf16[3840,2048]{1,0:T(8,128)(2,1)}, f32[8,128]{1,0:T(8,128)S(1)}, bf16[128,1536]{1,0:T(8,128)(2,1)S(1)}, bf16[128,1536]{1,0:T(8,128)(2,1)S(1)}) custom-call(bf16[128,3840]{1,0:T(8,128)(2,1)S(1)} %activations.1.refs_0_, bf16[128,3840]{1,0:T(8,128)(2,1)S(1)} %collective-permute-done.12.refs_1_, ...), custom_call_target="tpu_custom_call" | custom-call | tf_op jit(solution)/shard_map/down_grad/pallas_call | solution.py:46
  44.9 2.7 %collective-permute-done.14.refs_11_.refs_9_.refs_3_ = bf16[64,2048]{1,0:T(8,128)(2,1)S(1)} collective-permute-done((bf16[64,2048]{1,0:T(8,128)(2,1)S(1)}, bf16[64,2048]{1,0:T(8,128)(2,1)S(1)}, u32[]{:S(2)}, u32[]{:S(2)}) %collective-permute-start.14) | collective-permute-done | bytes 262176 | tf_op jit(solution)/shard_map/ppermute | solution.py:451
  52.4 8.7 %input_grads.2.refs_6_.refs_5_ = f32[256,2048]{1,0:T(8,128)S(1)} custom-call(s32[8]{0:T(128)S(1)} %stack.35.refs_0_, bf16[2,128,2304]{2,1,0:T(8,128)(2,1)S(1)} %get-tuple-element.46.refs_1_.refs_0_, bf16[2,128,2304]{2,1,0:T(8,128)(2,1)S(1)} %collective-permute-done.17.refs_2_.refs_1_, bf16[2048,3840]{1,0:T(8,128)(2,1)} %refs_3_.7, ...), custom_call_target="tpu_custom_call" | custom-call | tf_op jit(solution)/shard_map/input_grads/pallas_call | solution.py:46
  62.8 1.6 %collective-permute-done.19.refs_2_.refs_1_ = bf16[2,128,1536]{2,1,0:T(8,128)(2,1)S(1)} collective-permute-done((bf16[2,128,1536]{2,1,0:T(8,128)(2,1)S(1)}, bf16[2,128,1536]{2,1,0:T(8,128)(2,1)S(1)}, u32[]{:S(2)}, u32[]{:S(2)}) %collective-permute-start.19) | collective-permute-done | bytes 786464 | tf_op jit(solution)/shard_map/ppermute | solution.py:445
  64.4 6.7 %input_grads.3 = (bf16[64,2048]{1,0:T(8,128)(2,1)S(1)}, bf16[32,2048]{1,0:T(8,128)(2,1)S(1)}, bf16[96,2048]{1,0:T(8,128)(2,1)S(1)}, bf16[32,2048]{1,0:T(8,128)(2,1)S(1)}, bf16[32,2048]{1,0:T(8,128)(2,1)S(1)}) custom-call(s32[8]{0:T(128)S(1)} %stack.35.refs_0_, bf16[2,128,1536]{2,1,0:T(8,128)(2,1)S(1)} %hidden_grads.3.refs_5_.refs_1_.refs_0_, ...), custom_call_target="tpu_custom_call" | custom-call | tf_op jit(solution)/shard_map/input_grads/pallas_call | solution.py:46
  71.2 1.6 %collective-permute-start.20 = (bf16[64,2048]{1,0:T(8,128)(2,1)S(1)}, bf16[64,2048]{1,0:T(8,128)(2,1)S(1)}, u32[]{:S(2)}, u32[]{:S(2)}) collective-permute-start(bf16[64,2048]{1,0:T(8,128)(2,1)S(1)} %get-tuple-element.49), channel_id=1, source_target_pairs={{0,1},{1,0},{2,3},{3,2},{4,5},{5,4},{6,7},{7,6},{8,9},{9,8},{10,11... | collective-permute-start | bytes 786440 | tf_op jit(solution)/shard_map/ppermute | solution.py:451
  74.2 4.1 %weight_grads.3 = (bf16[2048,3840]{1,0:T(8,128)(2,1)}, bf16[2048,3840]{1,0:T(8,128)(2,1)}, f32[8,128]{1,0:T(8,128)S(1)}) custom-call(bf16[2,128,2304]{2,1,0:T(8,128)(2,1)S(1)} %get-tuple-element.46.refs_1_.refs_0_, bf16[2,128,2304]{2,1,0:T(8,128)(2,1)S(1)} %collective-permute-done.17.refs_2_.refs_1_, bf16[256,2048]{1,0:T(8,128)(2,1)S(1)} %assemble.1.refs_6_.refs_2_), custom_call_target="tpu_custom_call" | custom-call | tf_op jit(solution)/shard_map/weight_grads/pallas_call | solution.py:46
  79.7 1.5 %collective-permute-start.24 = (bf16[32,2048]{1,0:T(8,128)(2,1)S(1)}, bf16[32,2048]{1,0:T(8,128)(2,1)S(1)}, u32[]{:S(2)}, u32[]{:S(2)}) collective-permute-start(bf16[32,2048]{1,0:T(8,128)(2,1)S(1)} %get-tuple-element.55), channel_id=1, source_target_pairs={{0,2},{1,3},{2,0},{3,1},{4,6},{5,7},{6,4},{7,5},{8,10},{9,11},{10,... | collective-permute-start | bytes 393224 | tf_op jit(solution)/shard_map/ppermute | solution.py:451
  81.2 1.5 %collective-permute-start.22 = (bf16[32,2048]{1,0:T(8,128)(2,1)S(1)}, bf16[32,2048]{1,0:T(8,128)(2,1)S(1)}, u32[]{:S(2)}, u32[]{:S(2)}) collective-permute-start(bf16[32,2048]{1,0:T(8,128)(2,1)S(1)} %get-tuple-element.52.refs_5_), channel_id=1, source_target_pairs={{0,1},{1,0},{2,3},{3,2},{4,5},{5,4},{6,7},{7,6},{8,9},{9,8},{10,11... | collective-permute-start | bytes 393224 | tf_op jit(solution)/shard_map/ppermute | solution.py:451
  83.3 4.4 %weight_grads.4 = (bf16[2048,3840]{1,0:T(8,128)(2,1)}, bf16[2048,3840]{1,0:T(8,128)(2,1)}, f32[8,128]{1,0:T(8,128)S(1)}) custom-call(bf16[2,128,2304]{2,1,0:T(8,128)(2,1)S(1)} %get-tuple-element.46.refs_1_.refs_0_, bf16[2,128,2304]{2,1,0:T(8,128)(2,1)S(1)} %collective-permute-done.17.refs_2_.refs_1_, ...), custom_call_target="tpu_custom_call", output_to_operand_aliasing={{0}: (3, {}), {1}: (4, {})} | custom-call | tf_op jit(solution)/shard_map/weight_grads/pallas_call | solution.py:46
  87.7 2.2 %collective-permute-start.25 = (bf16[32,2048]{1,0:T(8,128)(2,1)S(1)}, bf16[32,2048]{1,0:T(8,128)(2,1)S(1)}, u32[]{:S(2)}, u32[]{:S(2)}) collective-permute-start(bf16[32,2048]{1,0:T(8,128)(2,1)S(1)} %fold.3.refs_5_), channel_id=1, source_target_pairs={{0,4},{1,5},{2,6},{3,7},{4,0},{5,1},{6,2},{7,3},{8,12},{9,13},{10,... | collective-permute-start | bytes 393224 | tf_op jit(solution)/shard_map/ppermute | solution.py:451
  90.0 5.7 %weight_grads.5 = (bf16[2048,3840]{1,0:T(8,128)(2,1)}, bf16[2048,3840]{1,0:T(8,128)(2,1)}, f32[8,128]{1,0:T(8,128)}) custom-call(bf16[2,128,1536]{2,1,0:T(8,128)(2,1)S(1)} %hidden_grads.3.refs_5_.refs_1_.refs_0_, bf16[2,128,1536]{2,1,0:T(8,128)(2,1)S(1)} %collective-permute-done.19.refs_2_.refs_1_, ...), custom_call_target="tpu_custom_call", output_to_operand_aliasing={{0}: (3, {}), {1}: (4, {})} | custom-call | tf_op jit(solution)/shard_map/weight_grads/pallas_call | solution.py:46
  (50 shorter events, 16.9 us)
Async XLA Ops:
  0.6 24.4 %collective-permute-start.7 = (bf16[64,3840]{1,0:T(8,128)(2,1)}, bf16[64,3840]{1,0:T(8,128)(2,1)S(1)}, u32[]{:S(2)}, u32[]{:S(2)}) collective-permute-start(bf16[64,3840]{1,0:T(8,128)(2,1)} %refs_2_.1), channel_id=1, source_target_pairs={{16,0},{24,8},{0,16},{8,24},{17,1},{25,9},{1,17},{9,25},{18,2},{26... | collective-permute-start | bytes 1474568 | tf_op jit(solution)/shard_map/ppermute | solution.py:448
  3.6 22.0 %collective-permute-start.8 = (bf16[64,3840]{1,0:T(8,128)(2,1)}, bf16[64,3840]{1,0:T(8,128)(2,1)S(1)}, u32[]{:S(2)}, u32[]{:S(2)}) collective-permute-start(bf16[64,3840]{1,0:T(8,128)(2,1)} %refs_3_.4), channel_id=1, source_target_pairs={{16,0},{24,8},{0,16},{8,24},{17,1},{25,9},{1,17},{9,25},{18,2},{26... | collective-permute-start | bytes 1474568 | tf_op jit(solution)/shard_map/ppermute | solution.py:448
  3.7 6.1 %collective-permute-start.9 = (bf16[32,2048]{1,0:T(8,128)(2,1)}, bf16[32,2048]{1,0:T(8,128)(2,1)S(1)}, u32[]{:S(2)}, u32[]{:S(2)}) collective-permute-start(bf16[32,2048]{1,0:T(8,128)(2,1)} %param.7), channel_id=1, source_target_pairs={{0,1},{1,0},{2,3},{3,2},{4,5},{5,4},{6,7},{7,6},{8,9},{9,8},{10,11... | collective-permute-start | bytes 393224 | tf_op jit(solution)/shard_map/ppermute | solution.py:451
  5.7 8.4 %collective-permute-start = (bf16[32,2048]{1,0:T(8,128)(2,1)}, bf16[32,2048]{1,0:T(8,128)(2,1)S(1)}, u32[]{:S(2)}, u32[]{:S(2)}) collective-permute-start(bf16[32,2048]{1,0:T(8,128)(2,1)} %refs_1_.1), channel_id=1, source_target_pairs={{0,4},{1,5},{2,6},{3,7},{4,0},{5,1},{6,2},{7,3},{8,12},{9,13},{10,... | collective-permute-start | bytes 393224 | tf_op jit(solution)/shard_map/ppermute | solution.py:451
  8.3 6.5 %collective-permute-start.3 = (bf16[32,2048]{1,0:T(8,128)(2,1)}, bf16[32,2048]{1,0:T(8,128)(2,1)S(1)}, u32[]{:S(2)}, u32[]{:S(2)}) collective-permute-start(bf16[32,2048]{1,0:T(8,128)(2,1)} %refs_1_.1), channel_id=1, source_target_pairs={{0,2},{1,3},{2,0},{3,1},{4,6},{5,7},{6,4},{7,5},{8,10},{9,11},{10,... | collective-permute-start | bytes 393224 | tf_op jit(solution)/shard_map/ppermute | solution.py:451
  9.9 5.4 %collective-permute-start.2 = (bf16[32,2048]{1,0:T(8,128)(2,1)}, bf16[32,2048]{1,0:T(8,128)(2,1)S(1)}, u32[]{:S(2)}, u32[]{:S(2)}) collective-permute-start(bf16[32,2048]{1,0:T(8,128)(2,1)} %refs_1_.1), channel_id=1, source_target_pairs={{0,1},{1,0},{2,3},{3,2},{4,5},{5,4},{6,7},{7,6},{8,9},{9,8},{10,11... | collective-permute-start | bytes 393224 | tf_op jit(solution)/shard_map/ppermute | solution.py:451
  14.1 5.3 %collective-permute-start.1 = (bf16[32,2048]{1,0:T(8,128)(2,1)S(1)}, bf16[32,2048]{1,0:T(8,128)(2,1)S(1)}, u32[]{:S(2)}, u32[]{:S(2)}) collective-permute-start(bf16[32,2048]{1,0:T(8,128)(2,1)S(1)} %collective-permute-done.refs_5_), channel_id=1, source_target_pairs={{0,2},{1,3},{2,0},{3,1},{4,6},{5,7},{6,4},{7,5},{8,10},{9,11},{10,... | collective-permute-start | bytes 393224 | tf_op jit(solution)/shard_map/ppermute | solution.py:451
  14.8 10.2 %collective-permute-start.5 = (bf16[32,2048]{1,0:T(8,128)(2,1)S(1)}, bf16[32,2048]{1,0:T(8,128)(2,1)S(1)}, u32[]{:S(2)}, u32[]{:S(2)}) collective-permute-start(bf16[32,2048]{1,0:T(8,128)(2,1)S(1)} %collective-permute-done.refs_5_), channel_id=1, source_target_pairs={{0,1},{1,0},{2,3},{3,2},{4,5},{5,4},{6,7},{7,6},{8,9},{9,8},{10,11... | collective-permute-start | bytes 393224 | tf_op jit(solution)/shard_map/ppermute | solution.py:451
  15.3 9.7 %collective-permute-start.4 = (bf16[32,2048]{1,0:T(8,128)(2,1)S(1)}, bf16[32,2048]{1,0:T(8,128)(2,1)S(1)}, u32[]{:S(2)}, u32[]{:S(2)}) collective-permute-start(bf16[32,2048]{1,0:T(8,128)(2,1)S(1)} %collective-permute-done.2.refs_2_), channel_id=1, source_target_pairs={{0,2},{1,3},{2,0},{3,1},{4,6},{5,7},{6,4},{7,5},{8,10},{9,11},{10,... | collective-permute-start | bytes 393224 | tf_op jit(solution)/shard_map/ppermute | solution.py:451
  19.4 5.6 %collective-permute-start.6 = (bf16[32,2048]{1,0:T(8,128)(2,1)S(1)}, bf16[32,2048]{1,0:T(8,128)(2,1)S(1)}, u32[]{:S(2)}, u32[]{:S(2)}) collective-permute-start(bf16[32,2048]{1,0:T(8,128)(2,1)S(1)} %collective-permute-done.1.refs_4_.refs_7_), channel_id=1, source_target_pairs={{0,1},{1,0},{2,3},{3,2},{4,5},{5,4},{6,7},{7,6},{8,9},{9,8},{10,11... | collective-permute-start | bytes 393224 | tf_op jit(solution)/shard_map/ppermute | solution.py:451
  29.3 7.8 %collective-permute-start.12 = (bf16[128,3840]{1,0:T(8,128)(2,1)S(1)}, bf16[128,3840]{1,0:T(8,128)(2,1)S(1)}, u32[]{:S(2)}, u32[]{:S(2)}) collective-permute-start(bf16[128,3840]{1,0:T(8,128)(2,1)S(1)} %activations.1.refs_0_), channel_id=1, source_target_pairs={{0,8},{8,0},{16,24},{24,16},{1,9},{9,1},{17,25},{25,17},{2,10},{10... | collective-permute-start | bytes 2949128 | tf_op jit(solution)/shard_map/ppermute | solution.py:445
  31.0 16.8 %collective-permute-start.11 = (bf16[128,2304]{1,0:T(8,128)(2,1)S(1)}, bf16[128,2304]{1,0:T(8,128)(2,1)S(1)}, u32[]{:S(2)}, u32[]{:S(2)}) collective-permute-start(bf16[128,2304]{1,0:T(8,128)(2,1)S(1)} %add_convert_fusion.refs_4_.refs_0_), channel_id=1, source_target_pairs={{16,0},{24,8},{0,16},{8,24},{17,1},{25,9},{1,17},{9,25},{18,2},{26... | collective-permute-start | bytes 1769480 | tf_op jit(solution)/shard_map/ppermute | solution.py:448
  32.9 14.8 %collective-permute-start.14 = (bf16[64,2048]{1,0:T(8,128)(2,1)S(1)}, bf16[64,2048]{1,0:T(8,128)(2,1)S(1)}, u32[]{:S(2)}, u32[]{:S(2)}) collective-permute-start(bf16[64,2048]{1,0:T(8,128)(2,1)S(1)} %constant_dynamic-update-slice_fusion.refs_5_.refs_9_.refs_7_.refs_1_), channel_id=1, source_target_pairs={{0,4},{1,5},{2,6},{3,7},{4,0},{5,1},{6,2},{7,3},{8,12},{9,13},{10,... | collective-permute-start | bytes 786440 | tf_op jit(solution)/shard_map/ppermute | solution.py:451
  35.5 12.3 %collective-permute-start.13 = (bf16[64,2048]{1,0:T(8,128)(2,1)S(1)}, bf16[64,2048]{1,0:T(8,128)(2,1)S(1)}, u32[]{:S(2)}, u32[]{:S(2)}) collective-permute-start(bf16[64,2048]{1,0:T(8,128)(2,1)S(1)} %constant_dynamic-update-slice_fusion.refs_5_.refs_9_.refs_7_.refs_1_), channel_id=1, source_target_pairs={{0,2},{1,3},{2,0},{3,1},{4,6},{5,7},{6,4},{7,5},{8,10},{9,11},{10,... | collective-permute-start | bytes 786440 | tf_op jit(solution)/shard_map/ppermute | solution.py:451
  48.6 3.8 %collective-permute-start.17 = (bf16[2,128,2304]{2,1,0:T(8,128)(2,1)S(1)}, bf16[2,128,2304]{2,1,0:T(8,128)(2,1)S(1)}, u32[]{:S(2)}, u32[]{:S(2)}) collective-permute-start(bf16[2,128,2304]{2,1,0:T(8,128)(2,1)S(1)} %get-tuple-element.46.refs_1_.refs_0_), channel_id=1, source_target_pairs={{0,8},{8,0},{16,24},{24,16},{1,9},{9,1},{17,25},{25,17},{2,10},{10... | collective-permute-start | bytes 3538952 | tf_op jit(solution)/shard_map/ppermute | solution.py:445
  50.4 11.2 %collective-permute-start.16 = (bf16[128,1536]{1,0:T(8,128)(2,1)S(1)}, bf16[128,1536]{1,0:T(8,128)(2,1)S(1)}, u32[]{:S(2)}, u32[]{:S(2)}) collective-permute-start(bf16[128,1536]{1,0:T(8,128)(2,1)S(1)} %add_convert_fusion.1.refs_5_.refs_0_), channel_id=1, source_target_pairs={{16,0},{24,8},{0,16},{8,24},{17,1},{25,9},{1,17},{9,25},{18,2},{26... | collective-permute-start | bytes 1179656 | tf_op jit(solution)/shard_map/ppermute | solution.py:448
  50.9 10.2 %collective-permute-start.18 = (bf16[64,2048]{1,0:T(8,128)(2,1)S(1)}, bf16[64,2048]{1,0:T(8,128)(2,1)S(1)}, u32[]{:S(2)}, u32[]{:S(2)}) collective-permute-start(bf16[64,2048]{1,0:T(8,128)(2,1)S(1)} %collective-permute-done.14.refs_11_.refs_9_.refs_3_), channel_id=1, source_target_pairs={{0,2},{1,3},{2,0},{3,1},{4,6},{5,7},{6,4},{7,5},{8,10},{9,11},{10,... | collective-permute-start | bytes 786440 | tf_op jit(solution)/shard_map/ppermute | solution.py:451
  62.1 2.4 %collective-permute-start.19 = (bf16[2,128,1536]{2,1,0:T(8,128)(2,1)S(1)}, bf16[2,128,1536]{2,1,0:T(8,128)(2,1)S(1)}, u32[]{:S(2)}, u32[]{:S(2)}) collective-permute-start(bf16[2,128,1536]{2,1,0:T(8,128)(2,1)S(1)} %hidden_grads.3.refs_5_.refs_1_.refs_0_), channel_id=1, source_target_pairs={{0,8},{8,0},{16,24},{24,16},{1,9},{9,1},{17,25},{25,17},{2,10},{10... | collective-permute-start | bytes 2359304 | tf_op jit(solution)/shard_map/ppermute | solution.py:445
  71.2 8.4 %collective-permute-start.20 = (bf16[64,2048]{1,0:T(8,128)(2,1)S(1)}, bf16[64,2048]{1,0:T(8,128)(2,1)S(1)}, u32[]{:S(2)}, u32[]{:S(2)}) collective-permute-start(bf16[64,2048]{1,0:T(8,128)(2,1)S(1)} %get-tuple-element.49), channel_id=1, source_target_pairs={{0,1},{1,0},{2,3},{3,2},{4,5},{5,4},{6,7},{7,6},{8,9},{9,8},{10,11... | collective-permute-start | bytes 786440 | tf_op jit(solution)/shard_map/ppermute | solution.py:451
  72.7 5.6 %collective-permute-start.21 = (bf16[32,2048]{1,0:T(8,128)(2,1)S(1)}, bf16[32,2048]{1,0:T(8,128)(2,1)S(1)}, u32[]{:S(2)}, u32[]{:S(2)}) collective-permute-start(bf16[32,2048]{1,0:T(8,128)(2,1)S(1)} %get-tuple-element.50), channel_id=1, source_target_pairs={{0,2},{1,3},{2,0},{3,1},{4,6},{5,7},{6,4},{7,5},{8,10},{9,11},{10,... | collective-permute-start | bytes 393224 | tf_op jit(solution)/shard_map/ppermute | solution.py:451
  79.7 8.0 %collective-permute-start.24 = (bf16[32,2048]{1,0:T(8,128)(2,1)S(1)}, bf16[32,2048]{1,0:T(8,128)(2,1)S(1)}, u32[]{:S(2)}, u32[]{:S(2)}) collective-permute-start(bf16[32,2048]{1,0:T(8,128)(2,1)S(1)} %get-tuple-element.55), channel_id=1, source_target_pairs={{0,2},{1,3},{2,0},{3,1},{4,6},{5,7},{6,4},{7,5},{8,10},{9,11},{10,... | collective-permute-start | bytes 393224 | tf_op jit(solution)/shard_map/ppermute | solution.py:451
  81.2 6.5 %collective-permute-start.22 = (bf16[32,2048]{1,0:T(8,128)(2,1)S(1)}, bf16[32,2048]{1,0:T(8,128)(2,1)S(1)}, u32[]{:S(2)}, u32[]{:S(2)}) collective-permute-start(bf16[32,2048]{1,0:T(8,128)(2,1)S(1)} %get-tuple-element.52.refs_5_), channel_id=1, source_target_pairs={{0,1},{1,0},{2,3},{3,2},{4,5},{5,4},{6,7},{7,6},{8,9},{9,8},{10,11... | collective-permute-start | bytes 393224 | tf_op jit(solution)/shard_map/ppermute | solution.py:451
  82.7 13.0 %collective-permute-start.23 = (bf16[32,2048]{1,0:T(8,128)(2,1)S(1)}, bf16[32,2048]{1,0:T(8,128)(2,1)S(1)}, u32[]{:S(2)}, u32[]{:S(2)}) collective-permute-start(bf16[32,2048]{1,0:T(8,128)(2,1)S(1)} %get-tuple-element.53), channel_id=1, source_target_pairs={{0,2},{1,3},{2,0},{3,1},{4,6},{5,7},{6,4},{7,5},{8,10},{9,11},{10,... | collective-permute-start | bytes 393224 | tf_op jit(solution)/shard_map/ppermute | solution.py:451
  87.7 7.9 %collective-permute-start.25 = (bf16[32,2048]{1,0:T(8,128)(2,1)S(1)}, bf16[32,2048]{1,0:T(8,128)(2,1)S(1)}, u32[]{:S(2)}, u32[]{:S(2)}) collective-permute-start(bf16[32,2048]{1,0:T(8,128)(2,1)S(1)} %fold.3.refs_5_), channel_id=1, source_target_pairs={{0,4},{1,5},{2,6},{3,7},{4,0},{5,1},{6,2},{7,3},{8,12},{9,13},{10,... | collective-permute-start | bytes 393224 | tf_op jit(solution)/shard_map/ppermute | solution.py:451
  (3 other events, 15.7 us)

commit v4 on v3

--- a/solution.py
+++ b/solution.py
@@ -113,7 +113,9 @@
 def run_copy(weight, lo, i, piece, ready, sems):
     at = pl.ds(pl.multiple_of(i * piece, piece), piece)
     return pltpu.make_async_copy(
-        weight.at[pl.ds(pl.multiple_of(lo + i * piece, piece), piece)], ready.at[at], sems.at[i]
+        weight.at[pl.ds(pl.multiple_of(lo + i * piece, math.gcd(lo, piece)), piece)],
+        ready.at[at],
+        sems.at[i],
     )
 
 
@@ -353,7 +355,7 @@
     )
 
 
-def fold(terms, wide, deps=()):
+def fold(terms, wide, rows, deps=()):
     arrays, refs_of = [], []
     for term in terms:
         refs_of.append([])
@@ -362,7 +364,7 @@
             if not known:
                 arrays.append(array)
             refs_of[-1].append((known[0] if known else len(arrays) - 1, row))
-    rows, width = min(a.shape[0] for a in arrays), arrays[0].shape[1]
+    width = arrays[0].shape[1]
     kinds = [F32 if w else BF16 for w in wide]
 
     def kernel(*refs):
@@ -510,7 +512,7 @@
 
     mine, *parts = hidden_grads(sums[0], gates, ups, spans[0], parts, [token, *in_blocks])
     grads = [(mine, swap_core(mine))]
-    groups = [(7, 5), (3,), (6, 4, 1), (2,), (0,)] if direct else [range(nr)]
+    groups = [(7, 5), (3, 2), (6, 4, 1), (0,)] if direct else [range(nr)]
     if direct:
         in_blocks.append(swap_col(in_blocks[2], 2))
     total = None
@@ -533,29 +535,32 @@
         return weights, token
 
     cut = divisor(first, first // 2)
-    weights, token = weight_part(None, 0, (0, cut), [])
+    parts = [(0, (0, cut)), (0, (cut, first - cut))]
+    parts = parts[: 1 if cut == first else 2]
+    if len(spans) > 1:
+        parts.insert(0, (1, spans[1]))
+    weights, token = weight_part(None, *parts[0], [])
     ready = blocks[0]
     if direct:
-        far, third, kept, second, result = blocks
-        far, third = swap_col(far, 1), swap_col(third, 2)
-        sent6, sum4, sent1 = fold(
-            [[(kept, 0), (far, 0)], [(kept, 1), (far, 1)], [(kept, 2), (third, 0)]],
-            [False, True, False],
-            deps=[token],
+        far, near, kept, result = blocks
+        far, near = swap_col(far, 1), swap_col(near, 2)
+        sent6, sum4 = fold(
+            [[(kept, 0), (far, 0)], [(kept, 1), (far, 1)]], [False, True], rows, deps=[token]
         )
-        part6, part1 = swap_col(sent6, 2), swap_col(sent1, 1)
-        ready = sent1
-    if cut < first:
-        weights, token = weight_part(weights, 0, (cut, first - cut), [ready])
-    if direct:
-        (sent4,) = fold([[(sum4, 0), (part6, 0)]], [False], deps=[token, part1])
+        part6 = swap_col(sent6, 2)
+        ready = sent6
+    if len(parts) > 1:
+        weights, token = weight_part(weights, *parts[1], [ready])
+    if direct:
+        sent4, sent1 = fold(
+            [[(sum4, 0), (part6, 0)], [(kept, 2), (near, 0)]], [False, False], rows, deps=[token]
+        )
         ready = sent4
-    if len(spans) > 1:
-        weights, token = weight_part(weights, 1, spans[1], [ready])
-    if direct:
-        result = result.astype(F32) + part1.astype(F32)
-        for part in (swap_col(second, 2), swap_col(sent4, 4)):
-            result = result + part.astype(F32)
+    if len(parts) > 2:
+        weights, token = weight_part(weights, *parts[2], [ready])
+    if direct:
+        result = result.astype(F32) + near[rows:].astype(F32) + swap_col(sent1, 1).astype(F32)
+        result = result + swap_col(sent4, 4).astype(F32)
         grad_inputs = result.astype(BF16)
     else:
         grad_inputs = lax.psum_scatter(blocks[0], "col", scatter_dimension=0, tiled=True)

time: 96.5 us -> 95.7 us (level)
    ppermute x17 -> x16, starting transfers between devices: 25.7 us -> 25.3 us  [swap_col(): return lax.ppermute(value, 'col', [(c, c ^ mask) for c in range(nc)])]
    ppermute x17 -> x16, waiting for transfers between devices: 10.2 us -> 9.77 us  [swap_col(): return lax.ppermute(value, 'col', [(c, c ^ mask) for c in range(nc)])]
  transfers between devices with their start and end apart: 26 -> 25, of which waited for: 10 -> 11; matrix products, arithmetic and copies ran while one was open for 0% -> 0% of each run, Pallas kernels for 37% -> 38%
where the time goes in v4:
time: 95.7 us; the launch traced here: 95.5 us
  Pallas kernels  47 us (49%)
  starting transfers between devices  32 us (33%)
  waiting for transfers between devices  14.7 us (15%)
    pallas_call x14, Pallas kernels, call(): pl.pallas_call(body, out_shape=out_shape, in_specs=list(in_specs) + [ANYW...  47 us
    ppermute x16, starting transfers between devices, swap_col(): return lax.ppermute(value, 'col', [(c, c ^ mask) for c in range(nc)])  25.3 us
    ppermute x16, waiting for transfers between devices, swap_col(): return lax.ppermute(value, 'col', [(c, c ^ mask) for c in range(nc)])  9.77 us
    ppermute x4, starting transfers between devices, from_x(): lax.ppermute(value, 'row', [((r + offset * CORES) % nr, r) for r in range...  5.44 us
    ppermute x5, waiting for transfers between devices, swap_core(): return lax.ppermute(value, 'row', [(r, r ^ 1) for r in range(nr)])  3.87 us
  transfers between devices with their start and end apart: 25, of which 11 were waited for; matrix products, arithmetic and copies ran while one was open for 0% of the time, Pallas kernels for 38%

profile of v4, /device:TPU:0, one launch (start us, length us, event | category | flops | bytes accessed | tf_op | source)
XLA Modules:
  0.0 95.5 jit_solution(13594446152126782545)
XLA Ops:
  0.6 3.0 %collective-permute-start.7 = (bf16[64,3840]{1,0:T(8,128)(2,1)}, bf16[64,3840]{1,0:T(8,128)(2,1)S(1)}, u32[]{:S(2)}, u32[]{:S(2)}) collective-permute-start(bf16[64,3840]{1,0:T(8,128)(2,1)} %refs_2_.1), channel_id=1, source_target_pairs={{16,0},{24,8},{0,16},{8,24},{17,1},{25,9},{1,17},{9,25},{18,2},{26... | collective-permute-start | bytes 1474568 | tf_op jit(solution)/shard_map/ppermute | solution.py:450
  3.7 2.0 %collective-permute-start.9 = (bf16[32,2048]{1,0:T(8,128)(2,1)}, bf16[32,2048]{1,0:T(8,128)(2,1)S(1)}, u32[]{:S(2)}, u32[]{:S(2)}) collective-permute-start(bf16[32,2048]{1,0:T(8,128)(2,1)} %param.7), channel_id=1, source_target_pairs={{0,1},{1,0},{2,3},{3,2},{4,5},{5,4},{6,7},{7,6},{8,9},{9,8},{10,11... | collective-permute-start | bytes 393224 | tf_op jit(solution)/shard_map/ppermute | solution.py:453
  5.7 2.6 %collective-permute-start = (bf16[32,2048]{1,0:T(8,128)(2,1)}, bf16[32,2048]{1,0:T(8,128)(2,1)S(1)}, u32[]{:S(2)}, u32[]{:S(2)}) collective-permute-start(bf16[32,2048]{1,0:T(8,128)(2,1)} %refs_1_.1), channel_id=1, source_target_pairs={{0,4},{1,5},{2,6},{3,7},{4,0},{5,1},{6,2},{7,3},{8,12},{9,13},{10,... | collective-permute-start | bytes 393224 | tf_op jit(solution)/shard_map/ppermute | solution.py:453
  8.3 1.6 %collective-permute-start.3 = (bf16[32,2048]{1,0:T(8,128)(2,1)}, bf16[32,2048]{1,0:T(8,128)(2,1)S(1)}, u32[]{:S(2)}, u32[]{:S(2)}) collective-permute-start(bf16[32,2048]{1,0:T(8,128)(2,1)} %refs_1_.1), channel_id=1, source_target_pairs={{0,2},{1,3},{2,0},{3,1},{4,6},{5,7},{6,4},{7,5},{8,10},{9,11},{10,... | collective-permute-start | bytes 393224 | tf_op jit(solution)/shard_map/ppermute | solution.py:453
  10.9 3.2 %collective-permute-done.refs_5_ = bf16[32,2048]{1,0:T(8,128)(2,1)S(1)} collective-permute-done((bf16[32,2048]{1,0:T(8,128)(2,1)}, bf16[32,2048]{1,0:T(8,128)(2,1)S(1)}, u32[]{:S(2)}, u32[]{:S(2)}) %collective-permute-start) | collective-permute-done | bytes 131104 | tf_op jit(solution)/shard_map/ppermute | solution.py:453
  16.6 2.8 %collective-permute-done.1.refs_4_.refs_7_ = bf16[32,2048]{1,0:T(8,128)(2,1)S(1)} collective-permute-done((bf16[32,2048]{1,0:T(8,128)(2,1)S(1)}, bf16[32,2048]{1,0:T(8,128)(2,1)S(1)}, u32[]{:S(2)}, u32[]{:S(2)}) %collective-permute-start.1) | collective-permute-done | bytes 131104 | tf_op jit(solution)/shard_map/ppermute | solution.py:453
  19.4 1.5 %collective-permute-start.6 = (bf16[32,2048]{1,0:T(8,128)(2,1)S(1)}, bf16[32,2048]{1,0:T(8,128)(2,1)S(1)}, u32[]{:S(2)}, u32[]{:S(2)}) collective-permute-start(bf16[32,2048]{1,0:T(8,128)(2,1)S(1)} %collective-permute-done.1.refs_4_.refs_7_), channel_id=1, source_target_pairs={{0,1},{1,0},{2,3},{3,2},{4,5},{5,4},{6,7},{7,6},{8,9},{9,8},{10,11... | collective-permute-start | bytes 393224 | tf_op jit(solution)/shard_map/ppermute | solution.py:453
  21.0 4.0 %fetch.1 = (bf16[2304,2048]{1,0:T(8,128)(2,1)S(1)}, bf16[32,2048]{1,0:T(8,128)(2,1)S(1)}, bf16[64,3840]{1,0:T(8,128)(2,1)S(1)}, bf16[64,3840]{1,0:T(8,128)(2,1)S(1)}) custom-call(bf16[3840,2048]{1,0:T(8,128)(2,1)} %refs_3_.5, bf16[32,2048]{1,0:T(8,128)(2,1)} %refs_1_.1, bf16[64,3840]{1,0:T(8,128)(2,1)} %refs_2_.1, bf16[64,3840]{1,0:T(8,128)(2,1)} %refs_3_.4, ...), custom_call_target="tpu_custom_call" | custom-call | tf_op jit(solution)/shard_map/fetch/pallas_call | solution.py:46
  25.6 3.2 %first_partial.1 = (bf16[128,2304]{1,0:T(8,128)(2,1)S(1)}, bf16[128,2304]{1,0:T(8,128)(2,1)S(1)}, bf16[256,2048]{1,0:T(8,128)(2,1)S(1)}) custom-call(s32[8]{0:T(128)S(1)} %stack.35.refs_0_, bf16[32,2048]{1,0:T(8,128)(2,1)S(1)} %get-tuple-element.34.refs_1_, bf16[32,2048]{1,0:T(8,128)(2,1)S(1)} %collective-permute-done.2.refs_2_, ...), custom_call_target="tpu_custom_call" | custom-call | tf_op jit(solution)/shard_map/first_partial/pallas_call | solution.py:46
  31.0 1.8 %collective-permute-start.11 = (bf16[128,2304]{1,0:T(8,128)(2,1)S(1)}, bf16[128,2304]{1,0:T(8,128)(2,1)S(1)}, u32[]{:S(2)}, u32[]{:S(2)}) collective-permute-start(bf16[128,2304]{1,0:T(8,128)(2,1)S(1)} %add_convert_fusion.refs_4_.refs_0_), channel_id=1, source_target_pairs={{16,0},{24,8},{0,16},{8,24},{17,1},{25,9},{1,17},{9,25},{18,2},{26... | collective-permute-start | bytes 1769480 | tf_op jit(solution)/shard_map/ppermute | solution.py:450
  32.9 2.7 %collective-permute-start.14 = (bf16[64,2048]{1,0:T(8,128)(2,1)S(1)}, bf16[64,2048]{1,0:T(8,128)(2,1)S(1)}, u32[]{:S(2)}, u32[]{:S(2)}) collective-permute-start(bf16[64,2048]{1,0:T(8,128)(2,1)S(1)} %constant_dynamic-update-slice_fusion.refs_5_.refs_9_.refs_7_.refs_1_), channel_id=1, source_target_pairs={{0,4},{1,5},{2,6},{3,7},{4,0},{5,1},{6,2},{7,3},{8,12},{9,13},{10,... | collective-permute-start | bytes 786440 | tf_op jit(solution)/shard_map/ppermute | solution.py:453
  35.5 1.6 %collective-permute-start.13 = (bf16[64,2048]{1,0:T(8,128)(2,1)S(1)}, bf16[64,2048]{1,0:T(8,128)(2,1)S(1)}, u32[]{:S(2)}, u32[]{:S(2)}) collective-permute-start(bf16[64,2048]{1,0:T(8,128)(2,1)S(1)} %constant_dynamic-update-slice_fusion.refs_5_.refs_9_.refs_7_.refs_1_), channel_id=1, source_target_pairs={{0,2},{1,3},{2,0},{3,1},{4,6},{5,7},{6,4},{7,5},{8,10},{9,11},{10,... | collective-permute-start | bytes 786440 | tf_op jit(solution)/shard_map/ppermute | solution.py:453
  37.1 7.8 %down_grad.1 = (bf16[3840,2048]{1,0:T(8,128)(2,1)}, f32[8,128]{1,0:T(8,128)S(1)}, bf16[128,1536]{1,0:T(8,128)(2,1)S(1)}, bf16[128,1536]{1,0:T(8,128)(2,1)S(1)}) custom-call(bf16[128,3840]{1,0:T(8,128)(2,1)S(1)} %activations.1.refs_0_, bf16[128,3840]{1,0:T(8,128)(2,1)S(1)} %collective-permute-done.12.refs_1_, ...), custom_call_target="tpu_custom_call" | custom-call | tf_op jit(solution)/shard_map/down_grad/pallas_call | solution.py:46
  44.9 2.7 %collective-permute-done.14.refs_11_.refs_9_.refs_3_ = bf16[64,2048]{1,0:T(8,128)(2,1)S(1)} collective-permute-done((bf16[64,2048]{1,0:T(8,128)(2,1)S(1)}, bf16[64,2048]{1,0:T(8,128)(2,1)S(1)}, u32[]{:S(2)}, u32[]{:S(2)}) %collective-permute-start.14) | collective-permute-done | bytes 262176 | tf_op jit(solution)/shard_map/ppermute | solution.py:453
  52.4 8.7 %input_grads.2.refs_6_.refs_5_ = f32[256,2048]{1,0:T(8,128)S(1)} custom-call(s32[8]{0:T(128)S(1)} %stack.35.refs_0_, bf16[2,128,2304]{2,1,0:T(8,128)(2,1)S(1)} %get-tuple-element.46.refs_1_.refs_0_, bf16[2,128,2304]{2,1,0:T(8,128)(2,1)S(1)} %collective-permute-done.17.refs_2_.refs_1_, bf16[2048,3840]{1,0:T(8,128)(2,1)} %refs_3_.7, ...), custom_call_target="tpu_custom_call" | custom-call | tf_op jit(solution)/shard_map/input_grads/pallas_call | solution.py:46
  62.8 1.6 %collective-permute-done.19.refs_2_.refs_1_ = bf16[2,128,1536]{2,1,0:T(8,128)(2,1)S(1)} collective-permute-done((bf16[2,128,1536]{2,1,0:T(8,128)(2,1)S(1)}, bf16[2,128,1536]{2,1,0:T(8,128)(2,1)S(1)}, u32[]{:S(2)}, u32[]{:S(2)}) %collective-permute-start.19) | collective-permute-done | bytes 786464 | tf_op jit(solution)/shard_map/ppermute | solution.py:447
  64.4 6.7 %input_grads.3 = (bf16[64,2048]{1,0:T(8,128)(2,1)S(1)}, bf16[64,2048]{1,0:T(8,128)(2,1)S(1)}, bf16[96,2048]{1,0:T(8,128)(2,1)S(1)}, bf16[32,2048]{1,0:T(8,128)(2,1)S(1)}) custom-call(s32[8]{0:T(128)S(1)} %stack.35.refs_0_, bf16[2,128,1536]{2,1,0:T(8,128)(2,1)S(1)} %hidden_grads.3.refs_5_.refs_1_.refs_0_, ...), custom_call_target="tpu_custom_call" | custom-call | tf_op jit(solution)/shard_map/input_grads/pallas_call | solution.py:46
  71.2 1.6 %collective-permute-start.21 = (bf16[64,2048]{1,0:T(8,128)(2,1)S(1)}, bf16[64,2048]{1,0:T(8,128)(2,1)S(1)}, u32[]{:S(2)}, u32[]{:S(2)}) collective-permute-start(bf16[64,2048]{1,0:T(8,128)(2,1)S(1)} %get-tuple-element.50), channel_id=1, source_target_pairs={{0,1},{1,0},{2,3},{3,2},{4,5},{5,4},{6,7},{7,6},{8,9},{9,8},{10,11... | collective-permute-start | bytes 786440 | tf_op jit(solution)/shard_map/ppermute | solution.py:453
  74.2 5.3 %weight_grads.3 = (bf16[2048,3840]{1,0:T(8,128)(2,1)}, bf16[2048,3840]{1,0:T(8,128)(2,1)}, f32[8,128]{1,0:T(8,128)S(1)}) custom-call(bf16[2,128,1536]{2,1,0:T(8,128)(2,1)S(1)} %hidden_grads.3.refs_5_.refs_1_.refs_0_, bf16[2,128,1536]{2,1,0:T(8,128)(2,1)S(1)} %collective-permute-done.19.refs_2_.refs_1_, bf16[256,2048]{1,0:T(8,128)(2,1)S(1)} %assemble.1.refs_6_.refs_2_), custom_call_target="tpu_custom_call" | custom-call | tf_op jit(solution)/shard_map/weight_grads/pallas_call | solution.py:46
  79.6 1.5 %collective-permute-start.22 = (bf16[32,2048]{1,0:T(8,128)(2,1)S(1)}, bf16[32,2048]{1,0:T(8,128)(2,1)S(1)}, u32[]{:S(2)}, u32[]{:S(2)}) collective-permute-start(bf16[32,2048]{1,0:T(8,128)(2,1)S(1)} %get-tuple-element.53.refs_5_), channel_id=1, source_target_pairs={{0,2},{1,3},{2,0},{3,1},{4,6},{5,7},{6,4},{7,5},{8,10},{9,11},{10,... | collective-permute-start | bytes 393224 | tf_op jit(solution)/shard_map/ppermute | solution.py:453
  81.1 4.1 %weight_grads.4 = (bf16[2048,3840]{1,0:T(8,128)(2,1)}, bf16[2048,3840]{1,0:T(8,128)(2,1)}, f32[8,128]{1,0:T(8,128)S(1)}) custom-call(bf16[2,128,2304]{2,1,0:T(8,128)(2,1)S(1)} %get-tuple-element.46.refs_1_.refs_0_, bf16[2,128,2304]{2,1,0:T(8,128)(2,1)S(1)} %collective-permute-done.17.refs_2_.refs_1_, ...), custom_call_target="tpu_custom_call", output_to_operand_aliasing={{0}: (3, {}), {1}: (4, {})} | custom-call | tf_op jit(solution)/shard_map/weight_grads/pallas_call | solution.py:46
  85.4 1.6 %collective-permute-start.23 = (bf16[32,2048]{1,0:T(8,128)(2,1)S(1)}, bf16[32,2048]{1,0:T(8,128)(2,1)S(1)}, u32[]{:S(2)}, u32[]{:S(2)}) collective-permute-start(bf16[32,2048]{1,0:T(8,128)(2,1)S(1)} %get-tuple-element.57), channel_id=1, source_target_pairs={{0,1},{1,0},{2,3},{3,2},{4,5},{5,4},{6,7},{7,6},{8,9},{9,8},{10,11... | collective-permute-start | bytes 393224 | tf_op jit(solution)/shard_map/ppermute | solution.py:453
  87.0 2.3 %collective-permute-start.24 = (bf16[32,2048]{1,0:T(8,128)(2,1)S(1)}, bf16[32,2048]{1,0:T(8,128)(2,1)S(1)}, u32[]{:S(2)}, u32[]{:S(2)}) collective-permute-start(bf16[32,2048]{1,0:T(8,128)(2,1)S(1)} %get-tuple-element.58.refs_5_), channel_id=1, source_target_pairs={{0,4},{1,5},{2,6},{3,7},{4,0},{5,1},{6,2},{7,3},{8,12},{9,13},{10,... | collective-permute-start | bytes 393224 | tf_op jit(solution)/shard_map/ppermute | solution.py:453
  89.3 4.7 %weight_grads.5 = (bf16[2048,3840]{1,0:T(8,128)(2,1)}, bf16[2048,3840]{1,0:T(8,128)(2,1)}, f32[8,128]{1,0:T(8,128)}) custom-call(bf16[2,128,2304]{2,1,0:T(8,128)(2,1)S(1)} %get-tuple-element.46.refs_1_.refs_0_, bf16[2,128,2304]{2,1,0:T(8,128)(2,1)S(1)} %collective-permute-done.17.refs_2_.refs_1_, ...), custom_call_target="tpu_custom_call", output_to_operand_aliasing={{0}: (3, {}), {1}: (4, {})} | custom-call | tf_op jit(solution)/shard_map/weight_grads/pallas_call | solution.py:46
  (48 shorter events, 15.9 us)
Async XLA Ops:
  0.6 24.4 %collective-permute-start.7 = (bf16[64,3840]{1,0:T(8,128)(2,1)}, bf16[64,3840]{1,0:T(8,128)(2,1)S(1)}, u32[]{:S(2)}, u32[]{:S(2)}) collective-permute-start(bf16[64,3840]{1,0:T(8,128)(2,1)} %refs_2_.1), channel_id=1, source_target_pairs={{16,0},{24,8},{0,16},{8,24},{17,1},{25,9},{1,17},{9,25},{18,2},{26... | collective-permute-start | bytes 1474568 | tf_op jit(solution)/shard_map/ppermute | solution.py:450
  3.6 22.0 %collective-permute-start.8 = (bf16[64,3840]{1,0:T(8,128)(2,1)}, bf16[64,3840]{1,0:T(8,128)(2,1)S(1)}, u32[]{:S(2)}, u32[]{:S(2)}) collective-permute-start(bf16[64,3840]{1,0:T(8,128)(2,1)} %refs_3_.4), channel_id=1, source_target_pairs={{16,0},{24,8},{0,16},{8,24},{17,1},{25,9},{1,17},{9,25},{18,2},{26... | collective-permute-start | bytes 1474568 | tf_op jit(solution)/shard_map/ppermute | solution.py:450
  3.7 6.1 %collective-permute-start.9 = (bf16[32,2048]{1,0:T(8,128)(2,1)}, bf16[32,2048]{1,0:T(8,128)(2,1)S(1)}, u32[]{:S(2)}, u32[]{:S(2)}) collective-permute-start(bf16[32,2048]{1,0:T(8,128)(2,1)} %param.7), channel_id=1, source_target_pairs={{0,1},{1,0},{2,3},{3,2},{4,5},{5,4},{6,7},{7,6},{8,9},{9,8},{10,11... | collective-permute-start | bytes 393224 | tf_op jit(solution)/shard_map/ppermute | solution.py:453
  5.7 8.4 %collective-permute-start = (bf16[32,2048]{1,0:T(8,128)(2,1)}, bf16[32,2048]{1,0:T(8,128)(2,1)S(1)}, u32[]{:S(2)}, u32[]{:S(2)}) collective-permute-start(bf16[32,2048]{1,0:T(8,128)(2,1)} %refs_1_.1), channel_id=1, source_target_pairs={{0,4},{1,5},{2,6},{3,7},{4,0},{5,1},{6,2},{7,3},{8,12},{9,13},{10,... | collective-permute-start | bytes 393224 | tf_op jit(solution)/shard_map/ppermute | solution.py:453
  8.3 6.5 %collective-permute-start.3 = (bf16[32,2048]{1,0:T(8,128)(2,1)}, bf16[32,2048]{1,0:T(8,128)(2,1)S(1)}, u32[]{:S(2)}, u32[]{:S(2)}) collective-permute-start(bf16[32,2048]{1,0:T(8,128)(2,1)} %refs_1_.1), channel_id=1, source_target_pairs={{0,2},{1,3},{2,0},{3,1},{4,6},{5,7},{6,4},{7,5},{8,10},{9,11},{10,... | collective-permute-start | bytes 393224 | tf_op jit(solution)/shard_map/ppermute | solution.py:453
  9.9 5.4 %collective-permute-start.2 = (bf16[32,2048]{1,0:T(8,128)(2,1)}, bf16[32,2048]{1,0:T(8,128)(2,1)S(1)}, u32[]{:S(2)}, u32[]{:S(2)}) collective-permute-start(bf16[32,2048]{1,0:T(8,128)(2,1)} %refs_1_.1), channel_id=1, source_target_pairs={{0,1},{1,0},{2,3},{3,2},{4,5},{5,4},{6,7},{7,6},{8,9},{9,8},{10,11... | collective-permute-start | bytes 393224 | tf_op jit(solution)/shard_map/ppermute | solution.py:453
  14.1 5.3 %collective-permute-start.1 = (bf16[32,2048]{1,0:T(8,128)(2,1)S(1)}, bf16[32,2048]{1,0:T(8,128)(2,1)S(1)}, u32[]{:S(2)}, u32[]{:S(2)}) collective-permute-start(bf16[32,2048]{1,0:T(8,128)(2,1)S(1)} %collective-permute-done.refs_5_), channel_id=1, source_target_pairs={{0,2},{1,3},{2,0},{3,1},{4,6},{5,7},{6,4},{7,5},{8,10},{9,11},{10,... | collective-permute-start | bytes 393224 | tf_op jit(solution)/shard_map/ppermute | solution.py:453
  14.8 10.2 %collective-permute-start.5 = (bf16[32,2048]{1,0:T(8,128)(2,1)S(1)}, bf16[32,2048]{1,0:T(8,128)(2,1)S(1)}, u32[]{:S(2)}, u32[]{:S(2)}) collective-permute-start(bf16[32,2048]{1,0:T(8,128)(2,1)S(1)} %collective-permute-done.refs_5_), channel_id=1, source_target_pairs={{0,1},{1,0},{2,3},{3,2},{4,5},{5,4},{6,7},{7,6},{8,9},{9,8},{10,11... | collective-permute-start | bytes 393224 | tf_op jit(solution)/shard_map/ppermute | solution.py:453
  15.3 9.7 %collective-permute-start.4 = (bf16[32,2048]{1,0:T(8,128)(2,1)S(1)}, bf16[32,2048]{1,0:T(8,128)(2,1)S(1)}, u32[]{:S(2)}, u32[]{:S(2)}) collective-permute-start(bf16[32,2048]{1,0:T(8,128)(2,1)S(1)} %collective-permute-done.2.refs_2_), channel_id=1, source_target_pairs={{0,2},{1,3},{2,0},{3,1},{4,6},{5,7},{6,4},{7,5},{8,10},{9,11},{10,... | collective-permute-start | bytes 393224 | tf_op jit(solution)/shard_map/ppermute | solution.py:453
  19.4 5.6 %collective-permute-start.6 = (bf16[32,2048]{1,0:T(8,128)(2,1)S(1)}, bf16[32,2048]{1,0:T(8,128)(2,1)S(1)}, u32[]{:S(2)}, u32[]{:S(2)}) collective-permute-start(bf16[32,2048]{1,0:T(8,128)(2,1)S(1)} %collective-permute-done.1.refs_4_.refs_7_), channel_id=1, source_target_pairs={{0,1},{1,0},{2,3},{3,2},{4,5},{5,4},{6,7},{7,6},{8,9},{9,8},{10,11... | collective-permute-start | bytes 393224 | tf_op jit(solution)/shard_map/ppermute | solution.py:453
  28.8 2.1 %collective-permute-start.10 = (bf16[128,2304]{1,0:T(8,128)(2,1)S(1)}, bf16[128,2304]{1,0:T(8,128)(2,1)S(1)}, u32[]{:S(2)}, u32[]{:S(2)}) collective-permute-start(bf16[128,2304]{1,0:T(8,128)(2,1)S(1)} %get-tuple-element.37), channel_id=1, source_target_pairs={{0,8},{8,0},{16,24},{24,16},{1,9},{9,1},{17,25},{25,17},{2,10},{10... | collective-permute-start | bytes 1769480 | tf_op jit(solution)/shard_map/ppermute | solution.py:447
  29.3 7.8 %collective-permute-start.12 = (bf16[128,3840]{1,0:T(8,128)(2,1)S(1)}, bf16[128,3840]{1,0:T(8,128)(2,1)S(1)}, u32[]{:S(2)}, u32[]{:S(2)}) collective-permute-start(bf16[128,3840]{1,0:T(8,128)(2,1)S(1)} %activations.1.refs_0_), channel_id=1, source_target_pairs={{0,8},{8,0},{16,24},{24,16},{1,9},{9,1},{17,25},{25,17},{2,10},{10... | collective-permute-start | bytes 2949128 | tf_op jit(solution)/shard_map/ppermute | solution.py:447
  31.0 16.8 %collective-permute-start.11 = (bf16[128,2304]{1,0:T(8,128)(2,1)S(1)}, bf16[128,2304]{1,0:T(8,128)(2,1)S(1)}, u32[]{:S(2)}, u32[]{:S(2)}) collective-permute-start(bf16[128,2304]{1,0:T(8,128)(2,1)S(1)} %add_convert_fusion.refs_4_.refs_0_), channel_id=1, source_target_pairs={{16,0},{24,8},{0,16},{8,24},{17,1},{25,9},{1,17},{9,25},{18,2},{26... | collective-permute-start | bytes 1769480 | tf_op jit(solution)/shard_map/ppermute | solution.py:450
  32.9 14.8 %collective-permute-start.14 = (bf16[64,2048]{1,0:T(8,128)(2,1)S(1)}, bf16[64,2048]{1,0:T(8,128)(2,1)S(1)}, u32[]{:S(2)}, u32[]{:S(2)}) collective-permute-start(bf16[64,2048]{1,0:T(8,128)(2,1)S(1)} %constant_dynamic-update-slice_fusion.refs_5_.refs_9_.refs_7_.refs_1_), channel_id=1, source_target_pairs={{0,4},{1,5},{2,6},{3,7},{4,0},{5,1},{6,2},{7,3},{8,12},{9,13},{10,... | collective-permute-start | bytes 786440 | tf_op jit(solution)/shard_map/ppermute | solution.py:453
  35.5 12.3 %collective-permute-start.13 = (bf16[64,2048]{1,0:T(8,128)(2,1)S(1)}, bf16[64,2048]{1,0:T(8,128)(2,1)S(1)}, u32[]{:S(2)}, u32[]{:S(2)}) collective-permute-start(bf16[64,2048]{1,0:T(8,128)(2,1)S(1)} %constant_dynamic-update-slice_fusion.refs_5_.refs_9_.refs_7_.refs_1_), channel_id=1, source_target_pairs={{0,2},{1,3},{2,0},{3,1},{4,6},{5,7},{6,4},{7,5},{8,10},{9,11},{10,... | collective-permute-start | bytes 786440 | tf_op jit(solution)/shard_map/ppermute | solution.py:453
  48.6 3.8 %collective-permute-start.17 = (bf16[2,128,2304]{2,1,0:T(8,128)(2,1)S(1)}, bf16[2,128,2304]{2,1,0:T(8,128)(2,1)S(1)}, u32[]{:S(2)}, u32[]{:S(2)}) collective-permute-start(bf16[2,128,2304]{2,1,0:T(8,128)(2,1)S(1)} %get-tuple-element.46.refs_1_.refs_0_), channel_id=1, source_target_pairs={{0,8},{8,0},{16,24},{24,16},{1,9},{9,1},{17,25},{25,17},{2,10},{10... | collective-permute-start | bytes 3538952 | tf_op jit(solution)/shard_map/ppermute | solution.py:447
  50.4 11.2 %collective-permute-start.16 = (bf16[128,1536]{1,0:T(8,128)(2,1)S(1)}, bf16[128,1536]{1,0:T(8,128)(2,1)S(1)}, u32[]{:S(2)}, u32[]{:S(2)}) collective-permute-start(bf16[128,1536]{1,0:T(8,128)(2,1)S(1)} %add_convert_fusion.1.refs_5_.refs_0_), channel_id=1, source_target_pairs={{16,0},{24,8},{0,16},{8,24},{17,1},{25,9},{1,17},{9,25},{18,2},{26... | collective-permute-start | bytes 1179656 | tf_op jit(solution)/shard_map/ppermute | solution.py:450
  50.9 10.2 %collective-permute-start.18 = (bf16[64,2048]{1,0:T(8,128)(2,1)S(1)}, bf16[64,2048]{1,0:T(8,128)(2,1)S(1)}, u32[]{:S(2)}, u32[]{:S(2)}) collective-permute-start(bf16[64,2048]{1,0:T(8,128)(2,1)S(1)} %collective-permute-done.14.refs_11_.refs_9_.refs_3_), channel_id=1, source_target_pairs={{0,2},{1,3},{2,0},{3,1},{4,6},{5,7},{6,4},{7,5},{8,10},{9,11},{10,... | collective-permute-start | bytes 786440 | tf_op jit(solution)/shard_map/ppermute | solution.py:453
  62.1 2.4 %collective-permute-start.19 = (bf16[2,128,1536]{2,1,0:T(8,128)(2,1)S(1)}, bf16[2,128,1536]{2,1,0:T(8,128)(2,1)S(1)}, u32[]{:S(2)}, u32[]{:S(2)}) collective-permute-start(bf16[2,128,1536]{2,1,0:T(8,128)(2,1)S(1)} %hidden_grads.3.refs_5_.refs_1_.refs_0_), channel_id=1, source_target_pairs={{0,8},{8,0},{16,24},{24,16},{1,9},{9,1},{17,25},{25,17},{2,10},{10... | collective-permute-start | bytes 2359304 | tf_op jit(solution)/shard_map/ppermute | solution.py:447
  71.2 8.4 %collective-permute-start.21 = (bf16[64,2048]{1,0:T(8,128)(2,1)S(1)}, bf16[64,2048]{1,0:T(8,128)(2,1)S(1)}, u32[]{:S(2)}, u32[]{:S(2)}) collective-permute-start(bf16[64,2048]{1,0:T(8,128)(2,1)S(1)} %get-tuple-element.50), channel_id=1, source_target_pairs={{0,1},{1,0},{2,3},{3,2},{4,5},{5,4},{6,7},{7,6},{8,9},{9,8},{10,11... | collective-permute-start | bytes 786440 | tf_op jit(solution)/shard_map/ppermute | solution.py:453
  72.7 12.6 %collective-permute-start.20 = (bf16[64,2048]{1,0:T(8,128)(2,1)S(1)}, bf16[64,2048]{1,0:T(8,128)(2,1)S(1)}, u32[]{:S(2)}, u32[]{:S(2)}) collective-permute-start(bf16[64,2048]{1,0:T(8,128)(2,1)S(1)} %get-tuple-element.48), channel_id=1, source_target_pairs={{0,2},{1,3},{2,0},{3,1},{4,6},{5,7},{6,4},{7,5},{8,10},{9,11},{10,... | collective-permute-start | bytes 786440 | tf_op jit(solution)/shard_map/ppermute | solution.py:453
  79.6 5.7 %collective-permute-start.22 = (bf16[32,2048]{1,0:T(8,128)(2,1)S(1)}, bf16[32,2048]{1,0:T(8,128)(2,1)S(1)}, u32[]{:S(2)}, u32[]{:S(2)}) collective-permute-start(bf16[32,2048]{1,0:T(8,128)(2,1)S(1)} %get-tuple-element.53.refs_5_), channel_id=1, source_target_pairs={{0,2},{1,3},{2,0},{3,1},{4,6},{5,7},{6,4},{7,5},{8,10},{9,11},{10,... | collective-permute-start | bytes 393224 | tf_op jit(solution)/shard_map/ppermute | solution.py:453
  85.4 8.7 %collective-permute-start.23 = (bf16[32,2048]{1,0:T(8,128)(2,1)S(1)}, bf16[32,2048]{1,0:T(8,128)(2,1)S(1)}, u32[]{:S(2)}, u32[]{:S(2)}) collective-permute-start(bf16[32,2048]{1,0:T(8,128)(2,1)S(1)} %get-tuple-element.57), channel_id=1, source_target_pairs={{0,1},{1,0},{2,3},{3,2},{4,5},{5,4},{6,7},{7,6},{8,9},{9,8},{10,11... | collective-permute-start | bytes 393224 | tf_op jit(solution)/shard_map/ppermute | solution.py:453
  87.0 7.9 %collective-permute-start.24 = (bf16[32,2048]{1,0:T(8,128)(2,1)S(1)}, bf16[32,2048]{1,0:T(8,128)(2,1)S(1)}, u32[]{:S(2)}, u32[]{:S(2)}) collective-permute-start(bf16[32,2048]{1,0:T(8,128)(2,1)S(1)} %get-tuple-element.58.refs_5_), channel_id=1, source_target_pairs={{0,4},{1,5},{2,6},{3,7},{4,0},{5,1},{6,2},{7,3},{8,12},{9,13},{10,... | collective-permute-start | bytes 393224 | tf_op jit(solution)/shard_map/ppermute | solution.py:453
  (2 other events, 13.7 us)

commit v5 on v4

--- a/solution.py
+++ b/solution.py
@@ -143,13 +143,13 @@
     tokens = sum(block.shape[0] for block in blocks)
     run = tokens // offsets.shape[0]
     half, units = tokens // CORES, rows.shape[0]
-    piece = divisor(units, 640, 256)
+    piece = min(units, 256)
 
     def kernel(offs, *refs):
         weight, keep, send, a = refs[count:]
         lay(refs[:count], offs, a, run)
         for lo in range(0, units, piece):
-            at = slice(lo, lo + piece)
+            at = slice(lo, min(lo + piece, units))
             part = lax.dot_general(a[...], weight[at, :], NT, preferred_element_type=F32)
             part = part.astype(BF16)
             keep[:, at] = part[:half]
@@ -189,14 +189,14 @@
     )
 
 
-def hidden_grads(sums, gates, ups, span, passed=(), deps=()):
+def hidden_grads(sums, gates, ups, span, deps=()):
     count = len(gates)
     rows = gates[0].shape[0]
     lo, units = span
     cols = slice(lo, lo + units)
 
     def kernel(*refs):
-        out = refs[3 * count + len(passed)]
+        out = refs[3 * count]
         for i in range(count):
             grad = 0.0
             for o in range(count):
@@ -209,17 +209,30 @@
             out[0, at, :] = (grad * up * sig * (1.0 + gate * (1.0 - sig))).astype(BF16)
             out[1, at, :] = (grad * gate * sig).astype(BF16)
 
-    shapes = [jax.ShapeDtypeStruct((2, rows * count, units), BF16)]
-    shapes += [jax.ShapeDtypeStruct(p.shape, p.dtype) for p in passed]
-    return call(
-        kernel,
-        [*sums, *gates, *ups, *passed],
-        [WHOLE] * (3 * count) + [ANYWHERE] * len(passed),
-        shapes,
-        [WHOLE] + [ANYWHERE] * len(passed),
-        deps,
-        aliases={3 * count + i: 1 + i for i in range(len(passed))},
+    return call(
+        kernel,
+        [*sums, *gates, *ups],
+        [WHOLE] * (3 * count),
+        jax.ShapeDtypeStruct((2, rows * count, units), BF16),
+        WHOLE,
+        deps,
         name="hidden_grads",
+    )
+
+
+def hand_over(arrays, deps):
+    def kernel(*refs):
+        del refs
+
+    return call(
+        kernel,
+        arrays,
+        [ANYWHERE] * len(arrays),
+        [jax.ShapeDtypeStruct(a.shape, a.dtype) for a in arrays],
+        [ANYWHERE] * len(arrays),
+        deps,
+        aliases={i: i for i in range(len(arrays))},
+        name="hand_over",
     )
 
 
@@ -227,7 +240,9 @@
     return jnp.concatenate([mine[at], other[at]], axis=0)
 
 
-def down_grad(hidden, hidden_other, out_all, down=None, span=(0, 0), deps=()):
+def down_grad(
+    hidden, hidden_other, out_all, down=None, span=(0, 0), coming=(), coming_span=(0, 0), head=0, deps=()
+):
     half, units = hidden.shape
     tokens, width = out_all.shape
     piece = divisor(units, 640)
@@ -241,8 +256,14 @@
         operands.append(down)
         specs.append(REMAIN)
         shapes += [jax.ShapeDtypeStruct((half, taken), BF16)] * 2
-        run = divisor(taken, 1280)
-        scratch += [pltpu.VMEM((taken, width), BF16), pltpu.SemaphoreType.DMA((taken // run,))]
+        run = divisor(taken, 1536)
+        operands += coming
+        specs += [REMAIN] * len(coming)
+        shapes += [pltpu.VMEM((head, coming_span[1]), BF16)] * len(coming)
+        scratch += [
+            pltpu.VMEM((taken, width), BF16),
+            pltpu.SemaphoreType.DMA((taken // run + len(coming),)),
+        ]
 
     def kernel(*refs):
         a, b, g = refs[:3]
@@ -252,6 +273,12 @@
         token[...] = jnp.zeros(token.shape, F32)
         if taken:
             start_copies(refs[3], lo, taken // run, run, refs[-2], refs[-1])
+            loads = []
+            for i in range(len(coming)):
+                source = refs[4 + i].at[pl.ds(0, head), pl.ds(*coming_span)]
+                sem = refs[-1].at[taken // run + i]
+                loads.append(pltpu.make_async_copy(source, refs[given + 4 + i], sem))
+                loads[-1].start()
 
         def store(i):
             slot = lax.rem(i, slots)
@@ -275,6 +302,8 @@
             dots_of(
                 g, refs[3], lo, taken // run, run, refs[-2], refs[-1], refs[given + 2], refs[given + 3]
             )
+            for load in loads:
+                load.wait()
         for i in range(count - slots, count):
             store(i).wait()
 
@@ -290,16 +319,20 @@
     )
 
 
-def input_grads(mine, other, gate_weight, up_weight, before, offsets, span, rows, groups, deps=()):
+def input_grads(
+    mine, other, gate_weight, up_weight, before, offsets, span, rows, groups, heads=(), deps=()
+):
     _, half, units = mine.shape
     tokens = 2 * half
     width = gate_weight.shape[0]
     piece = divisor(width, 512)
     pieces = width // piece
-    slots = min(4, pieces)
     cols = slice(span[0], span[0] + units)
-    operands = [offsets, mine, other, gate_weight, up_weight] + ([] if before is None else [before])
-    specs = [SCALARS, WHOLE, WHOLE, REMAIN, REMAIN] + ([] if before is None else [WHOLE])
+    skip = heads[0].shape[0] // piece if heads else 0
+    operands = [offsets, mine, other, gate_weight, up_weight, *heads]
+    operands += [] if before is None else [before]
+    specs = [SCALARS, WHOLE, WHOLE, REMAIN, REMAIN] + [RESIDENT] * len(heads)
+    specs += [] if before is None else [WHOLE]
     if groups is None:
         shapes = [jax.ShapeDtypeStruct((tokens, width), F32)]
     else:
@@ -310,28 +343,23 @@
         outs = refs[len(operands) : len(operands) + len(shapes)]
         sums, ready, sems = refs[-3:]
         copies = []
-        for j in range(pieces):
+        for j in range(skip, pieces):
             at = slice(j * piece, (j + 1) * piece)
             for i, w in enumerate((gw, uw)):
                 copies.append(
-                    pltpu.make_async_copy(
-                        w.at[at, cols], ready.at[i, j % slots], sems.at[i, j % slots]
-                    )
+                    pltpu.make_async_copy(w.at[at, cols], ready.at[i, j - skip], sems.at[i, j - skip])
                 )
-        for copy in copies[: 2 * slots]:
-            copy.start()
+                copies[-1].start()
         for j in range(pieces):
             at = slice(j * piece, (j + 1) * piece)
-            total = 0.0 if before is None else refs[5][:, at]
+            total = 0.0 if before is None else refs[len(operands) - 1][:, at]
+            if j >= skip:
+                for i in range(2):
+                    copies[2 * (j - skip) + i].wait()
             for i in range(2):
-                copies[2 * j + i].wait()
-            for i in range(2):
-                total = total + lax.dot_general(
-                    both(a, b, i), ready[i, j % slots], NT, preferred_element_type=F32
-                )
+                w = refs[5 + i][at, :] if j < skip else ready[i, j - skip]
+                total = total + lax.dot_general(both(a, b, i), w, NT, preferred_element_type=F32)
             sums[:, at] = total
-            for copy in copies[2 * (j + slots) : 2 * (j + slots + 1)]:
-                copy.start()
         if groups is None:
             outs[0][...] = sums[...]
         for out, group in zip(outs, groups or ()):
@@ -348,8 +376,8 @@
         deps,
         scratch=[
             pltpu.VMEM((tokens, width), F32),
-            pltpu.VMEM((2, slots, piece, units), BF16),
-            pltpu.SemaphoreType.DMA((2, slots)),
+            pltpu.VMEM((2, pieces - skip, piece, units), BF16),
+            pltpu.SemaphoreType.DMA((2, pieces - skip)),
         ],
         name="input_grads",
     )
@@ -439,7 +467,7 @@
     own_tokens = gate.shape[0]
     col_tokens = grad_out.shape[0]
     units = down_weight.shape[0]
-    first = units // 5 * 3 if units % 640 == 0 else units
+    first = units // 30 * 19 if units % 3840 == 0 else units
     spans = [(0, first)] + ([(first, units - first)] if first < units else [])
     direct = nc == 8 and nr * own_tokens == nc * col_tokens and own_tokens % col_tokens == 0
 
@@ -507,25 +535,38 @@
         in_blocks = [lax.all_gather(inputs, "col", axis=0, tiled=True)]
     span = spans[1] if len(spans) > 1 else (0, 0)
     grad_down, token, *parts = down_grad(
-        hidden, hidden_other, out_all, down_weight, span, deps=[sums[0][0], own]
-    )
-
-    mine, *parts = hidden_grads(sums[0], gates, ups, spans[0], parts, [token, *in_blocks])
+        hidden,
+        hidden_other,
+        out_all,
+        down_weight,
+        span,
+        [gate_weight, up_weight],
+        spans[0],
+        divisor(gate_weight.shape[0], 512),
+        deps=[sums[0][0], own],
+    )
+    parts, heads = parts[:2], parts[2:]
+
+    first_deps = [token, *sums[0][1:], *in_blocks, *heads]
+    if len(spans) > 1:
+        sums.append(exchanged(*hand_over(parts, first_deps)))
+        first_deps = sums[1][:1]
+    mine = hidden_grads(sums[0], gates, ups, spans[0], first_deps)
     grads = [(mine, swap_core(mine))]
     groups = [(7, 5), (3, 2), (6, 4, 1), (0,)] if direct else [range(nr)]
     if direct:
         in_blocks.append(swap_col(in_blocks[2], 2))
     total = None
     if len(spans) > 1:
-        sums.append(exchanged(*parts))
         (total,) = input_grads(
-            *grads[0], gate_weight, up_weight, None, offsets, spans[0], rows, None, sums[1][:1]
+            *grads[0], gate_weight, up_weight, None, offsets, spans[0], rows, None,
+            heads, sums[1][:1],
         )
-        (mine,) = hidden_grads(sums[1], gates, ups, spans[1], deps=[total, *in_blocks])
+        mine = hidden_grads(sums[1], gates, ups, spans[1], deps=[total, *in_blocks])
         grads.append((mine, swap_core(mine)))
     in_all = assemble(in_blocks, offsets if direct else in_order, deps=[mine])
     blocks = input_grads(
-        *grads[-1], gate_weight, up_weight, total, offsets, spans[-1], rows, groups, [in_all]
+        *grads[-1], gate_weight, up_weight, total, offsets, spans[-1], rows, groups, (), [in_all]
     )
 
     def weight_part(before, i, span, deps):
@@ -534,7 +575,7 @@
         )
         return weights, token
 
-    cut = divisor(first, first // 2)
+    cut = (first // 256 - 1) * 128 if first % 128 == 0 and first >= 512 else first
     parts = [(0, (0, cut)), (0, (cut, first - cut))]
     parts = parts[: 1 if cut == first else 2]
     if len(spans) > 1:

time: 95.7 us -> 95 us (level)
  waiting for transfers between devices: 14.7 us -> 12.7 us
    ppermute x16, waiting for transfers between devices: 9.77 us -> 7.96 us  [swap_col(): return lax.ppermute(value, 'col', [(c, c ^ mask) for c in range(nc)])]
    pallas_call x14 -> x15, Pallas kernels: 47 us -> 47.7 us  [call(): pl.pallas_call(body, out_shape=out_shape, in_specs=list(in_specs) + [ANYW...]
where the time goes in v5:
time: 95 us; the launch traced here: 94.9 us
  Pallas kernels  47.7 us (50%)
  starting transfers between devices  32.5 us (34%)
  waiting for transfers between devices  12.7 us (13%)
  other arithmetic  0.96 us (1%)
    pallas_call x15, Pallas kernels, call(): pl.pallas_call(body, out_shape=out_shape, in_specs=list(in_specs) + [ANYW...  47.7 us
    ppermute x16, starting transfers between devices, swap_col(): return lax.ppermute(value, 'col', [(c, c ^ mask) for c in range(nc)])  25.5 us
    ppermute x16, waiting for transfers between devices, swap_col(): return lax.ppermute(value, 'col', [(c, c ^ mask) for c in range(nc)])  7.96 us
    ppermute x4, starting transfers between devices, from_x(): lax.ppermute(value, 'row', [((r + offset * CORES) % nr, r) for r in range...  6 us
    ppermute x5, waiting for transfers between devices, swap_core(): return lax.ppermute(value, 'row', [(r, r ^ 1) for r in range(nr)])  4.28 us
  transfers between devices with their start and end apart: 25, of which 11 were waited for; matrix products, arithmetic and copies ran while one was open for 0% of the time, Pallas kernels for 38%

profile of v5, /device:TPU:0, one launch (start us, length us, event | category | flops | bytes accessed | tf_op | source)
XLA Modules:
  0.0 94.9 jit_solution(10162355187551258900)
XLA Ops:
  0.6 3.0 %collective-permute-start.2 = (bf16[64,3840]{1,0:T(8,128)(2,1)}, bf16[64,3840]{1,0:T(8,128)(2,1)S(1)}, u32[]{:S(2)}, u32[]{:S(2)}) collective-permute-start(bf16[64,3840]{1,0:T(8,128)(2,1)} %refs_2_.1), channel_id=1, source_target_pairs={{16,0},{24,8},{0,16},{8,24},{17,1},{25,9},{1,17},{9,25},{18,2},{26... | collective-permute-start | bytes 1474568 | tf_op jit(solution)/shard_map/ppermute | solution.py:478
  3.7 2.0 %collective-permute-start.9 = (bf16[32,2048]{1,0:T(8,128)(2,1)}, bf16[32,2048]{1,0:T(8,128)(2,1)S(1)}, u32[]{:S(2)}, u32[]{:S(2)}) collective-permute-start(bf16[32,2048]{1,0:T(8,128)(2,1)} %param.7), channel_id=1, source_target_pairs={{0,1},{1,0},{2,3},{3,2},{4,5},{5,4},{6,7},{7,6},{8,9},{9,8},{10,11... | collective-permute-start | bytes 393224 | tf_op jit(solution)/shard_map/ppermute | solution.py:481
  5.7 2.6 %collective-permute-start = (bf16[32,2048]{1,0:T(8,128)(2,1)}, bf16[32,2048]{1,0:T(8,128)(2,1)S(1)}, u32[]{:S(2)}, u32[]{:S(2)}) collective-permute-start(bf16[32,2048]{1,0:T(8,128)(2,1)} %refs_1_.1), channel_id=1, source_target_pairs={{0,4},{1,5},{2,6},{3,7},{4,0},{5,1},{6,2},{7,3},{8,12},{9,13},{10,... | collective-permute-start | bytes 393224 | tf_op jit(solution)/shard_map/ppermute | solution.py:481
  8.3 1.6 %collective-permute-start.5 = (bf16[32,2048]{1,0:T(8,128)(2,1)}, bf16[32,2048]{1,0:T(8,128)(2,1)S(1)}, u32[]{:S(2)}, u32[]{:S(2)}) collective-permute-start(bf16[32,2048]{1,0:T(8,128)(2,1)} %refs_1_.1), channel_id=1, source_target_pairs={{0,2},{1,3},{2,0},{3,1},{4,6},{5,7},{6,4},{7,5},{8,10},{9,11},{10,... | collective-permute-start | bytes 393224 | tf_op jit(solution)/shard_map/ppermute | solution.py:481
  10.9 3.2 %collective-permute-done.refs_5_ = bf16[32,2048]{1,0:T(8,128)(2,1)S(1)} collective-permute-done((bf16[32,2048]{1,0:T(8,128)(2,1)}, bf16[32,2048]{1,0:T(8,128)(2,1)S(1)}, u32[]{:S(2)}, u32[]{:S(2)}) %collective-permute-start) | collective-permute-done | bytes 131104 | tf_op jit(solution)/shard_map/ppermute | solution.py:481
  16.6 2.8 %collective-permute-done.1.refs_4_.refs_7_ = bf16[32,2048]{1,0:T(8,128)(2,1)S(1)} collective-permute-done((bf16[32,2048]{1,0:T(8,128)(2,1)S(1)}, bf16[32,2048]{1,0:T(8,128)(2,1)S(1)}, u32[]{:S(2)}, u32[]{:S(2)}) %collective-permute-start.1) | collective-permute-done | bytes 131104 | tf_op jit(solution)/shard_map/ppermute | solution.py:481
  19.4 1.5 %collective-permute-start.8 = (bf16[32,2048]{1,0:T(8,128)(2,1)S(1)}, bf16[32,2048]{1,0:T(8,128)(2,1)S(1)}, u32[]{:S(2)}, u32[]{:S(2)}) collective-permute-start(bf16[32,2048]{1,0:T(8,128)(2,1)S(1)} %collective-permute-done.1.refs_4_.refs_7_), channel_id=1, source_target_pairs={{0,1},{1,0},{2,3},{3,2},{4,5},{5,4},{6,7},{7,6},{8,9},{9,8},{10,11... | collective-permute-start | bytes 393224 | tf_op jit(solution)/shard_map/ppermute | solution.py:481
  21.0 4.1 %fetch.1 = (bf16[2432,2048]{1,0:T(8,128)(2,1)S(1)}, bf16[32,2048]{1,0:T(8,128)(2,1)S(1)}, bf16[64,3840]{1,0:T(8,128)(2,1)S(1)}, bf16[64,3840]{1,0:T(8,128)(2,1)S(1)}) custom-call(bf16[3840,2048]{1,0:T(8,128)(2,1)} %refs_3_.5, bf16[32,2048]{1,0:T(8,128)(2,1)} %refs_1_.1, bf16[64,3840]{1,0:T(8,128)(2,1)} %refs_2_.1, bf16[64,3840]{1,0:T(8,128)(2,1)} %refs_3_.4, ...), custom_call_target="tpu_custom_call" | custom-call | tf_op jit(solution)/shard_map/fetch/pallas_call | solution.py:46
  25.6 3.5 %first_partial.1 = (bf16[128,2432]{1,0:T(8,128)(2,1)S(1)}, bf16[128,2432]{1,0:T(8,128)(2,1)S(1)}, bf16[256,2048]{1,0:T(8,128)(2,1)S(1)}) custom-call(s32[8]{0:T(128)S(1)} %stack.35.refs_0_, bf16[32,2048]{1,0:T(8,128)(2,1)S(1)} %get-tuple-element.37.refs_1_, bf16[32,2048]{1,0:T(8,128)(2,1)S(1)} %collective-permute-done.4.refs_2_, ...), custom_call_target="tpu_custom_call" | custom-call | tf_op jit(solution)/shard_map/first_partial/pallas_call | solution.py:46
  31.3 1.8 %collective-permute-start.12 = (bf16[128,2432]{1,0:T(8,128)(2,1)S(1)}, bf16[128,2432]{1,0:T(8,128)(2,1)S(1)}, u32[]{:S(2)}, u32[]{:S(2)}) collective-permute-start(bf16[128,2432]{1,0:T(8,128)(2,1)S(1)} %add_convert_fusion.refs_6_.refs_0_), channel_id=1, source_target_pairs={{16,0},{24,8},{0,16},{8,24},{17,1},{25,9},{1,17},{9,25},{18,2},{26... | collective-permute-start | bytes 1867784 | tf_op jit(solution)/shard_map/ppermute | solution.py:478
  33.2 2.7 %collective-permute-start.14 = (bf16[64,2048]{1,0:T(8,128)(2,1)S(1)}, bf16[64,2048]{1,0:T(8,128)(2,1)S(1)}, u32[]{:S(2)}, u32[]{:S(2)}) collective-permute-start(bf16[64,2048]{1,0:T(8,128)(2,1)S(1)} %constant_dynamic-update-slice_fusion.refs_7_.refs_4_.refs_1_), channel_id=1, source_target_pairs={{0,4},{1,5},{2,6},{3,7},{4,0},{5,1},{6,2},{7,3},{8,12},{9,13},{10,... | collective-permute-start | bytes 786440 | tf_op jit(solution)/shard_map/ppermute | solution.py:481
  35.8 1.6 %collective-permute-start.13 = (bf16[64,2048]{1,0:T(8,128)(2,1)S(1)}, bf16[64,2048]{1,0:T(8,128)(2,1)S(1)}, u32[]{:S(2)}, u32[]{:S(2)}) collective-permute-start(bf16[64,2048]{1,0:T(8,128)(2,1)S(1)} %constant_dynamic-update-slice_fusion.refs_7_.refs_4_.refs_1_), channel_id=1, source_target_pairs={{0,2},{1,3},{2,0},{3,1},{4,6},{5,7},{6,4},{7,5},{8,10},{9,11},{10,... | collective-permute-start | bytes 786440 | tf_op jit(solution)/shard_map/ppermute | solution.py:481
  37.4 9.4 %down_grad.1 = (bf16[3840,2048]{1,0:T(8,128)(2,1)}, f32[8,128]{1,0:T(8,128)S(1)}, bf16[128,1408]{1,0:T(8,128)(2,1)S(1)}, bf16[128,1408]{1,0:T(8,128)(2,1)S(1)}, ...) custom-call(bf16[128,3840]{1,0:T(8,128)(2,1)S(1)} %activations.1.refs_0_, ...), custom_call_target="tpu_custom_call" | custom-call | tf_op jit(solution)/shard_map/down_grad/pallas_call | solution.py:46
  48.1 1.7 %collective-permute-done.15 = bf16[128,1408]{1,0:T(8,128)(2,1)S(1)} collective-permute-done((bf16[128,1408]{1,0:T(8,128)(2,1)S(1)}, bf16[128,1408]{1,0:T(8,128)(2,1)S(1)}, u32[]{:S(2)}, u32[]{:S(2)}) %collective-permute-start.15) | collective-permute-done | bytes 360480 | tf_op jit(solution)/shard_map/ppermute | solution.py:475
  51.9 1.6 %collective-permute-start.18 = (bf16[64,2048]{1,0:T(8,128)(2,1)S(1)}, bf16[64,2048]{1,0:T(8,128)(2,1)S(1)}, u32[]{:S(2)}, u32[]{:S(2)}) collective-permute-start(bf16[64,2048]{1,0:T(8,128)(2,1)S(1)} %collective-permute-done.14.refs_6_.refs_9_.refs_3_), channel_id=1, source_target_pairs={{0,2},{1,3},{2,0},{3,1},{4,6},{5,7},{6,4},{7,5},{8,10},{9,11},{10,... | collective-permute-start | bytes 786440 | tf_op jit(solution)/shard_map/ppermute | solution.py:481
  53.6 7.9 %input_grads.2.refs_6_.refs_5_ = f32[256,2048]{1,0:T(8,128)S(1)} custom-call(s32[8]{0:T(128)S(1)} %stack.35.refs_0_, bf16[2,128,2432]{2,1,0:T(8,128)(2,1)S(1)} %hidden_grads.2.refs_1_.refs_0_, bf16[2,128,2432]{2,1,0:T(8,128)(2,1)S(1)} %collective-permute-done.17.refs_2_.refs_1_, bf16[2048,3840]{1,0:T(8,128)(2,1)} %refs_3_.7, bf16[2048,3840]{1,0:T(8,128)(2,1)} %refs_4_.5, ...), custom_call_target="tpu_custom_call" | custom-call | tf_op jit(solution)/shard_map/input_grads/pallas_call | solution.py:46
  64.2 6.7 %input_grads.3 = (bf16[64,2048]{1,0:T(8,128)(2,1)S(1)}, bf16[64,2048]{1,0:T(8,128)(2,1)S(1)}, bf16[96,2048]{1,0:T(8,128)(2,1)S(1)}, bf16[32,2048]{1,0:T(8,128)(2,1)S(1)}) custom-call(s32[8]{0:T(128)S(1)} %stack.35.refs_0_, bf16[2,128,1408]{2,1,0:T(8,128)(2,1)S(1)} %hidden_grads.3.refs_5_.refs_1_.refs_0_, ...), custom_call_target="tpu_custom_call" | custom-call | tf_op jit(solution)/shard_map/input_grads/pallas_call | solution.py:46
  70.9 1.6 %collective-permute-start.21 = (bf16[64,2048]{1,0:T(8,128)(2,1)S(1)}, bf16[64,2048]{1,0:T(8,128)(2,1)S(1)}, u32[]{:S(2)}, u32[]{:S(2)}) collective-permute-start(bf16[64,2048]{1,0:T(8,128)(2,1)S(1)} %get-tuple-element.52), channel_id=1, source_target_pairs={{0,1},{1,0},{2,3},{3,2},{4,5},{5,4},{6,7},{7,6},{8,9},{9,8},{10,11... | collective-permute-start | bytes 786440 | tf_op jit(solution)/shard_map/ppermute | solution.py:481
  73.9 4.8 %weight_grads.3 = (bf16[2048,3840]{1,0:T(8,128)(2,1)}, bf16[2048,3840]{1,0:T(8,128)(2,1)}, f32[8,128]{1,0:T(8,128)S(1)}) custom-call(bf16[2,128,1408]{2,1,0:T(8,128)(2,1)S(1)} %hidden_grads.3.refs_5_.refs_1_.refs_0_, bf16[2,128,1408]{2,1,0:T(8,128)(2,1)S(1)} %collective-permute-done.19.refs_2_.refs_1_, bf16[256,2048]{1,0:T(8,128)(2,1)S(1)} %assemble.1.refs_6_.refs_2_), custom_call_target="tpu_custom_call" | custom-call | tf_op jit(solution)/shard_map/weight_grads/pallas_call | solution.py:46
  79.3 1.5 %collective-permute-start.22 = (bf16[32,2048]{1,0:T(8,128)(2,1)S(1)}, bf16[32,2048]{1,0:T(8,128)(2,1)S(1)}, u32[]{:S(2)}, u32[]{:S(2)}) collective-permute-start(bf16[32,2048]{1,0:T(8,128)(2,1)S(1)} %get-tuple-element.55.refs_5_), channel_id=1, source_target_pairs={{0,2},{1,3},{2,0},{3,1},{4,6},{5,7},{6,4},{7,5},{8,10},{9,11},{10,... | collective-permute-start | bytes 393224 | tf_op jit(solution)/shard_map/ppermute | solution.py:481
  80.9 3.7 %weight_grads.4 = (bf16[2048,3840]{1,0:T(8,128)(2,1)}, bf16[2048,3840]{1,0:T(8,128)(2,1)}, f32[8,128]{1,0:T(8,128)S(1)}) custom-call(bf16[2,128,2432]{2,1,0:T(8,128)(2,1)S(1)} %hidden_grads.2.refs_1_.refs_0_, bf16[2,128,2432]{2,1,0:T(8,128)(2,1)S(1)} %collective-permute-done.17.refs_2_.refs_1_, ...), custom_call_target="tpu_custom_call", output_to_operand_aliasing={{0}: (3, {}), {1}: (4, {})} | custom-call | tf_op jit(solution)/shard_map/weight_grads/pallas_call | solution.py:46
  84.7 1.6 %collective-permute-start.23 = (bf16[32,2048]{1,0:T(8,128)(2,1)S(1)}, bf16[32,2048]{1,0:T(8,128)(2,1)S(1)}, u32[]{:S(2)}, u32[]{:S(2)}) collective-permute-start(bf16[32,2048]{1,0:T(8,128)(2,1)S(1)} %get-tuple-element.59), channel_id=1, source_target_pairs={{0,1},{1,0},{2,3},{3,2},{4,5},{5,4},{6,7},{7,6},{8,9},{9,8},{10,11... | collective-permute-start | bytes 393224 | tf_op jit(solution)/shard_map/ppermute | solution.py:481
  86.3 2.4 %collective-permute-start.24 = (bf16[32,2048]{1,0:T(8,128)(2,1)S(1)}, bf16[32,2048]{1,0:T(8,128)(2,1)S(1)}, u32[]{:S(2)}, u32[]{:S(2)}) collective-permute-start(bf16[32,2048]{1,0:T(8,128)(2,1)S(1)} %get-tuple-element.60.refs_5_), channel_id=1, source_target_pairs={{0,4},{1,5},{2,6},{3,7},{4,0},{5,1},{6,2},{7,3},{8,12},{9,13},{10,... | collective-permute-start | bytes 393224 | tf_op jit(solution)/shard_map/ppermute | solution.py:481
  88.7 5.4 %weight_grads.5 = (bf16[2048,3840]{1,0:T(8,128)(2,1)}, bf16[2048,3840]{1,0:T(8,128)(2,1)}, f32[8,128]{1,0:T(8,128)}) custom-call(bf16[2,128,2432]{2,1,0:T(8,128)(2,1)S(1)} %hidden_grads.2.refs_1_.refs_0_, bf16[2,128,2432]{2,1,0:T(8,128)(2,1)S(1)} %collective-permute-done.17.refs_2_.refs_1_, ...), custom_call_target="tpu_custom_call", output_to_operand_aliasing={{0}: (3, {}), {1}: (4, {})} | custom-call | tf_op jit(solution)/shard_map/weight_grads/pallas_call | solution.py:46
  (49 shorter events, 15.5 us)
Async XLA Ops:
  0.6 24.5 %collective-permute-start.2 = (bf16[64,3840]{1,0:T(8,128)(2,1)}, bf16[64,3840]{1,0:T(8,128)(2,1)S(1)}, u32[]{:S(2)}, u32[]{:S(2)}) collective-permute-start(bf16[64,3840]{1,0:T(8,128)(2,1)} %refs_2_.1), channel_id=1, source_target_pairs={{16,0},{24,8},{0,16},{8,24},{17,1},{25,9},{1,17},{9,25},{18,2},{26... | collective-permute-start | bytes 1474568 | tf_op jit(solution)/shard_map/ppermute | solution.py:478
  3.6 22.0 %collective-permute-start.3 = (bf16[64,3840]{1,0:T(8,128)(2,1)}, bf16[64,3840]{1,0:T(8,128)(2,1)S(1)}, u32[]{:S(2)}, u32[]{:S(2)}) collective-permute-start(bf16[64,3840]{1,0:T(8,128)(2,1)} %refs_3_.4), channel_id=1, source_target_pairs={{16,0},{24,8},{0,16},{8,24},{17,1},{25,9},{1,17},{9,25},{18,2},{26... | collective-permute-start | bytes 1474568 | tf_op jit(solution)/shard_map/ppermute | solution.py:478
  3.7 6.1 %collective-permute-start.9 = (bf16[32,2048]{1,0:T(8,128)(2,1)}, bf16[32,2048]{1,0:T(8,128)(2,1)S(1)}, u32[]{:S(2)}, u32[]{:S(2)}) collective-permute-start(bf16[32,2048]{1,0:T(8,128)(2,1)} %param.7), channel_id=1, source_target_pairs={{0,1},{1,0},{2,3},{3,2},{4,5},{5,4},{6,7},{7,6},{8,9},{9,8},{10,11... | collective-permute-start | bytes 393224 | tf_op jit(solution)/shard_map/ppermute | solution.py:481
  5.7 8.4 %collective-permute-start = (bf16[32,2048]{1,0:T(8,128)(2,1)}, bf16[32,2048]{1,0:T(8,128)(2,1)S(1)}, u32[]{:S(2)}, u32[]{:S(2)}) collective-permute-start(bf16[32,2048]{1,0:T(8,128)(2,1)} %refs_1_.1), channel_id=1, source_target_pairs={{0,4},{1,5},{2,6},{3,7},{4,0},{5,1},{6,2},{7,3},{8,12},{9,13},{10,... | collective-permute-start | bytes 393224 | tf_op jit(solution)/shard_map/ppermute | solution.py:481
  8.3 6.5 %collective-permute-start.5 = (bf16[32,2048]{1,0:T(8,128)(2,1)}, bf16[32,2048]{1,0:T(8,128)(2,1)S(1)}, u32[]{:S(2)}, u32[]{:S(2)}) collective-permute-start(bf16[32,2048]{1,0:T(8,128)(2,1)} %refs_1_.1), channel_id=1, source_target_pairs={{0,2},{1,3},{2,0},{3,1},{4,6},{5,7},{6,4},{7,5},{8,10},{9,11},{10,... | collective-permute-start | bytes 393224 | tf_op jit(solution)/shard_map/ppermute | solution.py:481
  9.9 5.4 %collective-permute-start.4 = (bf16[32,2048]{1,0:T(8,128)(2,1)}, bf16[32,2048]{1,0:T(8,128)(2,1)S(1)}, u32[]{:S(2)}, u32[]{:S(2)}) collective-permute-start(bf16[32,2048]{1,0:T(8,128)(2,1)} %refs_1_.1), channel_id=1, source_target_pairs={{0,1},{1,0},{2,3},{3,2},{4,5},{5,4},{6,7},{7,6},{8,9},{9,8},{10,11... | collective-permute-start | bytes 393224 | tf_op jit(solution)/shard_map/ppermute | solution.py:481
  14.1 5.3 %collective-permute-start.1 = (bf16[32,2048]{1,0:T(8,128)(2,1)S(1)}, bf16[32,2048]{1,0:T(8,128)(2,1)S(1)}, u32[]{:S(2)}, u32[]{:S(2)}) collective-permute-start(bf16[32,2048]{1,0:T(8,128)(2,1)S(1)} %collective-permute-done.refs_5_), channel_id=1, source_target_pairs={{0,2},{1,3},{2,0},{3,1},{4,6},{5,7},{6,4},{7,5},{8,10},{9,11},{10,... | collective-permute-start | bytes 393224 | tf_op jit(solution)/shard_map/ppermute | solution.py:481
  14.8 10.3 %collective-permute-start.7 = (bf16[32,2048]{1,0:T(8,128)(2,1)S(1)}, bf16[32,2048]{1,0:T(8,128)(2,1)S(1)}, u32[]{:S(2)}, u32[]{:S(2)}) collective-permute-start(bf16[32,2048]{1,0:T(8,128)(2,1)S(1)} %collective-permute-done.refs_5_), channel_id=1, source_target_pairs={{0,1},{1,0},{2,3},{3,2},{4,5},{5,4},{6,7},{7,6},{8,9},{9,8},{10,11... | collective-permute-start | bytes 393224 | tf_op jit(solution)/shard_map/ppermute | solution.py:481
  15.3 9.8 %collective-permute-start.6 = (bf16[32,2048]{1,0:T(8,128)(2,1)S(1)}, bf16[32,2048]{1,0:T(8,128)(2,1)S(1)}, u32[]{:S(2)}, u32[]{:S(2)}) collective-permute-start(bf16[32,2048]{1,0:T(8,128)(2,1)S(1)} %collective-permute-done.4.refs_2_), channel_id=1, source_target_pairs={{0,2},{1,3},{2,0},{3,1},{4,6},{5,7},{6,4},{7,5},{8,10},{9,11},{10,... | collective-permute-start | bytes 393224 | tf_op jit(solution)/shard_map/ppermute | solution.py:481
  19.4 5.8 %collective-permute-start.8 = (bf16[32,2048]{1,0:T(8,128)(2,1)S(1)}, bf16[32,2048]{1,0:T(8,128)(2,1)S(1)}, u32[]{:S(2)}, u32[]{:S(2)}) collective-permute-start(bf16[32,2048]{1,0:T(8,128)(2,1)S(1)} %collective-permute-done.1.refs_4_.refs_7_), channel_id=1, source_target_pairs={{0,1},{1,0},{2,3},{3,2},{4,5},{5,4},{6,7},{7,6},{8,9},{9,8},{10,11... | collective-permute-start | bytes 393224 | tf_op jit(solution)/shard_map/ppermute | solution.py:481
  29.1 2.1 %collective-permute-start.11 = (bf16[128,2432]{1,0:T(8,128)(2,1)S(1)}, bf16[128,2432]{1,0:T(8,128)(2,1)S(1)}, u32[]{:S(2)}, u32[]{:S(2)}) collective-permute-start(bf16[128,2432]{1,0:T(8,128)(2,1)S(1)} %get-tuple-element.41), channel_id=1, source_target_pairs={{0,8},{8,0},{16,24},{24,16},{1,9},{9,1},{17,25},{25,17},{2,10},{10... | collective-permute-start | bytes 1867784 | tf_op jit(solution)/shard_map/ppermute | solution.py:475
  29.6 7.8 %collective-permute-start.10 = (bf16[128,3840]{1,0:T(8,128)(2,1)S(1)}, bf16[128,3840]{1,0:T(8,128)(2,1)S(1)}, u32[]{:S(2)}, u32[]{:S(2)}) collective-permute-start(bf16[128,3840]{1,0:T(8,128)(2,1)S(1)} %activations.1.refs_0_), channel_id=1, source_target_pairs={{0,8},{8,0},{16,24},{24,16},{1,9},{9,1},{17,25},{25,17},{2,10},{10... | collective-permute-start | bytes 2949128 | tf_op jit(solution)/shard_map/ppermute | solution.py:475
  31.3 16.8 %collective-permute-start.12 = (bf16[128,2432]{1,0:T(8,128)(2,1)S(1)}, bf16[128,2432]{1,0:T(8,128)(2,1)S(1)}, u32[]{:S(2)}, u32[]{:S(2)}) collective-permute-start(bf16[128,2432]{1,0:T(8,128)(2,1)S(1)} %add_convert_fusion.refs_6_.refs_0_), channel_id=1, source_target_pairs={{16,0},{24,8},{0,16},{8,24},{17,1},{25,9},{1,17},{9,25},{18,2},{26... | collective-permute-start | bytes 1867784 | tf_op jit(solution)/shard_map/ppermute | solution.py:478
  33.2 14.8 %collective-permute-start.14 = (bf16[64,2048]{1,0:T(8,128)(2,1)S(1)}, bf16[64,2048]{1,0:T(8,128)(2,1)S(1)}, u32[]{:S(2)}, u32[]{:S(2)}) collective-permute-start(bf16[64,2048]{1,0:T(8,128)(2,1)S(1)} %constant_dynamic-update-slice_fusion.refs_7_.refs_4_.refs_1_), channel_id=1, source_target_pairs={{0,4},{1,5},{2,6},{3,7},{4,0},{5,1},{6,2},{7,3},{8,12},{9,13},{10,... | collective-permute-start | bytes 786440 | tf_op jit(solution)/shard_map/ppermute | solution.py:481
  35.8 12.3 %collective-permute-start.13 = (bf16[64,2048]{1,0:T(8,128)(2,1)S(1)}, bf16[64,2048]{1,0:T(8,128)(2,1)S(1)}, u32[]{:S(2)}, u32[]{:S(2)}) collective-permute-start(bf16[64,2048]{1,0:T(8,128)(2,1)S(1)} %constant_dynamic-update-slice_fusion.refs_7_.refs_4_.refs_1_), channel_id=1, source_target_pairs={{0,2},{1,3},{2,0},{3,1},{4,6},{5,7},{6,4},{7,5},{8,10},{9,11},{10,... | collective-permute-start | bytes 786440 | tf_op jit(solution)/shard_map/ppermute | solution.py:481
  50.6 3.0 %collective-permute-start.17 = (bf16[2,128,2432]{2,1,0:T(8,128)(2,1)S(1)}, bf16[2,128,2432]{2,1,0:T(8,128)(2,1)S(1)}, u32[]{:S(2)}, u32[]{:S(2)}) collective-permute-start(bf16[2,128,2432]{2,1,0:T(8,128)(2,1)S(1)} %hidden_grads.2.refs_1_.refs_0_), channel_id=1, source_target_pairs={{0,8},{8,0},{16,24},{24,16},{1,9},{9,1},{17,25},{25,17},{2,10},{10... | collective-permute-start | bytes 3735560 | tf_op jit(solution)/shard_map/ppermute | solution.py:475
  50.8 10.7 %collective-permute-start.16 = (bf16[128,1408]{1,0:T(8,128)(2,1)S(1)}, bf16[128,1408]{1,0:T(8,128)(2,1)S(1)}, u32[]{:S(2)}, u32[]{:S(2)}) collective-permute-start(bf16[128,1408]{1,0:T(8,128)(2,1)S(1)} %add_convert_fusion.1.refs_6_.refs_7_.refs_0_), channel_id=1, source_target_pairs={{16,0},{24,8},{0,16},{8,24},{17,1},{25,9},{1,17},{9,25},{18,2},{26... | collective-permute-start | bytes 1081352 | tf_op jit(solution)/shard_map/ppermute | solution.py:478
  51.9 9.6 %collective-permute-start.18 = (bf16[64,2048]{1,0:T(8,128)(2,1)S(1)}, bf16[64,2048]{1,0:T(8,128)(2,1)S(1)}, u32[]{:S(2)}, u32[]{:S(2)}) collective-permute-start(bf16[64,2048]{1,0:T(8,128)(2,1)S(1)} %collective-permute-done.14.refs_6_.refs_9_.refs_3_), channel_id=1, source_target_pairs={{0,2},{1,3},{2,0},{3,1},{4,6},{5,7},{6,4},{7,5},{8,10},{9,11},{10,... | collective-permute-start | bytes 786440 | tf_op jit(solution)/shard_map/ppermute | solution.py:481
  61.9 2.3 %collective-permute-start.19 = (bf16[2,128,1408]{2,1,0:T(8,128)(2,1)S(1)}, bf16[2,128,1408]{2,1,0:T(8,128)(2,1)S(1)}, u32[]{:S(2)}, u32[]{:S(2)}) collective-permute-start(bf16[2,128,1408]{2,1,0:T(8,128)(2,1)S(1)} %hidden_grads.3.refs_5_.refs_1_.refs_0_), channel_id=1, source_target_pairs={{0,8},{8,0},{16,24},{24,16},{1,9},{9,1},{17,25},{25,17},{2,10},{10... | collective-permute-start | bytes 2162696 | tf_op jit(solution)/shard_map/ppermute | solution.py:475
  70.9 8.4 %collective-permute-start.21 = (bf16[64,2048]{1,0:T(8,128)(2,1)S(1)}, bf16[64,2048]{1,0:T(8,128)(2,1)S(1)}, u32[]{:S(2)}, u32[]{:S(2)}) collective-permute-start(bf16[64,2048]{1,0:T(8,128)(2,1)S(1)} %get-tuple-element.52), channel_id=1, source_target_pairs={{0,1},{1,0},{2,3},{3,2},{4,5},{5,4},{6,7},{7,6},{8,9},{9,8},{10,11... | collective-permute-start | bytes 786440 | tf_op jit(solution)/shard_map/ppermute | solution.py:481
  72.5 12.1 %collective-permute-start.20 = (bf16[64,2048]{1,0:T(8,128)(2,1)S(1)}, bf16[64,2048]{1,0:T(8,128)(2,1)S(1)}, u32[]{:S(2)}, u32[]{:S(2)}) collective-permute-start(bf16[64,2048]{1,0:T(8,128)(2,1)S(1)} %get-tuple-element.50), channel_id=1, source_target_pairs={{0,2},{1,3},{2,0},{3,1},{4,6},{5,7},{6,4},{7,5},{8,10},{9,11},{10,... | collective-permute-start | bytes 786440 | tf_op jit(solution)/shard_map/ppermute | solution.py:481
  79.3 5.3 %collective-permute-start.22 = (bf16[32,2048]{1,0:T(8,128)(2,1)S(1)}, bf16[32,2048]{1,0:T(8,128)(2,1)S(1)}, u32[]{:S(2)}, u32[]{:S(2)}) collective-permute-start(bf16[32,2048]{1,0:T(8,128)(2,1)S(1)} %get-tuple-element.55.refs_5_), channel_id=1, source_target_pairs={{0,2},{1,3},{2,0},{3,1},{4,6},{5,7},{6,4},{7,5},{8,10},{9,11},{10,... | collective-permute-start | bytes 393224 | tf_op jit(solution)/shard_map/ppermute | solution.py:481
  84.7 9.3 %collective-permute-start.23 = (bf16[32,2048]{1,0:T(8,128)(2,1)S(1)}, bf16[32,2048]{1,0:T(8,128)(2,1)S(1)}, u32[]{:S(2)}, u32[]{:S(2)}) collective-permute-start(bf16[32,2048]{1,0:T(8,128)(2,1)S(1)} %get-tuple-element.59), channel_id=1, source_target_pairs={{0,1},{1,0},{2,3},{3,2},{4,5},{5,4},{6,7},{7,6},{8,9},{9,8},{10,11... | collective-permute-start | bytes 393224 | tf_op jit(solution)/shard_map/ppermute | solution.py:481
  86.3 7.9 %collective-permute-start.24 = (bf16[32,2048]{1,0:T(8,128)(2,1)S(1)}, bf16[32,2048]{1,0:T(8,128)(2,1)S(1)}, u32[]{:S(2)}, u32[]{:S(2)}) collective-permute-start(bf16[32,2048]{1,0:T(8,128)(2,1)S(1)} %get-tuple-element.60.refs_5_), channel_id=1, source_target_pairs={{0,4},{1,5},{2,6},{3,7},{4,0},{5,1},{6,2},{7,3},{8,12},{9,13},{10,... | collective-permute-start | bytes 393224 | tf_op jit(solution)/shard_map/ppermute | solution.py:481
  (2 other events, 13.8 us)
